TPU v7x, 32 devices: a whole 2x2x4 slice. The times are simulated.
32 devices in a mesh: pts: 8 (over z, y), own: 4 (over x, core).
Axes of the slice: x: 2, y: 2, z: 4, core: 2. Of those that a mesh axis runs over, the one named last changes fastest.
Arguments:
- points: bfloat16 [8192, 1536], P(('pts', 'own')), may hold values from -6 to 6
- parent_of: int32 [8192, 1], P('pts'), may hold values from 0 to 63, as said below
- owner_of: int32 [64], replicated, may hold values from 0 to 3, as said below
- child_count: int32 [64], replicated, may hold values from 16 to 64, as said below
- centroids: bfloat16 [4, 1024, 1536], P('own'), may hold values from -6 to 6
Outputs:
- new_centroids: bfloat16 [4, 1024, 1536], P('own', 'pts')
Inputs may be any that keep to these rules, and one draw needn't show every extreme that they name: `owner_of`: each owner is named by exactly 16 parents. `child_count`: exactly 64 for at least one parent. `parent_of`: every parent is named by some point; in the 256 rows of one device, exactly 128 rows have parents of one owner, and all devices with the same pts index pick the same such owner; the rest of the device's rows go to the other owners as evenly as possible, so no owner gets more than 128 rows of one device.
All inputs are finite; a program needn't handle non-finite values.
Results may differ from a plain program's by a relative error of at most 0.0031.
Values may be sent and summed in bfloat16 or wider, within the bound.
No kernel may reach another device: no remote copies, remote signals or barrier semaphores. Data moves between devices by JAX's collectives and lax.ppermute only.
A program may use at most 128 MiB of HBM per device.

v0:
```python
import jax
import jax.numpy as jnp
from jax import lax
from jax.sharding import PartitionSpec as P

SWEEPS = 2


def unit_rms(values):
    values = values.astype(jnp.float32)
    return values * lax.rsqrt(jnp.mean(values * values, axis=-1, keepdims=True) + 1e-06)


def lookup(onehot, table):
    return jnp.sum(jnp.where(onehot, table[None, :], 0), axis=1)


def local(points, parent_of, owner_of, child_count, centroids):
    width = points.shape[1]
    point_unit = unit_rms(points).astype(jnp.bfloat16)
    parent_ids = parent_of[:, 0]
    parent_range = jnp.arange(owner_of.shape[0], dtype=jnp.int32)
    same_owner = owner_of[:, None] == owner_of[None, :]
    earlier = parent_range[None, :] < parent_range[:, None]
    first_slot = jnp.sum(jnp.where(same_owner & earlier, child_count[None, :], 0), axis=1)
    owner_index = lax.axis_index("own")
    cent_unit = unit_rms(centroids[0]).astype(jnp.bfloat16)
    slot_total = cent_unit.shape[0]
    slot_index = jnp.arange(slot_total, dtype=jnp.int32)
    rows = lax.all_gather(point_unit, "own", axis=0, tiled=True)
    onehot = parent_ids[:, None] == parent_range[None, :]
    row_owner = lookup(onehot, owner_of)
    row_first = lookup(onehot, first_slot)
    row_count = lookup(onehot, child_count)
    row_live = row_owner == owner_index
    in_range = (
        row_live[:, None]
        & (slot_index[None, :] >= row_first[:, None])
        & (slot_index[None, :] < (row_first + row_count)[:, None])
    )
    table_range = (
        (owner_of == owner_index)[:, None]
        & (slot_index[None, :] >= first_slot[:, None])
        & (slot_index[None, :] < (first_slot + child_count)[:, None])
    )
    slot_used = jnp.any(table_range, axis=0)
    scores = jnp.dot(rows, cent_unit.T, preferred_element_type=jnp.float32) / (width * 0.05)
    weights = jnp.where(in_range, jnp.exp(scores), jnp.float32(0.0))
    for sweep in range(SWEEPS):
        column_sum = lax.psum(jnp.sum(weights, axis=0), "pts")
        weights = weights / jnp.where(slot_used, column_sum, jnp.float32(1.0))[None, :]
        row_sum = jnp.sum(weights, axis=1)
        weights = weights / jnp.where(row_live, row_sum, jnp.float32(1.0))[:, None]
    assign = weights.astype(jnp.bfloat16)
    share = slot_total // lax.axis_size("pts")
    pts_index = lax.axis_index("pts")
    moved = lax.psum_scatter(
        lax.dot_general(assign, rows, (((0,), (0,)), ((), ())), preferred_element_type=jnp.float32),
        "pts",
        scatter_dimension=0,
        tiled=True,
    )
    base = lax.dynamic_slice_in_dim(cent_unit, pts_index * share, share, 0).astype(jnp.float32)
    updated = unit_rms(base + 8.0 * moved).astype(jnp.bfloat16)
    return updated[None]


def solution(mesh):
    in_specs = (P(("pts", "own"), None), P("pts", None), P(), P(), P("own", None, None))
    out_specs = P("own", "pts", None)
    return jax.shard_map(local, mesh=mesh, in_specs=in_specs, out_specs=out_specs, check_vma=False)
```

profile of v0, /device:TPU:0, one launch (start us, length us, event | category | flops | bytes accessed | tf_op | source)
XLA Modules:
  0.0 230.0 jit_solution(17263158895612676370)
XLA Ops:
  6.5 0.0 copy-start.2
  6.5 0.0 all-gather.2.cloned.1.call-start
  6.5 1.5 fusion.16
  8.1 2.2 fusion.17
  10.3 0.0 all-gather.2.cloned.1.call-update
  10.3 0.0 reduce-scatter.2.cloned.1.call-start
  10.4 0.9 select_reduce_fusion.3
  11.3 0.7 add.61
  11.9 0.8 select_reduce_fusion.2
  12.8 0.7 broadcast_compare_fusion.1
  13.5 0.1 fusion.21
  13.6 0.0 copy-done.2
  13.6 0.7 fusion
  14.3 2.3 fusion.1
  16.6 25.1 %all-gather.2.cloned.1.call-done = bf16[1024,1536]{1,0:T(8,128)(2,1)} async-done(((bf16[256,1536]{1,0:T(8,128)(2,1)}), bf16[1024,1536]{1,0:T(8,128)(2,1)}) %all-gather.2.cloned.1.call-update) | async-done | bytes 3145744 | tf_op jit(solution)/shard_map/all_gather | solution.py:30
  41.7 8.4 %fusion.23 = (f32[1024]{0:T(1024)S(1)}, f32[1024,1024]{1,0:T(8,128)}) fusion(bf16[1024,1536]{1,0:T(8,128)(2,1)} %all-gather.2.cloned.1.call-done, bf16[1024,1536]{1,0:T(8,128)(2,1)} %fusion.1, s32[1024]{0:T(1024)S(1)} %add.58, s32[1024]{0:T(1024)S(1)} %get-tuple-element.7, pred[1024]{0:T(1024)(128)(4,1)S(1)} %broadcast_compare_fusion), kind=kOutput, calls=%fused_computation.52 | convolution fusion | flops 3228564480 | bytes 10499072 | tf_op jit(solution)/shard_map/dot_general | solution.py:47
  50.1 21.3 %psum.14 = f32[1024]{0:T(1024)S(1)} all-reduce(f32[1024]{0:T(1024)S(1)} %get-tuple-element.8), channel_id=1, replica_groups=mesh['pts'=8,'own'=4] {'pts'}, use_global_device_ids=true, to_apply=%region_8.9 | all-reduce | flops 1024 | bytes 8192 | tf_op jit(solution)/shard_map/psum | solution.py:50
  71.5 0.0 copy-start
  71.5 2.7 %divide_reduce_fusion = f32[1024]{0:T(1024)S(1)} fusion(f32[1024,1024]{1,0:T(8,128)} %get-tuple-element.9, f32[1024]{0:T(1024)S(1)} %broadcast_select_fusion.3), kind=kLoop, calls=%fused_computation.13 | loop fusion | flops 2096128 | bytes 4202496 | tf_op jit(solution)/shard_map/reduce_sum | solution.py:52
  74.2 0.7 copy-done
  74.9 0.6 fusion.6
  75.5 17.1 %psum.15 = f32[1024]{0:T(1024)S(1)} all-reduce(f32[1024]{0:T(1024)S(1)} %fusion.6), channel_id=1, replica_groups=mesh['pts'=8,'own'=4] {'pts'}, use_global_device_ids=true, to_apply=%region_11.12 | all-reduce | flops 1024 | bytes 8192 | tf_op jit(solution)/shard_map/psum | solution.py:50
  92.7 0.0 copy-start.1
  92.7 3.3 %fusion.7 = f32[1024]{0:T(1024)S(1)} fusion(f32[1024,1024]{1,0:T(8,128)} %get-tuple-element.9, f32[1024]{0:T(1024)S(1)} %broadcast_select_fusion.1, f32[1024]{0:T(1024)S(1)} %broadcast_select_fusion.2, f32[1024]{0:T(1024)S(1)} %broadcast_select_fusion.3), kind=kLoop, calls=%fused_computation.15 | loop fusion | flops 4193280 | bytes 4210688 | tf_op jit(solution)/shard_map/reduce_sum | solution.py:52
  96.0 0.2 copy-done.1
  96.1 7.6 %fusion.10 = f32[1024,1536]{1,0:T(8,128)} fusion(bf16[1024,1536]{1,0:T(8,128)(2,1)} %all-gather.2.cloned.1.call-done, f32[1024,1024]{1,0:T(8,128)S(1)} %copy-done.1, f32[1024]{0:T(1024)S(1)} %broadcast_select_fusion, f32[1024]{0:T(1024)S(1)} %broadcast_select_fusion.1, f32[1024]{0:T(1024)S(1)} %broadcast_select_fusion.2, f32[1024]{0:T(1024)S(1)} %broadcast_select_fusion.3), kind=kOutput, calls=%fused_computation.18 | convolution fusion | flops 3226468352 | bytes 13647872 | tf_op jit(solution)/shard_map/dot_general | solution.py:58
  103.7 0.0 reduce-scatter.2.cloned.1.call-update
  103.7 115.9 %reduce-scatter.2.cloned.1.call-done = f32[128,1536]{1,0:T(8,128)} async-done(((f32[1024,1536]{1,0:T(8,128)}), f32[128,1536]{1,0:T(8,128)}) %reduce-scatter.2.cloned.1.call-update) | async-done | bytes 786448 | tf_op jit(solution)/shard_map/reduce_scatter | solution.py:57
  219.6 1.4 multiply_reduce_fusion
  221.1 2.1 fusion.18
  (9 shorter events, 0.1 us)
Async XLA Ops:
  6.5 7.1 %copy-start.2 = (bf16[1,1024,1536]{2,1,0:T(8,128)(2,1)S(1)}, bf16[1,1024,1536]{2,1,0:T(8,128)(2,1)}, u32[]{:S(2)}) copy-start(bf16[1,1024,1536]{2,1,0:T(8,128)(2,1)} %param.9) | copy-start | bytes 9437188
  6.5 35.2 %all-gather.2.cloned.1.call-start = ((), (), s32[]{:S(2)}) async-start(), calls=%async_computation.1 | async-start | bytes 3932160 | tf_op jit(solution)/shard_map/all_gather | solution.py:30
  10.3 209.3 %reduce-scatter.2.cloned.1.call-start = ((), (), s32[]{:S(2)}) async-start(), calls=%async_computation.2 | async-start | bytes 7077888 | tf_op jit(solution)/shard_map/reduce_scatter | solution.py:57
  71.5 3.4 %copy-start = (f32[1024,1024]{1,0:T(8,128)S(1)}, f32[1024,1024]{1,0:T(8,128)}, u32[]{:S(2)}) copy-start(f32[1024,1024]{1,0:T(8,128)} %get-tuple-element.9) | copy-start | bytes 12582916
  92.7 3.4 %copy-start.1 = (f32[1024,1024]{1,0:T(8,128)S(1)}, f32[1024,1024]{1,0:T(8,128)}, u32[]{:S(2)}) copy-start(f32[1024,1024]{1,0:T(8,128)} %get-tuple-element.9) | copy-start | bytes 12582916
Sparse Core Ops, SparseCore 0:
  10.4 31.2 all-gather.1
  103.8 115.7 reduce-scatter.1
where the time goes:
time: 230 us
  waiting for transfers between devices  141 us (61%)
  blocking collectives  38.5 us (17%)
  other arithmetic  20.1 us (9%)
  matrix products  16 us (7%)
  between operations  13.5 us (6%)
    reduce_scatter x1, waiting for transfers between devices, local(): lax.psum_scatter(lax.dot_general(assign, rows, (((0,), (0,)), ((), ())),...  116 us
    psum x2, blocking collectives, local(): column_sum = lax.psum(jnp.sum(weights, axis=0), 'pts')  38.5 us
    all_gather x1, waiting for transfers between devices, local(): rows = lax.all_gather(point_unit, 'own', axis=0, tiled=True)  25.1 us
    dot_general x1, matrix products, local(): jnp.dot(rows, cent_unit.T, preferred_element_type=jnp.float32)  8.41 us
    dot_general x1, matrix products, local(): lax.dot_general(assign, rows, (((0,), (0,)), ((), ())), preferred_element...  7.58 us
    reduce_sum x2, other arithmetic, local(): row_sum = jnp.sum(weights, axis=1)  5.95 us
  transfers between devices with their start and end apart: 2, of which 2 were waited for; matrix products, arithmetic and copies ran while one was open for 3% of the time, Pallas kernels for 0%

commit v1 on v0

v1 whole, which is shorter than its diff:
```python
import functools

import jax
import jax.numpy as jnp
from jax import lax
from jax.experimental import pallas as pl
from jax.experimental.pallas import tpu as pltpu
from jax.sharding import PartitionSpec as P

F32 = jnp.float32
BF16 = jnp.bfloat16
I32 = jnp.int32
CORES = 2
ROWS = 16
LANES = 128
VMEM_LIMIT = 40 * 1024 * 1024
OWNER_SHIFT = 1 << 17
FIRST_SHIFT = 1 << 7


def down(value):
    return value // ROWS * ROWS


def up(value):
    return -(-value // ROWS) * ROWS


def iota(shape, dim):
    return lax.broadcasted_iota(I32, shape, dim)


def unit_rms(values):
    values = values.astype(F32)
    return values * lax.rsqrt(jnp.mean(values * values, axis=-1, keepdims=True) + 1e-06)


def windows(tok, owners):
    chips = owners // CORES
    full = 2 * tok // owners
    least = CORES * ((tok - full) // max(owners - 1, 1))
    starts = [down(j * least) for j in range(chips)]
    ends = [up(tok - (chips - 1 - j) * least) for j in range(chips)]
    wide = max(e - s for s, e in zip(starts, ends))
    return [min(s, tok - wide) for s in starts], wide


def to_col(row):
    n = row.shape[1]
    return jnp.sum(jnp.where(iota((n, n), 0) == iota((n, n), 1), row, 0.0), axis=1, keepdims=True)


def to_row(col):
    n = col.shape[0]
    return jnp.sum(jnp.where(iota((n, n), 0) == iota((n, n), 1), col, 0.0), axis=0, keepdims=True)


def owner_codes(owner_ref, count_ref):
    owner = owner_ref[...].astype(F32)
    count = count_ref[...].astype(F32)
    n = owner.shape[1]
    earlier = (to_col(owner) == owner) & (iota((n, n), 0) < iota((n, n), 1))
    first = jnp.sum(jnp.where(earlier, to_col(count), 0.0), axis=0, keepdims=True)
    return owner * OWNER_SHIFT + first * FIRST_SHIFT + count


def code_and_key(parent_row, code_row, chip, chips):
    parent = to_col(parent_row.astype(F32)).astype(I32)
    tok = parent.shape[0]
    n = code_row.shape[1]
    code = jnp.sum(jnp.where(parent == iota((tok, n), 1), code_row, 0.0), axis=1, keepdims=True)
    owner = code.astype(I32) // OWNER_SHIFT
    order = (chips - 1) - ((owner // CORES) ^ chip)
    key = (order * tok + iota((tok, 1), 0)).astype(F32)
    return code, key


def sort_kernel(chips, points_ref, parents_ref, owner_ref, count_ref, out_ref):
    me = lax.axis_index("own")
    code_row = owner_codes(owner_ref, count_ref)
    parent = parents_ref[pl.ds(me, 1), :]
    code, key = code_and_key(parent, code_row, me // CORES, chips)
    tok = key.shape[0]
    key_row = to_row(key)
    place = jnp.sum(jnp.where(key < key_row, 1.0, 0.0), axis=0, keepdims=True).astype(I32)
    pick = jnp.where(iota((tok, tok), 0) == place, 1.0, 0.0).astype(BF16)
    unit = unit_rms(points_ref[...]).astype(BF16)
    out_ref[...] = jnp.dot(pick, unit, preferred_element_type=F32).astype(BF16)


def codes_kernel(chips, starts, parents_ref, owner_ref, count_ref, out_ref):
    me = lax.axis_index("own")
    code_row = owner_codes(owner_ref, count_ref)
    wide = out_ref.shape[1]
    for rel in range(out_ref.shape[0]):
        parent = parents_ref[pl.ds(me ^ rel, 1), :]
        code, key = code_and_key(parent, code_row, (me ^ rel) // CORES, chips)
        tok = key.shape[0]
        place = jnp.sum(jnp.where(to_row(key) < key, 1.0, 0.0), axis=1, keepdims=True).astype(I32)
        start = starts[chips - 1 - rel // CORES]
        hit = place == iota((tok, wide), 1) + start
        out_ref[rel : rel + 1, :] = jnp.sum(jnp.where(hit, code, 0.0), axis=0, keepdims=True)


def cent_kernel(in_ref, out_ref):
    out_ref[...] = unit_rms(in_ref[...]).astype(BF16)


def weights_kernel(rels, tile, *refs):
    n = len(rels)
    row_refs, (codes_ref, cent_ref, w_ref, sum_ref, rows_ref, low_ref, high_ref) = refs[:n], refs[n:]
    me = lax.axis_index("own")
    wide, width = row_refs[0].shape
    slots = cent_ref.shape[0]
    for k, rel in enumerate(rels):
        part = slice(k * wide, (k + 1) * wide)
        rows_ref[part, :] = row_refs[k][...]
        code = to_col(codes_ref[rel : rel + 1, :]).astype(I32)
        first = (code % OWNER_SHIFT) // FIRST_SHIFT
        low = jnp.where(code // OWNER_SHIFT == me, first, slots)
        low_ref[part, :] = low
        high_ref[part, :] = low + code % FIRST_SHIFT

    def step(i, carry):
        at = pl.multiple_of(i * tile, tile)
        cent = cent_ref[pl.ds(at, tile), :]
        scores = lax.dot_general(rows_ref[...], cent, (((1,), (1,)), ((), ())), preferred_element_type=F32)
        slot = iota(scores.shape, 1) + at
        live = (slot >= low_ref[...]) & (slot < high_ref[...])
        w = jnp.where(live, jnp.exp(scores * (1.0 / (width * 0.05))), 0.0)
        w_ref[:, pl.ds(at, tile)] = w
        sum_ref[:, pl.ds(at, tile)] = jnp.sum(w, axis=0, keepdims=True)
        return carry

    lax.fori_loop(0, slots // tile, step, 0)


def inverse(values):
    return jnp.where(values > 0.0, 1.0 / jnp.where(values > 0.0, values, 1.0), 0.0)


def balance_kernel(n, *refs):
    w_refs, col_ref, out_ref = refs[:n], refs[n], refs[n + 1]
    scale = inverse(col_ref[...])
    total = jnp.zeros_like(scale)
    for w_ref in w_refs:
        rows = w_ref.shape[0]
        for at in range(0, rows, ROWS * 2):
            w = w_ref[at : at + ROWS * 2, :]
            row = jnp.sum(w * scale, axis=1, keepdims=True)
            total = total + jnp.sum(w * inverse(row), axis=0, keepdims=True)
    out_ref[...] = total


def move_kernel(nw, nr, routes, cols, half_bit, low_mask, *refs):
    w_refs, row_refs, t_ref = refs[:nw], refs[nw : nw + nr], refs[nw + nr]
    rest = refs[nw + nr + 1 :]
    keep_refs, send_refs = rest[: len(routes)], rest[len(routes) : 2 * len(routes)]
    assign_ref, rows_ref, part_ref = rest[2 * len(routes) :]
    p = lax.axis_index("pts")
    scale = inverse(t_ref[...])
    half = assign_ref.shape[1]
    upper = (p // half_bit) % 2
    at = 0
    for w_ref in w_refs:
        rows = w_ref.shape[0]
        for lo in range(0, rows, ROWS * 2):
            w = w_ref[lo : lo + ROWS * 2, :] * scale
            row = inverse(jnp.sum(w, axis=1, keepdims=True))
            mine = jnp.where(upper == 0, w[:, :half], w[:, half:])
            assign_ref[at : at + ROWS * 2, :] = (mine * row).astype(BF16)
            at += ROWS * 2
    at = 0
    for r in row_refs:
        rows_ref[at : at + r.shape[0], :] = r[...]
        at += r.shape[0]
    low = p % half_bit
    share = half // half_bit
    for which, order in enumerate(routes):
        lanes = slice(which * cols, (which + 1) * cols)
        m = keep_refs[which].shape[0]

        for k, rel in enumerate(order):
            start = (low ^ rel) * share
            block = part_ref.shape[0]
            a = assign_ref[:, pl.ds(pl.multiple_of(start // block * block, block), block)]
            moved = lax.dot_general(
                a, rows_ref[:, lanes], (((0,), (0,)), ((), ())), preferred_element_type=F32
            )
            if share < block:
                part_ref[...] = moved
                moved = part_ref[pl.ds(pl.multiple_of(start % block, share), share), :]
            if k < m:
                keep_refs[which][k] = moved
            else:
                send_refs[which][k - m] = moved.astype(BF16)


def final_kernel(nroute, nterm, *refs):
    base_ref, out_ref = refs[nroute * nterm], refs[nroute * nterm + 1]
    parts = []
    for which in range(nroute):
        total = refs[which * nterm][...].astype(F32)
        for k in range(1, nterm):
            total = total + refs[which * nterm + k][...].astype(F32)
        parts.append(total)
    moved = jnp.concatenate(parts, axis=1)
    out_ref[...] = unit_rms(base_ref[...].astype(F32) + 8.0 * moved).astype(BF16)


def call(kernel, outs, *args, scratch=(), flops=0):
    shapes = [jax.ShapeDtypeStruct(s, d) for s, d in outs]
    size = sum(a.size * a.dtype.itemsize for a in args) + sum(s.size * s.dtype.itemsize for s in shapes)
    got = pl.pallas_call(
        kernel,
        out_shape=shapes,
        in_specs=[pl.BlockSpec(memory_space=pltpu.VMEM)] * len(args),
        out_specs=[pl.BlockSpec(memory_space=pltpu.VMEM)] * len(shapes),
        scratch_shapes=list(scratch),
        compiler_params=pltpu.CompilerParams(vmem_limit_bytes=VMEM_LIMIT),
        cost_estimate=pl.CostEstimate(flops=flops, bytes_accessed=size, transcendentals=0),
    )(*args)
    return got[0] if len(shapes) == 1 else got


def swap(values, axis, bit):
    return lax.ppermute(values, axis, [(i, i ^ bit) for i in range(lax.axis_size(axis))])


def bit_orders(bits):
    orders = []
    for k in range(len(bits)):
        order = bits[k:] + bits[:k]
        blocks = [0]
        for bit in reversed(order):
            blocks = blocks + [b | bit for b in blocks]
        orders.append((order, blocks))
    return orders


def local(points, parent_of, owner_of, child_count, centroids):
    owners, groups = lax.axis_size("own"), lax.axis_size("pts")
    chips = owners // CORES
    tok, width = points.shape
    slots = centroids.shape[1]
    share = slots // groups
    starts, wide = windows(tok, owners)
    parents = parent_of.reshape(owners, tok)
    owner_row = owner_of.reshape(1, -1)
    count_row = child_count.reshape(1, -1)
    half_bit = groups // 2

    ordered = call(
        functools.partial(sort_kernel, chips), [((tok, width), BF16)], points, parents, owner_row, count_row,
        flops=2 * tok * tok * width,
    )
    outward = starts[max(chips - 2, 0)] + wide

    def spread(head, tail):
        blocks = {}
        for chip in range(1, chips):
            start = starts[chips - 1 - chip]
            blocks[chip * CORES] = swap(head[start : start + wide], "own", chip * CORES)
        start = starts[chips - 1]
        blocks[0] = jnp.concatenate([head[start:], tail], axis=0)
        for chip in range(chips):
            blocks[chip * CORES + 1] = swap(blocks[chip * CORES], "own", 1)
        return blocks

    head, tail = ordered[:outward], ordered[outward:]
    near = spread(head, tail)
    far_head, far_tail = swap(head, "pts", half_bit), swap(tail, "pts", half_bit)
    far = spread(far_head, far_tail)
    codes = call(
        functools.partial(codes_kernel, chips, starts), [((owners, wide), F32)], parents, owner_row, count_row
    )
    far_codes = swap(codes, "pts", half_bit)
    cent = call(cent_kernel, [((slots, width), BF16)], centroids[0])

    def weigh(blocks, codes, rels):
        rows = wide * len(rels)
        return call(
            functools.partial(weights_kernel, rels, min(slots, 256)),
            [((rows, slots), F32), ((1, slots), F32)],
            *[blocks[r] for r in rels], codes, cent,
            scratch=[pltpu.VMEM((rows, width), BF16), pltpu.VMEM((rows, 1), I32), pltpu.VMEM((rows, 1), I32)],
            flops=2 * rows * width * slots,
        )

    def all_sum(values):
        bit = 1
        while bit < groups:
            values = values + swap(values, "pts", bit)
            bit *= 2
        return values

    pairs = [list(range(c * CORES, (c + 1) * CORES)) for c in range(chips)]
    near_w, far_w, partial = [], [], None
    for rels in pairs:
        w, s = weigh(near, codes, rels)
        near_w.append(w)
        partial = s if partial is None else partial + s
    for rels in pairs:
        far_w.append(weigh(far, far_codes, rels)[0])
    column = all_sum(partial)
    balance = all_sum(call(functools.partial(balance_kernel, chips), [((1, slots), F32)], *near_w, column))

    bits = []
    bit = 1
    while bit < half_bit:
        bits.append(bit)
        bit *= 2
    orders = bit_orders(bits)
    cols = width // len(orders)
    m = half_bit // 2
    rows = [near[r] for r in range(owners)] + [far[r] for r in range(owners)]
    total_rows = wide * len(rows)
    got = call(
        functools.partial(
            move_kernel, 2 * chips, len(rows), [b for _, b in orders], cols, half_bit, half_bit - 1
        ),
        [((m, share, cols), F32)] * len(orders) + [((m, share, cols), BF16)] * len(orders),
        *near_w, *far_w, *rows, balance,
        scratch=[pltpu.VMEM((total_rows, slots // 2), BF16), pltpu.VMEM((total_rows, width), BF16),
                 pltpu.VMEM((max(share, LANES), cols), F32)],
        flops=2 * total_rows * width * slots // 2,
    )
    keeps, sends = got[: len(orders)], got[len(orders) :]
    terms = [[k] for k in keeps]
    for step in range(len(bits)):
        arrived = [swap(s, "pts", orders[r][0][step]) for r, s in enumerate(sends)]
        sends = []
        for r, a in enumerate(arrived):
            terms[r].append(a)
            n = a.shape[0] // 2
            if n:
                sends.append(sum(t[n:].astype(F32) for t in terms[r]).astype(BF16))
                terms[r] = [t[:n] for t in terms[r]]
    own = lax.axis_index("pts") * share
    base = lax.dynamic_slice_in_dim(cent, own, share, 0)
    flat = [t.reshape(share, cols) for route in terms for t in route]
    out = call(
        functools.partial(final_kernel, len(orders), len(bits) + 1), [((share, width), BF16)], *flat, base
    )
    return out[None]


def solution(mesh):
    in_specs = (P(("pts", "own"), None), P("pts", None), P(), P(), P("own", None, None))
    out_specs = P("own", "pts", None)
    return jax.shard_map(local, mesh=mesh, in_specs=in_specs, out_specs=out_specs, check_vma=False)
```

time: 230 us -> 115 us (0.50)
  waiting for transfers between devices: 141 us -> 55 us
  blocking collectives: 38.5 us -> 0 us
  starting transfers between devices: 0.04 us -> 30.5 us
  Pallas kernels: 0 us -> 20.1 us
  other arithmetic: 20.1 us -> 2.7 us
  matrix products: 16 us -> 0 us
  between operations: 13.5 us -> 0.21 us
  local copies, waits for them, and re-layouts: 0.9 us -> 5.91 us
    reduce_scatter x1 -> x0, waiting for transfers between devices: 116 us -> none  [local(): lax.psum_scatter(lax.dot_general(assign, rows, (((0,), (0,)), ((), ())),...]
    ppermute x0 -> x19, waiting for transfers between devices: none -> 55 us  [swap(): lax.ppermute(values, axis, [(i, i ^ bit) for i in range(lax.axis_size(axi...]
    psum x2 -> x0, blocking collectives: 38.5 us -> none  [local(): column_sum = lax.psum(jnp.sum(weights, axis=0), 'pts')]
    ppermute x0 -> x19, starting transfers between devices: none -> 30.5 us  [swap(): lax.ppermute(values, axis, [(i, i ^ bit) for i in range(lax.axis_size(axi...]
    all_gather x1 -> x0, waiting for transfers between devices: 25.1 us -> none  [local(): rows = lax.all_gather(point_unit, 'own', axis=0, tiled=True)]
    pallas_call x0 -> x10, Pallas kernels: none -> 20.1 us  [call(): pl.pallas_call(kernel, out_shape=shapes, in_specs=[pl.BlockSpec(memory_sp...]
    dot_general x2 -> x0, matrix products: 16 us -> none  [the longest x1 8.41 us: local(): jnp.dot(rows, cent_unit.T, preferred_element_type=jnp.float32)]
    reduce_sum x8 -> x0, other arithmetic: 12 us -> none  [the longest x2 5.95 us: local(): row_sum = jnp.sum(weights, axis=1)]
  transfers between devices with their start and end apart: 2 -> 19, of which waited for: 2 -> 10; matrix products, arithmetic and copies ran while one was open for 3% -> 2% of each run, Pallas kernels for 0% -> 10%
where the time goes in v1:
time: 115 us; the launch traced here: 114 us
  waiting for transfers between devices  55 us (48%)
  starting transfers between devices  30.5 us (27%)
  Pallas kernels  20.1 us (17%)
  local copies, waits for them, and re-layouts  5.91 us (5%)
  other arithmetic  2.7 us (2%)
    ppermute x19, waiting for transfers between devices, swap(): lax.ppermute(values, axis, [(i, i ^ bit) for i in range(lax.axis_size(axi...  55 us
    ppermute x19, starting transfers between devices, swap(): lax.ppermute(values, axis, [(i, i ^ bit) for i in range(lax.axis_size(axi...  30.5 us
    pallas_call x10, Pallas kernels, call(): pl.pallas_call(kernel, out_shape=shapes, in_specs=[pl.BlockSpec(memory_sp...  20.1 us
    unnamed x19, local copies, waits for them, and re-layouts  4.8 us
  transfers between devices with their start and end apart: 19, of which 10 were waited for; matrix products, arithmetic and copies ran while one was open for 2% of the time, Pallas kernels for 10%

profile of v1, /device:TPU:0, one launch (start us, length us, event | category | flops | bytes accessed | tf_op | source)
XLA Modules:
  0.0 114.4 jit_solution(18435365448923473824)
XLA Ops:
  0.0 0.5 broadcast.3
  0.5 1.3 %reduce.3 = s32[1024]{0:T(1024)S(1)} reduce(s32[1024,1]{0,1:T(1,128)} %param.6, s32[]{:T(128)} %broadcast.3), dimensions={1}, to_apply=%param.6.reduce_sub_computation.3 | reduce | bytes 8196 | tf_op args[1]
  1.9 1.1 copy-done.4
  3.0 0.7 copy-done.5
  3.7 0.7 copy-done.7
  4.3 0.9 shard_map.55
  5.2 0.1 fusion
  5.3 4.1 %collective-permute-start.3 = (bf16[176,1536]{1,0:T(8,128)(2,1)S(1)}, bf16[176,1536]{1,0:T(8,128)(2,1)S(1)}, u32[]{:S(2)}, u32[]{:S(2)}) collective-permute-start(bf16[176,1536]{1,0:T(8,128)(2,1)S(1)} %get-tuple-element.29), channel_id=1, source_target_pairs={{0,16},{4,20},{8,24},{12,28},{16,0},{20,4},{24,8},{28,12},{1,17},{... | collective-permute-start | bytes 1622024 | tf_op jit(solution)/shard_map/ppermute | solution.py:227
  9.4 1.5 %collective-permute-start.1 = (bf16[176,1536]{1,0:T(8,128)(2,1)S(1)}, bf16[176,1536]{1,0:T(8,128)(2,1)S(1)}, u32[]{:S(2)}, u32[]{:S(2)}) collective-permute-start(bf16[176,1536]{1,0:T(8,128)(2,1)S(1)} %get-tuple-element.29), channel_id=1, source_target_pairs={{0,2},{1,3},{2,0},{3,1},{4,6},{5,7},{6,4},{7,5},{8,10},{9,11},{10,... | collective-permute-start | bytes 1622024 | tf_op jit(solution)/shard_map/ppermute | solution.py:227
  10.9 0.4 collective-permute-start.4
  11.3 28.0 %collective-permute-done.3 = bf16[176,1536]{1,0:T(8,128)(2,1)S(1)} collective-permute-done((bf16[176,1536]{1,0:T(8,128)(2,1)S(1)}, bf16[176,1536]{1,0:T(8,128)(2,1)S(1)}, u32[]{:S(2)}, u32[]{:S(2)}) %collective-permute-start.3) | collective-permute-done | bytes 540704 | tf_op jit(solution)/shard_map/ppermute | solution.py:227
  39.4 1.8 %collective-permute-start.7 = (bf16[176,1536]{1,0:T(8,128)(2,1)S(1)}, bf16[176,1536]{1,0:T(8,128)(2,1)S(1)}, u32[]{:S(2)}, u32[]{:S(2)}) collective-permute-start(bf16[176,1536]{1,0:T(8,128)(2,1)S(1)} %collective-permute-done.3), channel_id=1, source_target_pairs={{0,2},{1,3},{2,0},{3,1},{4,6},{5,7},{6,4},{7,5},{8,10},{9,11},{10,... | collective-permute-start | bytes 1622024 | tf_op jit(solution)/shard_map/ppermute | solution.py:227
  41.2 0.6 collective-permute-start.2
  41.8 2.0 %collective-permute-done.4 = bf16[80,1536]{1,0:T(8,128)(2,1)S(1)} collective-permute-done((bf16[80,1536]{1,0:T(8,128)(2,1)S(1)}, bf16[80,1536]{1,0:T(8,128)(2,1)S(1)}, u32[]{:S(2)}, u32[]{:S(2)}) %collective-permute-start.4) | collective-permute-done | bytes 245792 | tf_op jit(solution)/shard_map/ppermute | solution.py:227
  43.9 0.1 collective-permute-start.5
  43.9 8.1 %collective-permute-done.7.refs_0_.refs_10_ = bf16[176,1536]{1,0:T(8,128)(2,1)S(1)} collective-permute-done((bf16[176,1536]{1,0:T(8,128)(2,1)S(1)}, bf16[176,1536]{1,0:T(8,128)(2,1)S(1)}, u32[]{:S(2)}, u32[]{:S(2)}) %collective-permute-start.7) | collective-permute-done | bytes 540704 | tf_op jit(solution)/shard_map/ppermute | solution.py:227
  52.0 1.4 %shard_map.56.refs_2_ = f32[4,176]{1,0:T(4,128)S(1)} custom-call(s32[4,256]{1,0:T(4,128)S(1)} %reshape.27.parents_ref, s32[1,64]{1,0:T(1,128)S(1)} %bitcast.19, s32[1,64]{1,0:T(1,128)S(1)} %bitcast.21), custom_call_target="tpu_custom_call" | custom-call | bytes 7424 | tf_op jit(solution)/shard_map/pallas_call | solution.py:214
  53.4 1.0 shard_map.57.refs_3_
  54.5 2.6 %shard_map.58 = (f32[352,1024]{1,0:T(8,128)S(1)}, f32[1,1024]{1,0:T(1,128)S(1)}) custom-call(bf16[176,1536]{1,0:T(8,128)(2,1)S(1)} %get-tuple-element.30.refs_0_.refs_4_, bf16[176,1536]{1,0:T(8,128)(2,1)S(1)} %collective-permute-done.refs_1_.refs_5_, f32[4,176]{1,0:T(4,128)S(1)} %shard_map.56.refs_2_, bf16[1024,1536]{1,0:T(8,128)(2,1)S(1)} %shard_map.57.refs_3_), custom_call_target="tpu_custom_call" | custom-call | flops 1107296256 | bytes 5675776 | tf_op jit(solution)/shard_map/pallas_call | solution.py:214
  57.1 2.4 %shard_map.59 = (f32[352,1024]{1,0:T(8,128)S(1)}, f32[1,1024]{1,0:T(1,128)S(1)}) custom-call(bf16[176,1536]{1,0:T(8,128)(2,1)S(1)} %collective-permute-done.1.refs_0_.refs_6_, bf16[176,1536]{1,0:T(8,128)(2,1)S(1)} %collective-permute-done.2.refs_1_.refs_7_, f32[4,176]{1,0:T(4,128)S(1)} %shard_map.56.refs_2_, bf16[1024,1536]{1,0:T(8,128)(2,1)S(1)} %shard_map.57.refs_3_), custom_call_target="tpu_custom_call" | custom-call | flops 1107296256 | bytes 5675776 | tf_op jit(solution)/shard_map/pallas_call | solution.py:214
  59.5 1.3 %collective-permute-start.9 = (f32[1,1024]{1,0:T(1,128)S(1)}, f32[1,1024]{1,0:T(1,128)S(1)}, u32[]{:S(2)}, u32[]{:S(2)}) collective-permute-start(f32[1,1024]{1,0:T(1,128)S(1)} %add.30), channel_id=1, source_target_pairs={{0,4},{4,0},{8,12},{12,8},{16,20},{20,16},{24,28},{28,24},{1,5},{5... | collective-permute-start | bytes 12296 | tf_op jit(solution)/shard_map/ppermute | solution.py:227
  60.9 2.3 %collective-permute-done.9 = f32[1,1024]{1,0:T(1,128)S(1)} collective-permute-done((f32[1,1024]{1,0:T(1,128)S(1)}, f32[1,1024]{1,0:T(1,128)S(1)}, u32[]{:S(2)}, u32[]{:S(2)}) %collective-permute-start.9) | collective-permute-done | bytes 4128 | tf_op jit(solution)/shard_map/ppermute | solution.py:227
  63.2 1.5 %collective-permute-start.10 = (f32[1,1024]{1,0:T(1,128)S(1)}, f32[1,1024]{1,0:T(1,128)S(1)}, u32[]{:S(2)}, u32[]{:S(2)}) collective-permute-start(f32[1,1024]{1,0:T(1,128)S(1)} %add.31), channel_id=1, source_target_pairs={{0,8},{4,12},{8,0},{12,4},{16,24},{20,28},{24,16},{28,20},{1,9},{5... | collective-permute-start | bytes 12296 | tf_op jit(solution)/shard_map/ppermute | solution.py:227
  64.7 2.2 %collective-permute-done.10 = f32[1,1024]{1,0:T(1,128)S(1)} collective-permute-done((f32[1,1024]{1,0:T(1,128)S(1)}, f32[1,1024]{1,0:T(1,128)S(1)}, u32[]{:S(2)}, u32[]{:S(2)}) %collective-permute-start.10) | collective-permute-done | bytes 4128 | tf_op jit(solution)/shard_map/ppermute | solution.py:227
  66.8 2.8 %collective-permute-start.11 = (f32[1,1024]{1,0:T(1,128)S(1)}, f32[1,1024]{1,0:T(1,128)S(1)}, u32[]{:S(2)}, u32[]{:S(2)}) collective-permute-start(f32[1,1024]{1,0:T(1,128)S(1)} %add.32), channel_id=1, source_target_pairs={{0,16},{4,20},{8,24},{12,28},{16,0},{20,4},{24,8},{28,12},{1,17},{... | collective-permute-start | bytes 12296 | tf_op jit(solution)/shard_map/ppermute | solution.py:227
  69.7 1.7 %collective-permute-done.11 = f32[1,1024]{1,0:T(1,128)S(1)} collective-permute-done((f32[1,1024]{1,0:T(1,128)S(1)}, f32[1,1024]{1,0:T(1,128)S(1)}, u32[]{:S(2)}, u32[]{:S(2)}) %collective-permute-start.11) | collective-permute-done | bytes 4128 | tf_op jit(solution)/shard_map/ppermute | solution.py:227
  71.4 0.6 shard_map.62
  71.9 1.5 %collective-permute-start.12 = (f32[1,1024]{1,0:T(1,128)S(1)}, f32[1,1024]{1,0:T(1,128)S(1)}, u32[]{:S(2)}, u32[]{:S(2)}) collective-permute-start(f32[1,1024]{1,0:T(1,128)S(1)} %shard_map.62), channel_id=1, source_target_pairs={{0,4},{4,0},{8,12},{12,8},{16,20},{20,16},{24,28},{28,24},{1,5},{5... | collective-permute-start | bytes 12296 | tf_op jit(solution)/shard_map/ppermute | solution.py:227
  73.4 2.2 %collective-permute-done.12 = f32[1,1024]{1,0:T(1,128)S(1)} collective-permute-done((f32[1,1024]{1,0:T(1,128)S(1)}, f32[1,1024]{1,0:T(1,128)S(1)}, u32[]{:S(2)}, u32[]{:S(2)}) %collective-permute-start.12) | collective-permute-done | bytes 4128 | tf_op jit(solution)/shard_map/ppermute | solution.py:227
  75.6 1.9 %collective-permute-start.13 = (f32[1,1024]{1,0:T(1,128)S(1)}, f32[1,1024]{1,0:T(1,128)S(1)}, u32[]{:S(2)}, u32[]{:S(2)}) collective-permute-start(f32[1,1024]{1,0:T(1,128)S(1)} %add.34), channel_id=1, source_target_pairs={{0,8},{4,12},{8,0},{12,4},{16,24},{20,28},{24,16},{28,20},{1,9},{5... | collective-permute-start | bytes 12296 | tf_op jit(solution)/shard_map/ppermute | solution.py:227
  77.5 2.9 %collective-permute-start.6 = (f32[4,176]{1,0:T(4,128)S(1)}, f32[4,176]{1,0:T(4,128)S(1)}, u32[]{:S(2)}, u32[]{:S(2)}) collective-permute-start(f32[4,176]{1,0:T(4,128)S(1)} %shard_map.56.refs_2_), channel_id=1, source_target_pairs={{0,16},{4,20},{8,24},{12,28},{16,0},{20,4},{24,8},{28,12},{1,17},{... | collective-permute-start | bytes 8456 | tf_op jit(solution)/shard_map/ppermute | solution.py:227
  80.5 1.6 %collective-permute-start.14 = (f32[1,1024]{1,0:T(1,128)S(1)}, f32[1,1024]{1,0:T(1,128)S(1)}, u32[]{:S(2)}, u32[]{:S(2)}) collective-permute-start(f32[1,1024]{1,0:T(1,128)S(1)} %add.35), channel_id=1, source_target_pairs={{0,16},{4,20},{8,24},{12,28},{16,0},{20,4},{24,8},{28,12},{1,17},{... | collective-permute-start | bytes 12296 | tf_op jit(solution)/shard_map/ppermute | solution.py:227
  82.0 3.0 %shard_map.60 = (f32[352,1024]{1,0:T(8,128)S(1)}, f32[1,1024]{1,0:T(1,128)}) custom-call(bf16[176,1536]{1,0:T(8,128)(2,1)S(1)} %pad_maximum_fusion.refs_0_.refs_8_, bf16[176,1536]{1,0:T(8,128)(2,1)S(1)} %collective-permute-done.5.refs_1_.refs_9_, f32[4,176]{1,0:T(4,128)S(1)} %collective-permute-done.6.refs_2_, bf16[1024,1536]{1,0:T(8,128)(2,1)S(1)} %shard_map.57.refs_3_), custom_call_target="tpu_custom_call" | custom-call | flops 1107296256 | bytes 5675776 | tf_op jit(solution)/shard_map/pallas_call | solution.py:214
  85.1 3.0 %shard_map.61 = (f32[352,1024]{1,0:T(8,128)S(1)}, f32[1,1024]{1,0:T(1,128)}) custom-call(bf16[176,1536]{1,0:T(8,128)(2,1)S(1)} %collective-permute-done.7.refs_0_.refs_10_, bf16[176,1536]{1,0:T(8,128)(2,1)S(1)} %collective-permute-done.8.refs_1_.refs_11_, f32[4,176]{1,0:T(4,128)S(1)} %collective-permute-done.6.refs_2_, bf16[1024,1536]{1,0:T(8,128)(2,1)S(1)} %shard_map.57.refs_3_), custom_call_target="tpu_custom_call" | custom-call | flops 1107296256 | bytes 5675776 | tf_op jit(solution)/shard_map/pallas_call | solution.py:214
  88.1 4.0 %shard_map.63 = (f32[2,128,768]{2,1,0:T(8,128)S(1)}, f32[2,128,768]{2,1,0:T(8,128)S(1)}, bf16[2,128,768]{2,1,0:T(8,128)(2,1)}, bf16[2,128,768]{2,1,0:T(8,128)(2,1)S(1)}) custom-call(f32[352,1024]{1,0:T(8,128)S(1)} %get-tuple-element.15.refs_0_, f32[352,1024]{1,0:T(8,128)S(1)} %get-tuple-element.16.refs_1_, f32[352,1024]{1,0:T(8,128)S(1)} %get-tuple-element.17.refs_2_, ...), custom_call_target="tpu_custom_call" | custom-call | flops 2214592512 | bytes 12455936 | tf_op jit(solution)/shard_map/pallas_call | solution.py:214
  92.2 0.9 copy-done.1
  93.1 0.9 copy-done.3
  94.0 1.5 %collective-permute-start.15 = (bf16[2,128,768]{2,1,0:T(8,128)(2,1)}, bf16[2,128,768]{2,1,0:T(8,128)(2,1)}, u32[]{:S(2)}, u32[]{:S(2)}) collective-permute-start(bf16[2,128,768]{2,1,0:T(8,128)(2,1)} %get-tuple-element.22), channel_id=1, source_target_pairs={{0,4},{4,0},{8,12},{12,8},{16,20},{20,16},{24,28},{28,24},{1,5},{5... | collective-permute-start | bytes 1179656 | tf_op jit(solution)/shard_map/ppermute | solution.py:227
  95.5 2.0 %collective-permute-start.17 = (bf16[2,128,768]{2,1,0:T(8,128)(2,1)S(1)}, bf16[2,128,768]{2,1,0:T(8,128)(2,1)S(1)}, u32[]{:S(2)}, u32[]{:S(2)}) collective-permute-start(bf16[2,128,768]{2,1,0:T(8,128)(2,1)S(1)} %get-tuple-element.24), channel_id=1, source_target_pairs={{0,8},{4,12},{8,0},{12,4},{16,24},{20,28},{24,16},{28,20},{1,9},{5... | collective-permute-start | bytes 1179656 | tf_op jit(solution)/shard_map/ppermute | solution.py:227
  97.6 5.3 %collective-permute-done.15 = bf16[2,128,768]{2,1,0:T(8,128)(2,1)} collective-permute-done((bf16[2,128,768]{2,1,0:T(8,128)(2,1)}, bf16[2,128,768]{2,1,0:T(8,128)(2,1)}, u32[]{:S(2)}, u32[]{:S(2)}) %collective-permute-start.15) | collective-permute-done | bytes 393248 | tf_op jit(solution)/shard_map/ppermute | solution.py:227
  102.9 1.2 %add_convert_fusion.1 = (bf16[1,128,768]{2,1,0:T(8,128)(2,1)S(1)}, f32[128,768]{1,0:T(8,128)S(1)}) fusion(f32[2,128,768]{2,1,0:T(8,128)} %copy-done.3, bf16[2,128,768]{2,1,0:T(8,128)(2,1)} %collective-permute-done.15), kind=kLoop, calls=%fused_computation.3 | loop fusion | flops 294912 | bytes 1572864 | tf_op jit(solution)/shard_map/convert_element_type | solution.py:337
  104.1 3.4 %collective-permute-start.16 = (bf16[1,128,768]{2,1,0:T(8,128)(2,1)S(1)}, bf16[1,128,768]{2,1,0:T(8,128)(2,1)S(1)}, u32[]{:S(2)}, u32[]{:S(2)}) collective-permute-start(bf16[1,128,768]{2,1,0:T(8,128)(2,1)S(1)} %get-tuple-element.27), channel_id=1, source_target_pairs={{0,8},{4,12},{8,0},{12,4},{16,24},{20,28},{24,16},{28,20},{1,9},{5... | collective-permute-start | bytes 589832 | tf_op jit(solution)/shard_map/ppermute | solution.py:227
  107.5 0.1 add_convert_fusion
  107.6 1.6 %collective-permute-start.18 = (bf16[1,128,768]{2,1,0:T(8,128)(2,1)S(1)}, bf16[1,128,768]{2,1,0:T(8,128)(2,1)S(1)}, u32[]{:S(2)}, u32[]{:S(2)}) collective-permute-start(bf16[1,128,768]{2,1,0:T(8,128)(2,1)S(1)} %get-tuple-element.25), channel_id=1, source_target_pairs={{0,4},{4,0},{8,12},{12,8},{16,20},{20,16},{24,28},{28,24},{1,5},{5... | collective-permute-start | bytes 589832 | tf_op jit(solution)/shard_map/ppermute | solution.py:227
  109.1 0.9 slice_bitcast_fusion.3.refs_1_
  110.1 1.0 collective-permute-done.16
  111.2 2.1 %collective-permute-done.18 = bf16[1,128,768]{2,1,0:T(8,128)(2,1)S(1)} collective-permute-done((bf16[1,128,768]{2,1,0:T(8,128)(2,1)S(1)}, bf16[1,128,768]{2,1,0:T(8,128)(2,1)S(1)}, u32[]{:S(2)}, u32[]{:S(2)}) %collective-permute-start.18) | collective-permute-done | bytes 196640 | tf_op jit(solution)/shard_map/ppermute | solution.py:227
  113.3 1.1 shard_map.64
  (37 shorter events, 0.2 us)
Async XLA Ops:
  1.9 1.1 copy-start.4
  3.0 0.7 copy-start.5
  3.7 0.7 copy-start.7
  5.2 48.3 %copy-start = (bf16[1,1024,1536]{2,1,0:T(8,128)(2,1)S(1)}, bf16[1,1024,1536]{2,1,0:T(8,128)(2,1)}, u32[]{:S(2)}) copy-start(bf16[1,1024,1536]{2,1,0:T(8,128)(2,1)} %param.9) | copy-start | bytes 9437188
  5.3 46.7 %copy-start.6 = (s32[64]{0:T(128)S(1)}, s32[64]{0:T(128)}, u32[]{:S(2)}) copy-start(s32[64]{0:T(128)} %param.7) | copy-start | bytes 772
  5.3 46.7 %copy-start.8 = (s32[64]{0:T(128)S(1)}, s32[64]{0:T(128)}, u32[]{:S(2)}) copy-start(s32[64]{0:T(128)} %param.8) | copy-start | bytes 772
  5.3 34.1 %collective-permute-start.3 = (bf16[176,1536]{1,0:T(8,128)(2,1)S(1)}, bf16[176,1536]{1,0:T(8,128)(2,1)S(1)}, u32[]{:S(2)}, u32[]{:S(2)}) collective-permute-start(bf16[176,1536]{1,0:T(8,128)(2,1)S(1)} %get-tuple-element.29), channel_id=1, source_target_pairs={{0,16},{4,20},{8,24},{12,28},{16,0},{20,4},{24,8},{28,12},{1,17},{... | collective-permute-start | bytes 1622024 | tf_op jit(solution)/shard_map/ppermute | solution.py:227
  9.4 31.8 %collective-permute-start.1 = (bf16[176,1536]{1,0:T(8,128)(2,1)S(1)}, bf16[176,1536]{1,0:T(8,128)(2,1)S(1)}, u32[]{:S(2)}, u32[]{:S(2)}) collective-permute-start(bf16[176,1536]{1,0:T(8,128)(2,1)S(1)} %get-tuple-element.29), channel_id=1, source_target_pairs={{0,2},{1,3},{2,0},{3,1},{4,6},{5,7},{6,4},{7,5},{8,10},{9,11},{10,... | collective-permute-start | bytes 1622024 | tf_op jit(solution)/shard_map/ppermute | solution.py:227
  10.9 32.9 %collective-permute-start.4 = (bf16[80,1536]{1,0:T(8,128)(2,1)S(1)}, bf16[80,1536]{1,0:T(8,128)(2,1)S(1)}, u32[]{:S(2)}, u32[]{:S(2)}) collective-permute-start(bf16[80,1536]{1,0:T(8,128)(2,1)S(1)} %slice.49), channel_id=1, source_target_pairs={{0,16},{4,20},{8,24},{12,28},{16,0},{20,4},{24,8},{28,12},{1,17},{... | collective-permute-start | bytes 737288 | tf_op jit(solution)/shard_map/ppermute | solution.py:227
  39.4 12.6 %collective-permute-start.7 = (bf16[176,1536]{1,0:T(8,128)(2,1)S(1)}, bf16[176,1536]{1,0:T(8,128)(2,1)S(1)}, u32[]{:S(2)}, u32[]{:S(2)}) collective-permute-start(bf16[176,1536]{1,0:T(8,128)(2,1)S(1)} %collective-permute-done.3), channel_id=1, source_target_pairs={{0,2},{1,3},{2,0},{3,1},{4,6},{5,7},{6,4},{7,5},{8,10},{9,11},{10,... | collective-permute-start | bytes 1622024 | tf_op jit(solution)/shard_map/ppermute | solution.py:227
  41.2 13.2 %collective-permute-start = (bf16[176,1536]{1,0:T(8,128)(2,1)S(1)}, bf16[176,1536]{1,0:T(8,128)(2,1)S(1)}, u32[]{:S(2)}, u32[]{:S(2)}) collective-permute-start(bf16[176,1536]{1,0:T(8,128)(2,1)S(1)} %get-tuple-element.30.refs_0_.refs_4_), channel_id=1, source_target_pairs={{0,1},{1,0},{2,3},{3,2},{4,5},{5,4},{6,7},{7,6},{8,9},{9,8},{10,11... | collective-permute-start | bytes 1622024 | tf_op jit(solution)/shard_map/ppermute | solution.py:227
  41.2 15.8 %collective-permute-start.2 = (bf16[176,1536]{1,0:T(8,128)(2,1)S(1)}, bf16[176,1536]{1,0:T(8,128)(2,1)S(1)}, u32[]{:S(2)}, u32[]{:S(2)}) collective-permute-start(bf16[176,1536]{1,0:T(8,128)(2,1)S(1)} %collective-permute-done.1.refs_0_.refs_6_), channel_id=1, source_target_pairs={{0,1},{1,0},{2,3},{3,2},{4,5},{5,4},{6,7},{7,6},{8,9},{9,8},{10,11... | collective-permute-start | bytes 1622024 | tf_op jit(solution)/shard_map/ppermute | solution.py:227
  43.9 38.2 %collective-permute-start.5 = (bf16[176,1536]{1,0:T(8,128)(2,1)S(1)}, bf16[176,1536]{1,0:T(8,128)(2,1)S(1)}, u32[]{:S(2)}, u32[]{:S(2)}) collective-permute-start(bf16[176,1536]{1,0:T(8,128)(2,1)S(1)} %pad_maximum_fusion.refs_0_.refs_8_), channel_id=1, source_target_pairs={{0,1},{1,0},{2,3},{3,2},{4,5},{5,4},{6,7},{7,6},{8,9},{9,8},{10,11... | collective-permute-start | bytes 1622024 | tf_op jit(solution)/shard_map/ppermute | solution.py:227
  52.0 33.1 %collective-permute-start.8 = (bf16[176,1536]{1,0:T(8,128)(2,1)S(1)}, bf16[176,1536]{1,0:T(8,128)(2,1)S(1)}, u32[]{:S(2)}, u32[]{:S(2)}) collective-permute-start(bf16[176,1536]{1,0:T(8,128)(2,1)S(1)} %collective-permute-done.7.refs_0_.refs_10_), channel_id=1, source_target_pairs={{0,1},{1,0},{2,3},{3,2},{4,5},{5,4},{6,7},{7,6},{8,9},{9,8},{10,11... | collective-permute-start | bytes 1622024 | tf_op jit(solution)/shard_map/ppermute | solution.py:227
  59.5 3.7 %collective-permute-start.9 = (f32[1,1024]{1,0:T(1,128)S(1)}, f32[1,1024]{1,0:T(1,128)S(1)}, u32[]{:S(2)}, u32[]{:S(2)}) collective-permute-start(f32[1,1024]{1,0:T(1,128)S(1)} %add.30), channel_id=1, source_target_pairs={{0,4},{4,0},{8,12},{12,8},{16,20},{20,16},{24,28},{28,24},{1,5},{5... | collective-permute-start | bytes 12296 | tf_op jit(solution)/shard_map/ppermute | solution.py:227
  63.2 3.6 %collective-permute-start.10 = (f32[1,1024]{1,0:T(1,128)S(1)}, f32[1,1024]{1,0:T(1,128)S(1)}, u32[]{:S(2)}, u32[]{:S(2)}) collective-permute-start(f32[1,1024]{1,0:T(1,128)S(1)} %add.31), channel_id=1, source_target_pairs={{0,8},{4,12},{8,0},{12,4},{16,24},{20,28},{24,16},{28,20},{1,9},{5... | collective-permute-start | bytes 12296 | tf_op jit(solution)/shard_map/ppermute | solution.py:227
  66.8 4.5 %collective-permute-start.11 = (f32[1,1024]{1,0:T(1,128)S(1)}, f32[1,1024]{1,0:T(1,128)S(1)}, u32[]{:S(2)}, u32[]{:S(2)}) collective-permute-start(f32[1,1024]{1,0:T(1,128)S(1)} %add.32), channel_id=1, source_target_pairs={{0,16},{4,20},{8,24},{12,28},{16,0},{20,4},{24,8},{28,12},{1,17},{... | collective-permute-start | bytes 12296 | tf_op jit(solution)/shard_map/ppermute | solution.py:227
  71.9 3.7 %collective-permute-start.12 = (f32[1,1024]{1,0:T(1,128)S(1)}, f32[1,1024]{1,0:T(1,128)S(1)}, u32[]{:S(2)}, u32[]{:S(2)}) collective-permute-start(f32[1,1024]{1,0:T(1,128)S(1)} %shard_map.62), channel_id=1, source_target_pairs={{0,4},{4,0},{8,12},{12,8},{16,20},{20,16},{24,28},{28,24},{1,5},{5... | collective-permute-start | bytes 12296 | tf_op jit(solution)/shard_map/ppermute | solution.py:227
  75.6 4.8 %collective-permute-start.13 = (f32[1,1024]{1,0:T(1,128)S(1)}, f32[1,1024]{1,0:T(1,128)S(1)}, u32[]{:S(2)}, u32[]{:S(2)}) collective-permute-start(f32[1,1024]{1,0:T(1,128)S(1)} %add.34), channel_id=1, source_target_pairs={{0,8},{4,12},{8,0},{12,4},{16,24},{20,28},{24,16},{28,20},{1,9},{5... | collective-permute-start | bytes 12296 | tf_op jit(solution)/shard_map/ppermute | solution.py:227
  77.5 4.5 %collective-permute-start.6 = (f32[4,176]{1,0:T(4,128)S(1)}, f32[4,176]{1,0:T(4,128)S(1)}, u32[]{:S(2)}, u32[]{:S(2)}) collective-permute-start(f32[4,176]{1,0:T(4,128)S(1)} %shard_map.56.refs_2_), channel_id=1, source_target_pairs={{0,16},{4,20},{8,24},{12,28},{16,0},{20,4},{24,8},{28,12},{1,17},{... | collective-permute-start | bytes 8456 | tf_op jit(solution)/shard_map/ppermute | solution.py:227
  80.5 4.6 %collective-permute-start.14 = (f32[1,1024]{1,0:T(1,128)S(1)}, f32[1,1024]{1,0:T(1,128)S(1)}, u32[]{:S(2)}, u32[]{:S(2)}) collective-permute-start(f32[1,1024]{1,0:T(1,128)S(1)} %add.35), channel_id=1, source_target_pairs={{0,16},{4,20},{8,24},{12,28},{16,0},{20,4},{24,8},{28,12},{1,17},{... | collective-permute-start | bytes 12296 | tf_op jit(solution)/shard_map/ppermute | solution.py:227
  92.2 0.9 copy-start.1
  93.1 0.9 copy-start.3
  94.0 8.8 %collective-permute-start.15 = (bf16[2,128,768]{2,1,0:T(8,128)(2,1)}, bf16[2,128,768]{2,1,0:T(8,128)(2,1)}, u32[]{:S(2)}, u32[]{:S(2)}) collective-permute-start(bf16[2,128,768]{2,1,0:T(8,128)(2,1)} %get-tuple-element.22), channel_id=1, source_target_pairs={{0,4},{4,0},{8,12},{12,8},{16,20},{20,16},{24,28},{28,24},{1,5},{5... | collective-permute-start | bytes 1179656 | tf_op jit(solution)/shard_map/ppermute | solution.py:227
  95.5 12.0 %copy-start.2 = (f32[2,128,768]{2,1,0:T(8,128)S(1)}, f32[2,128,768]{2,1,0:T(8,128)}, u32[]{:S(2)}) copy-start(f32[2,128,768]{2,1,0:T(8,128)} %copy-done.1) | copy-start | bytes 2359300
  95.5 12.0 %collective-permute-start.17 = (bf16[2,128,768]{2,1,0:T(8,128)(2,1)S(1)}, bf16[2,128,768]{2,1,0:T(8,128)(2,1)S(1)}, u32[]{:S(2)}, u32[]{:S(2)}) collective-permute-start(bf16[2,128,768]{2,1,0:T(8,128)(2,1)S(1)} %get-tuple-element.24), channel_id=1, source_target_pairs={{0,8},{4,12},{8,0},{12,4},{16,24},{20,28},{24,16},{28,20},{1,9},{5... | collective-permute-start | bytes 1179656 | tf_op jit(solution)/shard_map/ppermute | solution.py:227
  104.1 7.1 %collective-permute-start.16 = (bf16[1,128,768]{2,1,0:T(8,128)(2,1)S(1)}, bf16[1,128,768]{2,1,0:T(8,128)(2,1)S(1)}, u32[]{:S(2)}, u32[]{:S(2)}) collective-permute-start(bf16[1,128,768]{2,1,0:T(8,128)(2,1)S(1)} %get-tuple-element.27), channel_id=1, source_target_pairs={{0,8},{4,12},{8,0},{12,4},{16,24},{20,28},{24,16},{28,20},{1,9},{5... | collective-permute-start | bytes 589832 | tf_op jit(solution)/shard_map/ppermute | solution.py:227
  107.6 5.7 %collective-permute-start.18 = (bf16[1,128,768]{2,1,0:T(8,128)(2,1)S(1)}, bf16[1,128,768]{2,1,0:T(8,128)(2,1)S(1)}, u32[]{:S(2)}, u32[]{:S(2)}) collective-permute-start(bf16[1,128,768]{2,1,0:T(8,128)(2,1)S(1)} %get-tuple-element.25), channel_id=1, source_target_pairs={{0,4},{4,0},{8,12},{12,8},{16,20},{20,16},{24,28},{28,24},{1,5},{5... | collective-permute-start | bytes 589832 | tf_op jit(solution)/shard_map/ppermute | solution.py:227

commit v2 on v1

v2 whole, which is shorter than its diff:
```python
import functools

import jax
import jax.numpy as jnp
from jax import lax
from jax.experimental import pallas as pl
from jax.experimental.pallas import tpu as pltpu
from jax.sharding import PartitionSpec as P

F32 = jnp.float32
BF16 = jnp.bfloat16
I32 = jnp.int32
CORES = 2
ROWS = 16
LANES = 128
OWNER_SHIFT = 1 << 17
FIRST_SHIFT = 1 << 7


def down(value):
    return value // ROWS * ROWS


def up(value):
    return -(-value // ROWS) * ROWS


def iota(shape, dim):
    return lax.broadcasted_iota(I32, shape, dim)


def unit_rms(values):
    values = values.astype(F32)
    return values * lax.rsqrt(jnp.mean(values * values, axis=-1, keepdims=True) + 1e-06)


def windows(tok, owners):
    chips = owners // CORES
    full = 2 * tok // owners
    least = CORES * ((tok - full) // max(owners - 1, 1))
    starts = [down(j * least) for j in range(chips)]
    ends = [up(tok - (chips - 1 - j) * least) for j in range(chips)]
    wide = max(e - s for s, e in zip(starts, ends))
    starts = [min(s, tok - wide) for s in starts]
    return starts, wide


def to_col(row):
    n = row.shape[1]
    return jnp.sum(jnp.where(iota((n, n), 0) == iota((n, n), 1), row, 0.0), axis=1, keepdims=True)


def to_row(col):
    n = col.shape[0]
    return jnp.sum(jnp.where(iota((n, n), 0) == iota((n, n), 1), col, 0.0), axis=0, keepdims=True)


def owner_codes(owner_ref, count_ref):
    owner = owner_ref[...].astype(F32)
    count = count_ref[...].astype(F32)
    n = owner.shape[1]
    earlier = (to_col(owner) == owner) & (iota((n, n), 0) < iota((n, n), 1))
    first = jnp.sum(jnp.where(earlier, to_col(count), 0.0), axis=0, keepdims=True)
    return owner * OWNER_SHIFT + first * FIRST_SHIFT + count


def code_and_key(parent_row, code_row, chip, chips):
    parent = to_col(parent_row.astype(F32)).astype(I32)
    tok = parent.shape[0]
    n = code_row.shape[1]
    code = jnp.sum(jnp.where(parent == iota((tok, n), 1), code_row, 0.0), axis=1, keepdims=True)
    owner = code.astype(I32) // OWNER_SHIFT
    order = (chips - 1) - ((owner // CORES) ^ chip)
    key = (order * tok + iota((tok, 1), 0)).astype(F32)
    return code, key


def fetch(pairs, sems):
    copies = [pltpu.make_async_copy(src, dst, sems.at[k]) for k, (src, dst) in enumerate(pairs)]
    for copy in copies:
        copy.start()
    return copies


def sort_kernel(chips, ranges, *refs):
    points_ref, parents_ref, owner_ref, count_ref = refs[:4]
    out_refs, (points, parents, owner, count, sems) = refs[4:-5], refs[-5:]
    copies = fetch(
        [(points_ref, points), (parents_ref, parents), (owner_ref, owner), (count_ref, count)], sems
    )
    me = lax.axis_index("own")
    tok = points.shape[0]
    for copy in copies[1:]:
        copy.wait()
    code_row = owner_codes(owner, count)
    parent = parents[:, pl.ds(pl.multiple_of(me * tok, tok), tok)]
    code, key = code_and_key(parent, code_row, me // CORES, chips)
    key_row = to_row(key)
    place = jnp.sum(jnp.where(key < key_row, 1.0, 0.0), axis=0, keepdims=True).astype(I32)
    pick = jnp.where(iota((tok, tok), 0) == place, 1.0, 0.0).astype(BF16)
    copies[0].wait()
    unit = unit_rms(points[...]).astype(BF16)
    ordered = jnp.dot(pick, unit, preferred_element_type=F32).astype(BF16)
    for (lo, hi), out_ref in zip(ranges, out_refs):
        out_ref[...] = ordered[lo:hi]


def codes_kernel(chips, starts, tok, parents_ref, owner_ref, count_ref, out_ref, parents, owner, count, sems):
    for copy in fetch([(parents_ref, parents), (owner_ref, owner), (count_ref, count)], sems):
        copy.wait()
    me = lax.axis_index("own")
    code_row = owner_codes(owner, count)
    wide = out_ref.shape[1]
    for rel in range(out_ref.shape[0]):
        parent = parents[:, pl.ds(pl.multiple_of((me ^ rel) * tok, tok), tok)]
        code, key = code_and_key(parent, code_row, (me ^ rel) // CORES, chips)
        place = jnp.sum(jnp.where(to_row(key) < key, 1.0, 0.0), axis=1, keepdims=True).astype(I32)
        start = starts[chips - 1 - rel // CORES]
        hit = place == iota((tok, wide), 1) + start
        out_ref[rel : rel + 1, :] = jnp.sum(jnp.where(hit, code, 0.0), axis=0, keepdims=True)


def cent_kernel(in_ref, out_ref):
    out_ref[...] = unit_rms(in_ref[...]).astype(BF16)


def weights_kernel(rels, tile, skips, *refs):
    row_refs, (codes_ref, cent_ref, w_ref, sum_ref, rows_ref, low_ref, high_ref) = refs[:-7], refs[-7:]
    me = lax.axis_index("own")
    slots, width = cent_ref.shape
    wide = codes_ref.shape[1]
    at = 0
    for row_ref, skip in zip(row_refs, skips):
        size = row_ref.shape[0] - skip
        rows_ref[at : at + size, :] = row_ref[skip:, :]
        at += size
    for k, rel in enumerate(rels):
        part = slice(k * wide, (k + 1) * wide)
        code = to_col(codes_ref[rel : rel + 1, :]).astype(I32)
        first = (code % OWNER_SHIFT) // FIRST_SHIFT
        low = jnp.where(code // OWNER_SHIFT == me, first, slots)
        low_ref[part, :] = low
        high_ref[part, :] = low + code % FIRST_SHIFT

    def step(i, carry):
        at = pl.multiple_of(i * tile, tile)
        cent = cent_ref[pl.ds(at, tile), :]
        scores = lax.dot_general(rows_ref[...], cent, (((1,), (1,)), ((), ())), preferred_element_type=F32)
        slot = iota(scores.shape, 1) + at
        live = (slot >= low_ref[...]) & (slot < high_ref[...])
        w = jnp.where(live, jnp.exp(scores * (1.0 / (width * 0.05))), 0.0)
        w_ref[:, pl.ds(at, tile)] = w
        sum_ref[:, pl.ds(at, tile)] = jnp.sum(w, axis=0, keepdims=True)
        return carry

    lax.fori_loop(0, slots // tile, step, 0)


def inverse(values):
    return jnp.where(values > 0.0, 1.0 / jnp.where(values > 0.0, values, 1.0), 0.0)


def balance_kernel(n, *refs):
    w_refs, col_ref, out_ref = refs[:n], refs[n], refs[n + 1]
    scale = inverse(col_ref[...])
    total = jnp.zeros_like(scale)
    for w_ref in w_refs:
        rows = w_ref.shape[0]
        for at in range(0, rows, ROWS * 2):
            w = w_ref[at : at + ROWS * 2, :]
            row = jnp.sum(w * scale, axis=1, keepdims=True)
            total = total + jnp.sum(w * inverse(row), axis=0, keepdims=True)
    out_ref[...] = total


def assign_kernel(half_bit, *refs):
    w_refs, (t_ref, assign_ref) = refs[:-2], refs[-2:]
    scale = inverse(t_ref[...])
    half = assign_ref.shape[1]
    upper = (lax.axis_index("pts") // half_bit) % 2
    at = 0
    for w_ref in w_refs:
        for lo in range(0, w_ref.shape[0], ROWS * 2):
            w = w_ref[lo : lo + ROWS * 2, :] * scale
            row = inverse(jnp.sum(w, axis=1, keepdims=True))
            mine = jnp.where(upper == 0, w[:, :half], w[:, half:])
            assign_ref[at : at + ROWS * 2, :] = (mine * row).astype(BF16)
            at += ROWS * 2


def move_kernel(routes, half_bit, assign_ref, row_refs, out_refs, part_ref):
    low = lax.axis_index("pts") % half_bit
    for which, (order, out_ref) in enumerate(zip(routes, out_refs)):
        share, cols = out_ref.shape[1:]
        block = part_ref.shape[0]
        lanes = slice(which * cols, (which + 1) * cols)
        for k, rel in enumerate(order):
            start = (low ^ rel) * share
            columns = pl.ds(pl.multiple_of(start // block * block, block), block)
            moved, at = 0.0, 0
            for r in row_refs:
                a = assign_ref[at : at + r.shape[0], columns]
                moved = moved + lax.dot_general(
                    a, r[:, lanes], (((0,), (0,)), ((), ())), preferred_element_type=F32
                )
                at += r.shape[0]
            if share < block:
                part_ref[...] = moved
                moved = part_ref[pl.ds(pl.multiple_of(start % block, share), share), :]
            out_ref[k] = moved.astype(out_ref.dtype)


def send_kernel(routes, half_bit, nw, *refs):
    n = len(routes)
    row_refs, out_refs = refs[nw + 1 : -n - 2], refs[-n - 2 : -2]
    assign_ref, part_ref = refs[-2:]
    assign_kernel(half_bit, *refs[: nw + 1], assign_ref)
    move_kernel(routes, half_bit, assign_ref, row_refs, out_refs, part_ref)


def keep_kernel(routes, half_bit, *refs):
    n = len(routes)
    move_kernel(routes, half_bit, refs[0], refs[1 : -n - 1], refs[-n - 1 : -1], refs[-1])


def merge_kernel(keep_ref, came_ref, *out_refs):
    total = keep_ref[...] + came_ref[...].astype(F32)
    n = total.shape[0] // 2
    out_refs[0][...] = total[:n]
    out_refs[1][...] = total[n:].astype(BF16)


def final_kernel(nroute, nterm, *refs):
    base_ref, out_ref = refs[nroute * nterm], refs[nroute * nterm + 1]
    parts = []
    for which in range(nroute):
        total = refs[which * nterm][...].astype(F32)
        for k in range(1, nterm):
            total = total + refs[which * nterm + k][...].astype(F32)
        parts.append(total)
    moved = jnp.concatenate(parts, axis=1)
    out_ref[...] = unit_rms(base_ref[...].astype(F32) + 8.0 * moved).astype(BF16)


def call(kernel, outs, *args, scratch=(), vmem=16, where=pltpu.VMEM):
    shapes = [jax.ShapeDtypeStruct(s, d) for s, d in outs]
    size = sum(a.size * a.dtype.itemsize for a in args) + sum(s.size * s.dtype.itemsize for s in shapes)
    got = pl.pallas_call(
        kernel,
        out_shape=shapes,
        in_specs=[pl.BlockSpec(memory_space=where)] * len(args),
        out_specs=[pl.BlockSpec(memory_space=pltpu.VMEM)] * len(shapes),
        scratch_shapes=list(scratch),
        compiler_params=pltpu.CompilerParams(vmem_limit_bytes=vmem << 20),
        cost_estimate=pl.CostEstimate(flops=0, bytes_accessed=0, transcendentals=0),
    )(*args)
    return got[0] if len(shapes) == 1 else got


def after(values, gate):
    return lax.optimization_barrier((values, gate))[0]


def swap(values, axis, bit):
    return lax.ppermute(values, axis, [(i, i ^ bit) for i in range(lax.axis_size(axis))])


def bit_orders(bits):
    orders = []
    for k in range(len(bits)):
        order = bits[k:] + bits[:k]
        blocks = [0]
        for bit in reversed(order):
            blocks = blocks + [b | bit for b in blocks]
        orders.append((order, blocks))
    return orders


def local(points, parent_of, owner_of, child_count, centroids):
    owners, groups = lax.axis_size("own"), lax.axis_size("pts")
    chips = owners // CORES
    tok, width = points.shape
    slots = centroids.shape[1]
    share = slots // groups
    starts, wide = windows(tok, owners)
    parents = parent_of.T
    table = [owner_of.reshape(1, -1), child_count.reshape(1, -1)]
    half_bit = groups // 2
    small = [pltpu.VMEM(a.shape, I32) for a in [parents, *table]]
    own_start, outward = starts[-1], starts[max(chips - 2, 0)] + wide

    ranges = [(0, outward), (outward, tok), (own_start, tok)]
    head, tail, mine = call(
        functools.partial(sort_kernel, chips, ranges), [((hi - lo, width), BF16) for lo, hi in ranges],
        points, parents, *table,
        scratch=[pltpu.VMEM((tok, width), BF16), *small, pltpu.SemaphoreType.DMA((4,))], where=pl.ANY, vmem=62,
    )

    def across(held, chip):
        start = starts[chips - 1 - chip]
        whole = start == 0 and start + wide == held.shape[0]
        return swap(held if whole else held[start : start + wide], "own", chip * CORES)

    def both(rows):
        return [*rows, *[swap(r, "own", 1) for r in rows]]

    def weigh(blocks, codes, chip, skip):
        rows = wide * CORES
        skips = [skip, 0] * CORES if skip else [0] * len(blocks)
        return call(
            functools.partial(weights_kernel, [chip * CORES, chip * CORES + 1], min(slots, 256), skips),
            [((rows, slots), F32), ((1, slots), F32), ((rows, width), BF16)],
            *blocks, codes, cent,
            scratch=[pltpu.VMEM((rows, 1), I32), pltpu.VMEM((rows, 1), I32)],
        )

    def all_sum(values):
        seen = [values]
        bit = 1
        while bit < groups:
            values = values + swap(values, "pts", bit)
            seen.append(values)
            bit *= 2
        return values, seen

    near = [both([mine])] + [both([across(head, chip)]) for chip in range(1, chips)]
    far_head, far_tail = swap(head, "pts", half_bit), swap(tail, "pts", half_bit)
    codes = call(
        functools.partial(codes_kernel, chips, starts, tok), [((owners, wide), F32)], parents, *table,
        scratch=[*small, pltpu.SemaphoreType.DMA((3,))], where=pl.ANY,
    )
    far_codes = swap(codes, "pts", half_bit)
    cent = call(cent_kernel, [((slots, width), BF16)], centroids[0])

    near_got = [
        weigh(near[chip], codes if chip == 0 else after(codes, far_codes), chip, 0) for chip in range(chips)
    ]
    near_w, near_s, near_x = zip(*near_got)
    column, seen = all_sum(sum(near_s))
    balance, then = all_sum(
        call(functools.partial(balance_kernel, chips), [((1, slots), F32)], *near_w, column)
    )
    far_cross = [across(after(far_head, seen[0]), chip) for chip in range(1, chips)]
    far = [both([after(far_head, column), after(far_tail, column)])] + [both([after(r, then[1])]) for r in far_cross]
    far_got = [
        weigh(far[chip], after(far_codes, then[1] if chip == 0 else then[-2]), chip, own_start if chip == 0 else 0)
        for chip in range(chips)
    ]
    far_w, _, far_x = zip(*far_got)

    bits = []
    bit = 1
    while bit < half_bit:
        bits.append(bit)
        bit *= 2
    orders = bit_orders(bits)
    cols = width // len(orders)
    m = half_bit // 2
    rows = [*near_x, *far_x]
    total_rows = sum(r.shape[0] for r in rows)
    part = pltpu.VMEM((max(share, LANES), cols), F32)
    got = call(
        functools.partial(send_kernel, [b[m:] for _, b in orders], half_bit, 2 * chips),
        [((m, share, cols), BF16)] * len(orders) + [((total_rows, slots // 2), BF16)],
        *near_w, *far_w, balance, *rows, scratch=[part],
    )
    sends, assign = got[:-1], got[-1]
    keeps = call(
        functools.partial(keep_kernel, [b[:m] for _, b in orders], half_bit),
        [((m, share, cols), F32)] * len(orders), assign, *rows, scratch=[part],
    )
    keeps = list(keeps) if len(orders) > 1 else [keeps]
    last = []
    for step in range(len(bits)):
        came = [swap(s, "pts", orders[r][0][step]) for r, s in enumerate(sends)]
        n = came[0].shape[0] // 2
        if n == 0:
            last = came
            break
        sends = []
        for r, c in enumerate(came):
            keeps[r], send = call(
                merge_kernel, [((n, share, cols), F32), ((n, share, cols), BF16)], keeps[r], c, vmem=8
            )
            sends.append(send)
    own = lax.axis_index("pts") * share
    base = lax.dynamic_slice_in_dim(cent, own, share, 0)
    flat = [t.reshape(share, cols) for pair in zip(keeps, last) for t in pair]
    out = call(
        functools.partial(final_kernel, len(orders), 2), [((share, width), BF16)], *flat, base, vmem=8
    )
    return out[None]


def solution(mesh):
    in_specs = (P(("pts", "own"), None), P("pts", None), P(), P(), P("own", None, None))
    out_specs = P("own", "pts", None)
    return jax.shard_map(local, mesh=mesh, in_specs=in_specs, out_specs=out_specs, check_vma=False)
```

time: 115 us -> 123 us (1.070)
  waiting for transfers between devices: 55 us -> 64.4 us
  starting transfers between devices: 30.5 us -> 21.5 us
  local copies, waits for them, and re-layouts: 5.91 us -> 11.4 us
  Pallas kernels: 20.1 us -> 24.5 us
  other arithmetic: 2.7 us -> 0.04 us
    ppermute x19 -> x20, waiting for transfers between devices: 55 us -> 64.4 us  [swap(): lax.ppermute(values, axis, [(i, i ^ bit) for i in range(lax.axis_size(axi...]
    ppermute x19 -> x20, starting transfers between devices: 30.5 us -> 21.5 us  [swap(): lax.ppermute(values, axis, [(i, i ^ bit) for i in range(lax.axis_size(axi...]
    unnamed x19 -> x32, local copies, waits for them, and re-layouts: 4.8 us -> 11.3 us
    pallas_call x10 -> x13, Pallas kernels: 20.1 us -> 24.5 us  [call(): pl.pallas_call(kernel, out_shape=shapes, in_specs=[pl.BlockSpec(memory_sp...]
    unnamed x1 -> x0, other arithmetic: 1.35 us -> none
    convert_element_type x2 -> x0, other arithmetic: 1.27 us -> none  [local(): sends.append(sum((t[n:].astype(F32) for t in terms[r])).astype(BF16))]
  transfers between devices with their start and end apart: 19 -> 20, of which waited for: 10 -> 11; matrix products, arithmetic and copies ran while one was open for 2% -> 0% of each run, Pallas kernels for 10% -> 11%
where the time goes in v2:
time: 123 us; the launch traced here: 122 us
  waiting for transfers between devices  64.4 us (52%)
  Pallas kernels  24.5 us (20%)
  starting transfers between devices  21.5 us (17%)
  local copies, waits for them, and re-layouts  11.4 us (9%)
    ppermute x20, waiting for transfers between devices, swap(): lax.ppermute(values, axis, [(i, i ^ bit) for i in range(lax.axis_size(axi...  64.4 us
    pallas_call x13, Pallas kernels, call(): pl.pallas_call(kernel, out_shape=shapes, in_specs=[pl.BlockSpec(memory_sp...  24.5 us
    ppermute x20, starting transfers between devices, swap(): lax.ppermute(values, axis, [(i, i ^ bit) for i in range(lax.axis_size(axi...  21.5 us
    unnamed x32, local copies, waits for them, and re-layouts  11.3 us
  transfers between devices with their start and end apart: 20, of which 11 were waited for; matrix products, arithmetic and copies ran while one was open for 0% of the time, Pallas kernels for 11%

profile of v2, /device:TPU:0, one launch (start us, length us, event | category | flops | bytes accessed | tf_op | source)
XLA Modules:
  0.0 122.1 jit_solution(1791927785131487597)
XLA Ops:
  0.0 3.1 %shard_map.55 = (bf16[176,1536]{1,0:T(8,128)(2,1)}, bf16[80,1536]{1,0:T(8,128)(2,1)}, bf16[176,1536]{1,0:T(8,128)(2,1)}) custom-call(bf16[256,1536]{1,0:T(8,128)(2,1)} %refs_0_.1, s32[1,1024]{1,0:T(1,128)} %bitcast.14, s32[1,64]{1,0:T(1,128)} %bitcast.16, s32[1,64]{1,0:T(1,128)} %bitcast.18), custom_call_target="tpu_custom_call" | custom-call | tf_op jit(solution)/shard_map/pallas_call | solution.py:248
  3.1 3.0 %collective-permute-start.1 = (bf16[176,1536]{1,0:T(8,128)(2,1)}, bf16[176,1536]{1,0:T(8,128)(2,1)S(1)}, u32[]{:S(2)}, u32[]{:S(2)}) collective-permute-start(bf16[176,1536]{1,0:T(8,128)(2,1)} %get-tuple-element.36), channel_id=1, source_target_pairs={{0,2},{1,3},{2,0},{3,1},{4,6},{5,7},{6,4},{7,5},{8,10},{9,11},{10,... | collective-permute-start | bytes 1622024 | tf_op jit(solution)/shard_map/ppermute | solution.py:265
  6.1 12.5 %collective-permute-done.1.refs_0_ = bf16[176,1536]{1,0:T(8,128)(2,1)S(1)} collective-permute-done((bf16[176,1536]{1,0:T(8,128)(2,1)}, bf16[176,1536]{1,0:T(8,128)(2,1)S(1)}, u32[]{:S(2)}, u32[]{:S(2)}) %collective-permute-start.1) | collective-permute-done | bytes 540704 | tf_op jit(solution)/shard_map/ppermute | solution.py:265
  18.6 2.8 %collective-permute-start.4 = (bf16[176,1536]{1,0:T(8,128)(2,1)}, bf16[176,1536]{1,0:T(8,128)(2,1)S(1)}, u32[]{:S(2)}, u32[]{:S(2)}) collective-permute-start(bf16[176,1536]{1,0:T(8,128)(2,1)} %get-tuple-element.36), channel_id=1, source_target_pairs={{0,16},{4,20},{8,24},{12,28},{16,0},{20,4},{24,8},{28,12},{1,17},{... | collective-permute-start | bytes 1622024 | tf_op jit(solution)/shard_map/ppermute | solution.py:265
  21.4 0.7 copy-done.12
  22.1 0.7 copy-done.13
  22.8 0.7 copy-done.14
  23.4 1.4 %shard_map.56.refs_2_ = f32[4,176]{1,0:T(4,128)S(1)} custom-call(s32[1,1024]{1,0:T(1,128)S(1)} %bitcast.15, s32[1,64]{1,0:T(1,128)S(1)} %bitcast.17, s32[1,64]{1,0:T(1,128)S(1)} %bitcast.19), custom_call_target="tpu_custom_call" | custom-call | tf_op jit(solution)/shard_map/pallas_call | solution.py:248
  24.9 0.2 collective-permute-start.3
  25.0 1.9 %copy-done.8 = bf16[1,1024,1536]{2,1,0:T(8,128)(2,1)S(1)} copy-done((bf16[1,1024,1536]{2,1,0:T(8,128)(2,1)S(1)}, bf16[1,1024,1536]{2,1,0:T(8,128)(2,1)}, u32[]{:S(2)}) %copy-start.8) | copy-done | bytes 3145752
  26.9 1.0 shard_map.57.refs_3_.refs_5_
  27.9 18.4 %collective-permute-done.3.refs_4_.refs_2_ = f32[4,176]{1,0:T(4,128)S(1)} collective-permute-done((f32[4,176]{1,0:T(4,128)S(1)}, f32[4,176]{1,0:T(4,128)S(1)}, u32[]{:S(2)}, u32[]{:S(2)}) %collective-permute-start.3) | collective-permute-done | bytes 2848 | tf_op jit(solution)/shard_map/ppermute | solution.py:265
  46.4 2.4 %shard_map.58 = (f32[352,1024]{1,0:T(8,128)S(1)}, f32[1,1024]{1,0:T(1,128)S(1)}, bf16[352,1536]{1,0:T(8,128)(2,1)S(1)}) custom-call(bf16[176,1536]{1,0:T(8,128)(2,1)S(1)} %copy-done.11, bf16[176,1536]{1,0:T(8,128)(2,1)S(1)} %collective-permute-done.refs_1_, f32[4,176]{1,0:T(4,128)S(1)} %shard_map.56.refs_2_, bf16[1024,1536]{1,0:T(8,128)(2,1)S(1)} %shard_map.57.refs_3_.refs_5_), custom_call_target="tpu_custom_call" | custom-call | tf_op jit(solution)/shard_map/pallas_call | solution.py:248
  48.8 2.5 %shard_map.59 = (f32[352,1024]{1,0:T(8,128)S(1)}, f32[1,1024]{1,0:T(1,128)S(1)}, bf16[352,1536]{1,0:T(8,128)(2,1)S(1)}) custom-call(bf16[176,1536]{1,0:T(8,128)(2,1)S(1)} %collective-permute-done.1.refs_0_, bf16[176,1536]{1,0:T(8,128)(2,1)S(1)} %collective-permute-done.2.refs_1_, f32[4,176]{1,0:T(4,128)S(1)} %shard_map.56.refs_2_, ...), custom_call_target="tpu_custom_call" | custom-call | tf_op jit(solution)/shard_map/pallas_call | solution.py:248
  51.3 1.6 %collective-permute-start.12 = (bf16[176,1536]{1,0:T(8,128)(2,1)S(1)}, bf16[176,1536]{1,0:T(8,128)(2,1)S(1)}, u32[]{:S(2)}, u32[]{:S(2)}) collective-permute-start(bf16[176,1536]{1,0:T(8,128)(2,1)S(1)} %collective-permute-done.4.refs_0_), channel_id=1, source_target_pairs={{0,2},{1,3},{2,0},{3,1},{4,6},{5,7},{6,4},{7,5},{8,10},{9,11},{10,... | collective-permute-start | bytes 1622024 | tf_op jit(solution)/shard_map/ppermute | solution.py:265
  53.0 1.5 %collective-permute-start.5 = (f32[1,1024]{1,0:T(1,128)S(1)}, f32[1,1024]{1,0:T(1,128)S(1)}, u32[]{:S(2)}, u32[]{:S(2)}) collective-permute-start(f32[1,1024]{1,0:T(1,128)S(1)} %add.24), channel_id=1, source_target_pairs={{0,4},{4,0},{8,12},{12,8},{16,20},{20,16},{24,28},{28,24},{1,5},{5... | collective-permute-start | bytes 12296 | tf_op jit(solution)/shard_map/ppermute | solution.py:265
  54.5 2.1 %collective-permute-done.5 = f32[1,1024]{1,0:T(1,128)S(1)} collective-permute-done((f32[1,1024]{1,0:T(1,128)S(1)}, f32[1,1024]{1,0:T(1,128)S(1)}, u32[]{:S(2)}, u32[]{:S(2)}) %collective-permute-start.5) | collective-permute-done | bytes 4128 | tf_op jit(solution)/shard_map/ppermute | solution.py:265
  56.6 0.7 collective-permute-start.6
  57.3 2.9 %collective-permute-done.6 = f32[1,1024]{1,0:T(1,128)S(1)} collective-permute-done((f32[1,1024]{1,0:T(1,128)S(1)}, f32[1,1024]{1,0:T(1,128)S(1)}, u32[]{:S(2)}, u32[]{:S(2)}) %collective-permute-start.6) | collective-permute-done | bytes 4128 | tf_op jit(solution)/shard_map/ppermute | solution.py:265
  60.2 2.0 %collective-permute-start.7 = (f32[1,1024]{1,0:T(1,128)S(1)}, f32[1,1024]{1,0:T(1,128)S(1)}, u32[]{:S(2)}, u32[]{:S(2)}) collective-permute-start(f32[1,1024]{1,0:T(1,128)S(1)} %add.26), channel_id=1, source_target_pairs={{0,16},{4,20},{8,24},{12,28},{16,0},{20,4},{24,8},{28,12},{1,17},{... | collective-permute-start | bytes 12296 | tf_op jit(solution)/shard_map/ppermute | solution.py:265
  62.2 2.5 %collective-permute-done.7 = f32[1,1024]{1,0:T(1,128)S(1)} collective-permute-done((f32[1,1024]{1,0:T(1,128)S(1)}, f32[1,1024]{1,0:T(1,128)S(1)}, u32[]{:S(2)}, u32[]{:S(2)}) %collective-permute-start.7) | collective-permute-done | bytes 4128 | tf_op jit(solution)/shard_map/ppermute | solution.py:265
  64.7 0.6 shard_map.60
  65.3 1.6 %collective-permute-start.11 = (f32[1,1024]{1,0:T(1,128)S(1)}, f32[1,1024]{1,0:T(1,128)S(1)}, u32[]{:S(2)}, u32[]{:S(2)}) collective-permute-start(f32[1,1024]{1,0:T(1,128)S(1)} %shard_map.60), channel_id=1, source_target_pairs={{0,4},{4,0},{8,12},{12,8},{16,20},{20,16},{24,28},{28,24},{1,5},{5... | collective-permute-start | bytes 12296 | tf_op jit(solution)/shard_map/ppermute | solution.py:265
  66.9 2.1 %collective-permute-done.11 = f32[1,1024]{1,0:T(1,128)S(1)} collective-permute-done((f32[1,1024]{1,0:T(1,128)S(1)}, f32[1,1024]{1,0:T(1,128)S(1)}, u32[]{:S(2)}, u32[]{:S(2)}) %collective-permute-start.11) | collective-permute-done | bytes 4128 | tf_op jit(solution)/shard_map/ppermute | solution.py:265
  69.0 2.1 %collective-permute-start.8 = (bf16[80,1536]{1,0:T(8,128)(2,1)S(1)}, bf16[80,1536]{1,0:T(8,128)(2,1)S(1)}, u32[]{:S(2)}, u32[]{:S(2)}) collective-permute-start(bf16[80,1536]{1,0:T(8,128)(2,1)S(1)} %copy-done.15), channel_id=1, source_target_pairs={{0,16},{4,20},{8,24},{12,28},{16,0},{20,4},{24,8},{28,12},{1,17},{... | collective-permute-start | bytes 737288 | tf_op jit(solution)/shard_map/ppermute | solution.py:265
  71.1 12.4 %collective-permute-done.8.refs_1_ = bf16[80,1536]{1,0:T(8,128)(2,1)S(1)} collective-permute-done((bf16[80,1536]{1,0:T(8,128)(2,1)S(1)}, bf16[80,1536]{1,0:T(8,128)(2,1)S(1)}, u32[]{:S(2)}, u32[]{:S(2)}) %collective-permute-start.8) | collective-permute-done | bytes 245792 | tf_op jit(solution)/shard_map/ppermute | solution.py:265
  83.6 0.2 collective-permute-start.14
  83.8 3.4 %collective-permute-done.14 = f32[1,1024]{1,0:T(1,128)S(1)} collective-permute-done((f32[1,1024]{1,0:T(1,128)S(1)}, f32[1,1024]{1,0:T(1,128)S(1)}, u32[]{:S(2)}, u32[]{:S(2)}) %collective-permute-start.14) | collective-permute-done | bytes 4128 | tf_op jit(solution)/shard_map/ppermute | solution.py:265
  87.2 1.5 %collective-permute-start.15 = (f32[1,1024]{1,0:T(1,128)S(1)}, f32[1,1024]{1,0:T(1,128)S(1)}, u32[]{:S(2)}, u32[]{:S(2)}) collective-permute-start(f32[1,1024]{1,0:T(1,128)S(1)} %add.29), channel_id=1, source_target_pairs={{0,16},{4,20},{8,24},{12,28},{16,0},{20,4},{24,8},{28,12},{1,17},{... | collective-permute-start | bytes 12296 | tf_op jit(solution)/shard_map/ppermute | solution.py:265
  88.7 3.0 %collective-permute-done.15 = f32[1,1024]{1,0:T(1,128)S(1)} collective-permute-done((f32[1,1024]{1,0:T(1,128)S(1)}, f32[1,1024]{1,0:T(1,128)S(1)}, u32[]{:S(2)}, u32[]{:S(2)}) %collective-permute-start.15) | collective-permute-done | bytes 4128 | tf_op jit(solution)/shard_map/ppermute | solution.py:265
  91.7 3.1 %shard_map.61 = (f32[352,1024]{1,0:T(8,128)S(1)}, f32[1,1024]{1,0:T(1,128)}, bf16[352,1536]{1,0:T(8,128)(2,1)S(1)}) custom-call(bf16[176,1536]{1,0:T(8,128)(2,1)S(1)} %collective-permute-done.4.refs_0_, bf16[80,1536]{1,0:T(8,128)(2,1)S(1)} %collective-permute-done.8.refs_1_, bf16[176,1536]{1,0:T(8,128)(2,1)S(1)} %collective-permute-done.9.refs_2_, ...), custom_call_target="tpu_custom_call" | custom-call | tf_op jit(solution)/shard_map/pallas_call | solution.py:248
  94.8 3.0 %shard_map.62 = (f32[352,1024]{1,0:T(8,128)S(1)}, f32[1,1024]{1,0:T(1,128)}, bf16[352,1536]{1,0:T(8,128)(2,1)S(1)}) custom-call(bf16[176,1536]{1,0:T(8,128)(2,1)S(1)} %collective-permute-done.12.refs_0_, bf16[176,1536]{1,0:T(8,128)(2,1)S(1)} %collective-permute-done.13.refs_1_, f32[4,176]{1,0:T(4,128)S(1)} %collective-permute-done.3.refs_4_.refs_2_, ...), custom_call_target="tpu_custom_call" | custom-call | tf_op jit(solution)/shard_map/pallas_call | solution.py:248
  97.8 3.4 %shard_map.63 = (bf16[2,128,768]{2,1,0:T(8,128)(2,1)}, bf16[2,128,768]{2,1,0:T(8,128)(2,1)}, bf16[1408,512]{1,0:T(8,128)(2,1)S(1)}) custom-call(f32[352,1024]{1,0:T(8,128)S(1)} %get-tuple-element.35.refs_0_, f32[352,1024]{1,0:T(8,128)S(1)} %get-tuple-element.38.refs_1_, f32[352,1024]{1,0:T(8,128)S(1)} %get-tuple-element.45.refs_2_, ...), custom_call_target="tpu_custom_call" | custom-call | tf_op jit(solution)/shard_map/pallas_call | solution.py:248
  101.3 1.1 copy-done.9
  102.4 1.5 %collective-permute-start.16 = (bf16[2,128,768]{2,1,0:T(8,128)(2,1)}, bf16[2,128,768]{2,1,0:T(8,128)(2,1)}, u32[]{:S(2)}, u32[]{:S(2)}) collective-permute-start(bf16[2,128,768]{2,1,0:T(8,128)(2,1)} %get-tuple-element.56), channel_id=1, source_target_pairs={{0,4},{4,0},{8,12},{12,8},{16,20},{20,16},{24,28},{28,24},{1,5},{5... | collective-permute-start | bytes 1179656 | tf_op jit(solution)/shard_map/ppermute | solution.py:265
  103.9 0.6 collective-permute-start.18
  104.6 1.2 %copy-done.1 = bf16[352,1536]{1,0:T(8,128)(2,1)S(1)} copy-done((bf16[352,1536]{1,0:T(8,128)(2,1)S(1)}, bf16[352,1536]{1,0:T(8,128)(2,1)}, u32[]{:S(2)}) %copy-start.1) | copy-done | bytes 1081368
  105.8 1.2 %copy-done.3 = bf16[352,1536]{1,0:T(8,128)(2,1)S(1)} copy-done((bf16[352,1536]{1,0:T(8,128)(2,1)S(1)}, bf16[352,1536]{1,0:T(8,128)(2,1)}, u32[]{:S(2)}) %copy-start.3) | copy-done | bytes 1081368
  107.0 1.2 %copy-done.5 = bf16[352,1536]{1,0:T(8,128)(2,1)S(1)} copy-done((bf16[352,1536]{1,0:T(8,128)(2,1)S(1)}, bf16[352,1536]{1,0:T(8,128)(2,1)}, u32[]{:S(2)}) %copy-start.5) | copy-done | bytes 1081368
  108.3 1.2 %copy-done.7 = bf16[352,1536]{1,0:T(8,128)(2,1)S(1)} copy-done((bf16[352,1536]{1,0:T(8,128)(2,1)S(1)}, bf16[352,1536]{1,0:T(8,128)(2,1)}, u32[]{:S(2)}) %copy-start.7) | copy-done | bytes 1081368
  109.5 1.4 %copy-done.10 = bf16[1408,512]{1,0:T(8,128)(2,1)S(1)} copy-done((bf16[1408,512]{1,0:T(8,128)(2,1)S(1)}, bf16[1408,512]{1,0:T(8,128)(2,1)}, u32[]{:S(2)}) %copy-start.10) | copy-done | bytes 1441816
  110.9 1.8 %shard_map.64 = (f32[2,128,768]{2,1,0:T(8,128)S(1)}, f32[2,128,768]{2,1,0:T(8,128)S(1)}) custom-call(bf16[1408,512]{1,0:T(8,128)(2,1)S(1)} %copy-done.10, bf16[352,1536]{1,0:T(8,128)(2,1)S(1)} %copy-done.1, bf16[352,1536]{1,0:T(8,128)(2,1)S(1)} %copy-done.3, bf16[352,1536]{1,0:T(8,128)(2,1)S(1)} %copy-done.5, bf16[352,1536]{1,0:T(8,128)(2,1)S(1)} %copy-done.7), custom_call_target="tpu_custom_call" | custom-call | tf_op jit(solution)/shard_map/pallas_call | solution.py:248
  112.7 1.1 shard_map.65
  113.8 1.5 %collective-permute-start.17 = (bf16[1,128,768]{2,1,0:T(8,128)(2,1)S(1)}, bf16[1,128,768]{2,1,0:T(8,128)(2,1)S(1)}, u32[]{:S(2)}, u32[]{:S(2)}) collective-permute-start(bf16[1,128,768]{2,1,0:T(8,128)(2,1)S(1)} %get-tuple-element.58), channel_id=1, source_target_pairs={{0,8},{4,12},{8,0},{12,4},{16,24},{20,28},{24,16},{28,20},{1,9},{5... | collective-permute-start | bytes 589832 | tf_op jit(solution)/shard_map/ppermute | solution.py:265
  115.3 0.6 collective-permute-start.19
  116.0 3.6 %collective-permute-done.17 = bf16[1,128,768]{2,1,0:T(8,128)(2,1)S(1)} collective-permute-done((bf16[1,128,768]{2,1,0:T(8,128)(2,1)S(1)}, bf16[1,128,768]{2,1,0:T(8,128)(2,1)S(1)}, u32[]{:S(2)}, u32[]{:S(2)}) %collective-permute-start.17) | collective-permute-done | bytes 196640 | tf_op jit(solution)/shard_map/ppermute | solution.py:265
  119.5 1.5 %collective-permute-done.19 = bf16[1,128,768]{2,1,0:T(8,128)(2,1)S(1)} collective-permute-done((bf16[1,128,768]{2,1,0:T(8,128)(2,1)S(1)}, bf16[1,128,768]{2,1,0:T(8,128)(2,1)S(1)}, u32[]{:S(2)}, u32[]{:S(2)}) %collective-permute-start.19) | collective-permute-done | bytes 196640 | tf_op jit(solution)/shard_map/ppermute | solution.py:265
  121.1 1.0 shard_map.67
  (45 shorter events, 0.3 us)
Async XLA Ops:
  3.1 15.5 %collective-permute-start.1 = (bf16[176,1536]{1,0:T(8,128)(2,1)}, bf16[176,1536]{1,0:T(8,128)(2,1)S(1)}, u32[]{:S(2)}, u32[]{:S(2)}) collective-permute-start(bf16[176,1536]{1,0:T(8,128)(2,1)} %get-tuple-element.36), channel_id=1, source_target_pairs={{0,2},{1,3},{2,0},{3,1},{4,6},{5,7},{6,4},{7,5},{8,10},{9,11},{10,... | collective-permute-start | bytes 1622024 | tf_op jit(solution)/shard_map/ppermute | solution.py:265
  6.1 40.2 %collective-permute-start = (bf16[176,1536]{1,0:T(8,128)(2,1)}, bf16[176,1536]{1,0:T(8,128)(2,1)S(1)}, u32[]{:S(2)}, u32[]{:S(2)}) collective-permute-start(bf16[176,1536]{1,0:T(8,128)(2,1)} %get-tuple-element.34.refs_0_), channel_id=1, source_target_pairs={{0,1},{1,0},{2,3},{3,2},{4,5},{5,4},{6,7},{7,6},{8,9},{9,8},{10,11... | collective-permute-start | bytes 1622024 | tf_op jit(solution)/shard_map/ppermute | solution.py:265
  18.6 30.2 %collective-permute-start.2 = (bf16[176,1536]{1,0:T(8,128)(2,1)S(1)}, bf16[176,1536]{1,0:T(8,128)(2,1)S(1)}, u32[]{:S(2)}, u32[]{:S(2)}) collective-permute-start(bf16[176,1536]{1,0:T(8,128)(2,1)S(1)} %collective-permute-done.1.refs_0_), channel_id=1, source_target_pairs={{0,1},{1,0},{2,3},{3,2},{4,5},{5,4},{6,7},{7,6},{8,9},{9,8},{10,11... | collective-permute-start | bytes 1622024 | tf_op jit(solution)/shard_map/ppermute | solution.py:265
  18.6 32.7 %collective-permute-start.4 = (bf16[176,1536]{1,0:T(8,128)(2,1)}, bf16[176,1536]{1,0:T(8,128)(2,1)S(1)}, u32[]{:S(2)}, u32[]{:S(2)}) collective-permute-start(bf16[176,1536]{1,0:T(8,128)(2,1)} %get-tuple-element.36), channel_id=1, source_target_pairs={{0,16},{4,20},{8,24},{12,28},{16,0},{20,4},{24,8},{28,12},{1,17},{... | collective-permute-start | bytes 1622024 | tf_op jit(solution)/shard_map/ppermute | solution.py:265
  21.4 0.7 copy-start.12
  22.1 0.7 copy-start.13
  22.8 0.7 copy-start.14
  24.9 21.5 %collective-permute-start.3 = (f32[4,176]{1,0:T(4,128)S(1)}, f32[4,176]{1,0:T(4,128)S(1)}, u32[]{:S(2)}, u32[]{:S(2)}) collective-permute-start(f32[4,176]{1,0:T(4,128)S(1)} %shard_map.56.refs_2_), channel_id=1, source_target_pairs={{0,16},{4,20},{8,24},{12,28},{16,0},{20,4},{24,8},{28,12},{1,17},{... | collective-permute-start | bytes 8456 | tf_op jit(solution)/shard_map/ppermute | solution.py:265
  25.0 1.9 %copy-start.8 = (bf16[1,1024,1536]{2,1,0:T(8,128)(2,1)S(1)}, bf16[1,1024,1536]{2,1,0:T(8,128)(2,1)}, u32[]{:S(2)}) copy-start(bf16[1,1024,1536]{2,1,0:T(8,128)(2,1)} %param.9) | copy-start | bytes 9437188
  26.9 19.4 %copy-start.11 = (bf16[176,1536]{1,0:T(8,128)(2,1)S(1)}, bf16[176,1536]{1,0:T(8,128)(2,1)}, u32[]{:S(2)}) copy-start(bf16[176,1536]{1,0:T(8,128)(2,1)} %get-tuple-element.34.refs_0_) | copy-start | bytes 1622020
  48.8 49.0 %copy-start = (bf16[352,1536]{1,0:T(8,128)(2,1)}, bf16[352,1536]{1,0:T(8,128)(2,1)S(1)}, u32[]{:S(2)}) copy-start(bf16[352,1536]{1,0:T(8,128)(2,1)S(1)} %get-tuple-element.50.refs_5_.refs_1_) | copy-start | bytes 3244036
  51.3 46.5 %copy-start.2 = (bf16[352,1536]{1,0:T(8,128)(2,1)}, bf16[352,1536]{1,0:T(8,128)(2,1)S(1)}, u32[]{:S(2)}) copy-start(bf16[352,1536]{1,0:T(8,128)(2,1)S(1)} %get-tuple-element.51.refs_6_.refs_2_) | copy-start | bytes 3244036
  51.3 17.6 %collective-permute-start.12 = (bf16[176,1536]{1,0:T(8,128)(2,1)S(1)}, bf16[176,1536]{1,0:T(8,128)(2,1)S(1)}, u32[]{:S(2)}, u32[]{:S(2)}) collective-permute-start(bf16[176,1536]{1,0:T(8,128)(2,1)S(1)} %collective-permute-done.4.refs_0_), channel_id=1, source_target_pairs={{0,2},{1,3},{2,0},{3,1},{4,6},{5,7},{6,4},{7,5},{8,10},{9,11},{10,... | collective-permute-start | bytes 1622024 | tf_op jit(solution)/shard_map/ppermute | solution.py:265
  53.0 3.6 %collective-permute-start.5 = (f32[1,1024]{1,0:T(1,128)S(1)}, f32[1,1024]{1,0:T(1,128)S(1)}, u32[]{:S(2)}, u32[]{:S(2)}) collective-permute-start(f32[1,1024]{1,0:T(1,128)S(1)} %add.24), channel_id=1, source_target_pairs={{0,4},{4,0},{8,12},{12,8},{16,20},{20,16},{24,28},{28,24},{1,5},{5... | collective-permute-start | bytes 12296 | tf_op jit(solution)/shard_map/ppermute | solution.py:265
  56.6 3.6 %collective-permute-start.6 = (f32[1,1024]{1,0:T(1,128)S(1)}, f32[1,1024]{1,0:T(1,128)S(1)}, u32[]{:S(2)}, u32[]{:S(2)}) collective-permute-start(f32[1,1024]{1,0:T(1,128)S(1)} %add.25), channel_id=1, source_target_pairs={{0,8},{4,12},{8,0},{12,4},{16,24},{20,28},{24,16},{28,20},{1,9},{5... | collective-permute-start | bytes 12296 | tf_op jit(solution)/shard_map/ppermute | solution.py:265
  60.2 4.5 %collective-permute-start.7 = (f32[1,1024]{1,0:T(1,128)S(1)}, f32[1,1024]{1,0:T(1,128)S(1)}, u32[]{:S(2)}, u32[]{:S(2)}) collective-permute-start(f32[1,1024]{1,0:T(1,128)S(1)} %add.26), channel_id=1, source_target_pairs={{0,16},{4,20},{8,24},{12,28},{16,0},{20,4},{24,8},{28,12},{1,17},{... | collective-permute-start | bytes 12296 | tf_op jit(solution)/shard_map/ppermute | solution.py:265
  64.7 4.3 %copy-start.15 = (bf16[80,1536]{1,0:T(8,128)(2,1)S(1)}, bf16[80,1536]{1,0:T(8,128)(2,1)}, u32[]{:S(2)}) copy-start(bf16[80,1536]{1,0:T(8,128)(2,1)} %get-tuple-element.42) | copy-start | bytes 737284
  65.3 3.7 %collective-permute-start.11 = (f32[1,1024]{1,0:T(1,128)S(1)}, f32[1,1024]{1,0:T(1,128)S(1)}, u32[]{:S(2)}, u32[]{:S(2)}) collective-permute-start(f32[1,1024]{1,0:T(1,128)S(1)} %shard_map.60), channel_id=1, source_target_pairs={{0,4},{4,0},{8,12},{12,8},{16,20},{20,16},{24,28},{28,24},{1,5},{5... | collective-permute-start | bytes 12296 | tf_op jit(solution)/shard_map/ppermute | solution.py:265
  66.9 24.9 %collective-permute-start.9 = (bf16[176,1536]{1,0:T(8,128)(2,1)S(1)}, bf16[176,1536]{1,0:T(8,128)(2,1)S(1)}, u32[]{:S(2)}, u32[]{:S(2)}) collective-permute-start(bf16[176,1536]{1,0:T(8,128)(2,1)S(1)} %collective-permute-done.4.refs_0_), channel_id=1, source_target_pairs={{0,1},{1,0},{2,3},{3,2},{4,5},{5,4},{6,7},{7,6},{8,9},{9,8},{10,11... | collective-permute-start | bytes 1622024 | tf_op jit(solution)/shard_map/ppermute | solution.py:265
  69.0 25.8 %collective-permute-start.13 = (bf16[176,1536]{1,0:T(8,128)(2,1)S(1)}, bf16[176,1536]{1,0:T(8,128)(2,1)S(1)}, u32[]{:S(2)}, u32[]{:S(2)}) collective-permute-start(bf16[176,1536]{1,0:T(8,128)(2,1)S(1)} %collective-permute-done.12.refs_0_), channel_id=1, source_target_pairs={{0,1},{1,0},{2,3},{3,2},{4,5},{5,4},{6,7},{7,6},{8,9},{9,8},{10,11... | collective-permute-start | bytes 1622024 | tf_op jit(solution)/shard_map/ppermute | solution.py:265
  69.0 14.5 %collective-permute-start.8 = (bf16[80,1536]{1,0:T(8,128)(2,1)S(1)}, bf16[80,1536]{1,0:T(8,128)(2,1)S(1)}, u32[]{:S(2)}, u32[]{:S(2)}) collective-permute-start(bf16[80,1536]{1,0:T(8,128)(2,1)S(1)} %copy-done.15), channel_id=1, source_target_pairs={{0,16},{4,20},{8,24},{12,28},{16,0},{20,4},{24,8},{28,12},{1,17},{... | collective-permute-start | bytes 737288 | tf_op jit(solution)/shard_map/ppermute | solution.py:265
  83.6 8.1 %collective-permute-start.10 = (bf16[80,1536]{1,0:T(8,128)(2,1)S(1)}, bf16[80,1536]{1,0:T(8,128)(2,1)S(1)}, u32[]{:S(2)}, u32[]{:S(2)}) collective-permute-start(bf16[80,1536]{1,0:T(8,128)(2,1)S(1)} %collective-permute-done.8.refs_1_), channel_id=1, source_target_pairs={{0,1},{1,0},{2,3},{3,2},{4,5},{5,4},{6,7},{7,6},{8,9},{9,8},{10,11... | collective-permute-start | bytes 737288 | tf_op jit(solution)/shard_map/ppermute | solution.py:265
  83.6 3.6 %collective-permute-start.14 = (f32[1,1024]{1,0:T(1,128)S(1)}, f32[1,1024]{1,0:T(1,128)S(1)}, u32[]{:S(2)}, u32[]{:S(2)}) collective-permute-start(f32[1,1024]{1,0:T(1,128)S(1)} %add.28), channel_id=1, source_target_pairs={{0,8},{4,12},{8,0},{12,4},{16,24},{20,28},{24,16},{28,20},{1,9},{5... | collective-permute-start | bytes 12296 | tf_op jit(solution)/shard_map/ppermute | solution.py:265
  87.2 4.5 %collective-permute-start.15 = (f32[1,1024]{1,0:T(1,128)S(1)}, f32[1,1024]{1,0:T(1,128)S(1)}, u32[]{:S(2)}, u32[]{:S(2)}) collective-permute-start(f32[1,1024]{1,0:T(1,128)S(1)} %add.29), channel_id=1, source_target_pairs={{0,16},{4,20},{8,24},{12,28},{16,0},{20,4},{24,8},{28,12},{1,17},{... | collective-permute-start | bytes 12296 | tf_op jit(solution)/shard_map/ppermute | solution.py:265
  94.8 3.1 %copy-start.4 = (bf16[352,1536]{1,0:T(8,128)(2,1)}, bf16[352,1536]{1,0:T(8,128)(2,1)S(1)}, u32[]{:S(2)}) copy-start(bf16[352,1536]{1,0:T(8,128)(2,1)S(1)} %get-tuple-element.52.refs_7_.refs_3_) | copy-start | bytes 3244036
  97.8 3.5 %copy-start.6 = (bf16[352,1536]{1,0:T(8,128)(2,1)}, bf16[352,1536]{1,0:T(8,128)(2,1)S(1)}, u32[]{:S(2)}) copy-start(bf16[352,1536]{1,0:T(8,128)(2,1)S(1)} %get-tuple-element.53.refs_8_.refs_4_) | copy-start | bytes 3244036
  101.3 1.1 copy-start.9
  102.4 10.3 %collective-permute-start.16 = (bf16[2,128,768]{2,1,0:T(8,128)(2,1)}, bf16[2,128,768]{2,1,0:T(8,128)(2,1)}, u32[]{:S(2)}, u32[]{:S(2)}) collective-permute-start(bf16[2,128,768]{2,1,0:T(8,128)(2,1)} %get-tuple-element.56), channel_id=1, source_target_pairs={{0,4},{4,0},{8,12},{12,8},{16,20},{20,16},{24,28},{28,24},{1,5},{5... | collective-permute-start | bytes 1179656 | tf_op jit(solution)/shard_map/ppermute | solution.py:265
  103.9 11.3 %collective-permute-start.18 = (bf16[2,128,768]{2,1,0:T(8,128)(2,1)}, bf16[2,128,768]{2,1,0:T(8,128)(2,1)S(1)}, u32[]{:S(2)}, u32[]{:S(2)}) collective-permute-start(bf16[2,128,768]{2,1,0:T(8,128)(2,1)} %get-tuple-element.60), channel_id=1, source_target_pairs={{0,8},{4,12},{8,0},{12,4},{16,24},{20,28},{24,16},{28,20},{1,9},{5... | collective-permute-start | bytes 1179656 | tf_op jit(solution)/shard_map/ppermute | solution.py:265
  104.6 1.2 %copy-start.1 = (bf16[352,1536]{1,0:T(8,128)(2,1)S(1)}, bf16[352,1536]{1,0:T(8,128)(2,1)}, u32[]{:S(2)}) copy-start(bf16[352,1536]{1,0:T(8,128)(2,1)} %copy-done) | copy-start | bytes 3244036
  105.8 1.2 %copy-start.3 = (bf16[352,1536]{1,0:T(8,128)(2,1)S(1)}, bf16[352,1536]{1,0:T(8,128)(2,1)}, u32[]{:S(2)}) copy-start(bf16[352,1536]{1,0:T(8,128)(2,1)} %copy-done.2) | copy-start | bytes 3244036
  107.0 1.2 %copy-start.5 = (bf16[352,1536]{1,0:T(8,128)(2,1)S(1)}, bf16[352,1536]{1,0:T(8,128)(2,1)}, u32[]{:S(2)}) copy-start(bf16[352,1536]{1,0:T(8,128)(2,1)} %copy-done.4) | copy-start | bytes 3244036
  108.3 1.2 %copy-start.7 = (bf16[352,1536]{1,0:T(8,128)(2,1)S(1)}, bf16[352,1536]{1,0:T(8,128)(2,1)}, u32[]{:S(2)}) copy-start(bf16[352,1536]{1,0:T(8,128)(2,1)} %copy-done.6) | copy-start | bytes 3244036
  109.5 1.4 %copy-start.10 = (bf16[1408,512]{1,0:T(8,128)(2,1)S(1)}, bf16[1408,512]{1,0:T(8,128)(2,1)}, u32[]{:S(2)}) copy-start(bf16[1408,512]{1,0:T(8,128)(2,1)} %copy-done.9) | copy-start | bytes 4325380
  113.8 5.7 %collective-permute-start.17 = (bf16[1,128,768]{2,1,0:T(8,128)(2,1)S(1)}, bf16[1,128,768]{2,1,0:T(8,128)(2,1)S(1)}, u32[]{:S(2)}, u32[]{:S(2)}) collective-permute-start(bf16[1,128,768]{2,1,0:T(8,128)(2,1)S(1)} %get-tuple-element.58), channel_id=1, source_target_pairs={{0,8},{4,12},{8,0},{12,4},{16,24},{20,28},{24,16},{28,20},{1,9},{5... | collective-permute-start | bytes 589832 | tf_op jit(solution)/shard_map/ppermute | solution.py:265
  115.3 5.7 %collective-permute-start.19 = (bf16[1,128,768]{2,1,0:T(8,128)(2,1)S(1)}, bf16[1,128,768]{2,1,0:T(8,128)(2,1)S(1)}, u32[]{:S(2)}, u32[]{:S(2)}) collective-permute-start(bf16[1,128,768]{2,1,0:T(8,128)(2,1)S(1)} %get-tuple-element.62), channel_id=1, source_target_pairs={{0,4},{4,0},{8,12},{12,8},{16,20},{20,16},{24,28},{28,24},{1,5},{5... | collective-permute-start | bytes 589832 | tf_op jit(solution)/shard_map/ppermute | solution.py:265

commit v3 on v2

--- a/solution.py
+++ b/solution.py
@@ -42,7 +42,11 @@
     ends = [up(tok - (chips - 1 - j) * least) for j in range(chips)]
     wide = max(e - s for s, e in zip(starts, ends))
     starts = [min(s, tok - wide) for s in starts]
-    return starts, wide
+    starts = [min(s, tok - wide) for s in starts]
+    cuts = sorted(set(starts + [s + wide for s in starts] + [0, tok]))
+    pieces = list(zip(cuts[:-1], cuts[1:]))
+    parts = [[k for k, (lo, hi) in enumerate(pieces) if s <= lo and hi <= s + wide] for s in starts]
+    return starts, wide, pieces, parts
 
 
 def to_col(row):
@@ -84,7 +88,7 @@
 
 def sort_kernel(chips, ranges, *refs):
     points_ref, parents_ref, owner_ref, count_ref = refs[:4]
-    out_refs, (points, parents, owner, count, sems) = refs[4:-5], refs[-5:]
+    out_refs, (parents, table, points, owner, count, sems) = refs[4:-6], refs[-6:]
     copies = fetch(
         [(points_ref, points), (parents_ref, parents), (owner_ref, owner), (count_ref, count)], sems
     )
@@ -93,6 +97,7 @@
     for copy in copies[1:]:
         copy.wait()
     code_row = owner_codes(owner, count)
+    table[...] = code_row
     parent = parents[:, pl.ds(pl.multiple_of(me * tok, tok), tok)]
     code, key = code_and_key(parent, code_row, me // CORES, chips)
     key_row = to_row(key)
@@ -105,38 +110,40 @@
         out_ref[...] = ordered[lo:hi]
 
 
-def codes_kernel(chips, starts, tok, parents_ref, owner_ref, count_ref, out_ref, parents, owner, count, sems):
-    for copy in fetch([(parents_ref, parents), (owner_ref, owner), (count_ref, count)], sems):
-        copy.wait()
+def codes_kernel(chips, starts, tok, wide, parents, table, out_ref):
     me = lax.axis_index("own")
-    code_row = owner_codes(owner, count)
-    wide = out_ref.shape[1]
-    for rel in range(out_ref.shape[0]):
+    code_row = table[...]
+    total = out_ref.shape[1]
+    out = jnp.zeros((1, total), F32)
+    for rel in range(total // wide):
         parent = parents[:, pl.ds(pl.multiple_of((me ^ rel) * tok, tok), tok)]
         code, key = code_and_key(parent, code_row, (me ^ rel) // CORES, chips)
         place = jnp.sum(jnp.where(to_row(key) < key, 1.0, 0.0), axis=1, keepdims=True).astype(I32)
-        start = starts[chips - 1 - rel // CORES]
-        hit = place == iota((tok, wide), 1) + start
-        out_ref[rel : rel + 1, :] = jnp.sum(jnp.where(hit, code, 0.0), axis=0, keepdims=True)
-
-
-def cent_kernel(in_ref, out_ref):
+        inside = iota((tok, total), 1) - rel * wide
+        hit = (inside >= 0) & (inside < wide) & (place == inside + starts[chips - 1 - rel // CORES])
+        out = out + jnp.sum(jnp.where(hit, code, 0.0), axis=0, keepdims=True)
+    out_ref[...] = out
+
+
+def cent_kernel(in_ref, out_ref, base_ref):
     out_ref[...] = unit_rms(in_ref[...]).astype(BF16)
-
-
-def weights_kernel(rels, tile, skips, *refs):
+    share = base_ref.shape[0]
+    base_ref[...] = out_ref[pl.ds(pl.multiple_of(lax.axis_index("pts") * share, share), share), :]
+
+
+def weights_kernel(places, tile, *refs):
     row_refs, (codes_ref, cent_ref, w_ref, sum_ref, rows_ref, low_ref, high_ref) = refs[:-7], refs[-7:]
     me = lax.axis_index("own")
     slots, width = cent_ref.shape
-    wide = codes_ref.shape[1]
+    total = codes_ref.shape[1]
     at = 0
-    for row_ref, skip in zip(row_refs, skips):
-        size = row_ref.shape[0] - skip
-        rows_ref[at : at + size, :] = row_ref[skip:, :]
+    for row_ref, place in zip(row_refs, places):
+        size = row_ref.shape[0]
+        part = slice(at, at + size)
         at += size
-    for k, rel in enumerate(rels):
-        part = slice(k * wide, (k + 1) * wide)
-        code = to_col(codes_ref[rel : rel + 1, :]).astype(I32)
+        rows_ref[part, :] = row_ref[...]
+        hit = iota((size, total), 1) == iota((size, total), 0) + place
+        code = jnp.sum(jnp.where(hit, codes_ref[...], 0.0), axis=1, keepdims=True).astype(I32)
         first = (code % OWNER_SHIFT) // FIRST_SHIFT
         low = jnp.where(code // OWNER_SHIFT == me, first, slots)
         low_ref[part, :] = low
@@ -265,6 +272,10 @@
     return lax.ppermute(values, axis, [(i, i ^ bit) for i in range(lax.axis_size(axis))])
 
 
+def powers(end):
+    return [1 << k for k in range(end.bit_length() - 1)]
+
+
 def bit_orders(bits):
     orders = []
     for k in range(len(bits)):
@@ -282,77 +293,92 @@
     tok, width = points.shape
     slots = centroids.shape[1]
     share = slots // groups
-    starts, wide = windows(tok, owners)
+    starts, wide, pieces, parts = windows(tok, owners)
     parents = parent_of.T
     table = [owner_of.reshape(1, -1), child_count.reshape(1, -1)]
     half_bit = groups // 2
-    small = [pltpu.VMEM(a.shape, I32) for a in [parents, *table]]
-    own_start, outward = starts[-1], starts[max(chips - 2, 0)] + wide
-
-    ranges = [(0, outward), (outward, tok), (own_start, tok)]
-    head, tail, mine = call(
-        functools.partial(sort_kernel, chips, ranges), [((hi - lo, width), BF16) for lo, hi in ranges],
+
+    ranges = pieces + [(s, s + wide) for s in starts]
+    *ordered, parents, codes = call(
+        functools.partial(sort_kernel, chips, ranges),
+        [((hi - lo, width), BF16) for lo, hi in ranges] + [(parents.shape, I32), (table[0].shape, F32)],
         points, parents, *table,
-        scratch=[pltpu.VMEM((tok, width), BF16), *small, pltpu.SemaphoreType.DMA((4,))], where=pl.ANY, vmem=62,
-    )
-
-    def across(held, chip):
-        start = starts[chips - 1 - chip]
-        whole = start == 0 and start + wide == held.shape[0]
-        return swap(held if whole else held[start : start + wide], "own", chip * CORES)
-
-    def both(rows):
-        return [*rows, *[swap(r, "own", 1) for r in rows]]
-
-    def weigh(blocks, codes, chip, skip):
-        rows = wide * CORES
-        skips = [skip, 0] * CORES if skip else [0] * len(blocks)
+        scratch=[
+            pltpu.VMEM((tok, width), BF16), *[pltpu.VMEM(a.shape, I32) for a in table],
+            pltpu.SemaphoreType.DMA((4,)),
+        ],
+        where=pl.ANY, vmem=62,
+    )
+    held, whole = ordered[: len(pieces)], ordered[len(pieces) :]
+
+    def place(chip, core, lo):
+        return (chip * CORES + core) * wide + lo - starts[chips - 1 - chip]
+
+    def weigh(rows, places, codes):
+        count = sum(r.shape[0] for r in rows)
         return call(
-            functools.partial(weights_kernel, [chip * CORES, chip * CORES + 1], min(slots, 256), skips),
-            [((rows, slots), F32), ((1, slots), F32), ((rows, width), BF16)],
-            *blocks, codes, cent,
-            scratch=[pltpu.VMEM((rows, 1), I32), pltpu.VMEM((rows, 1), I32)],
+            functools.partial(weights_kernel, places, min(slots, 256)),
+            [((count, slots), F32), ((1, slots), F32), ((count, width), BF16)], *rows, codes, cent,
+            scratch=[pltpu.VMEM((count, 1), I32), pltpu.VMEM((count, 1), I32)],
         )
 
-    def all_sum(values):
-        seen = [values]
-        bit = 1
-        while bit < groups:
-            values = values + swap(values, "pts", bit)
-            seen.append(values)
-            bit *= 2
-        return values, seen
-
-    near = [both([mine])] + [both([across(head, chip)]) for chip in range(1, chips)]
-    far_head, far_tail = swap(head, "pts", half_bit), swap(tail, "pts", half_bit)
+    near = [whole[-1]] + [swap(whole[chips - 1 - chip], "own", chip * CORES) for chip in range(1, chips)]
+    far_held = [swap(held[0], "pts", half_bit)]
+    near = [(r, swap(r, "own", 1)) for r in near]
     codes = call(
-        functools.partial(codes_kernel, chips, starts, tok), [((owners, wide), F32)], parents, *table,
-        scratch=[*small, pltpu.SemaphoreType.DMA((3,))], where=pl.ANY,
-    )
-    far_codes = swap(codes, "pts", half_bit)
-    cent = call(cent_kernel, [((slots, width), BF16)], centroids[0])
-
-    near_got = [
-        weigh(near[chip], codes if chip == 0 else after(codes, far_codes), chip, 0) for chip in range(chips)
-    ]
-    near_w, near_s, near_x = zip(*near_got)
-    column, seen = all_sum(sum(near_s))
-    balance, then = all_sum(
-        call(functools.partial(balance_kernel, chips), [((1, slots), F32)], *near_w, column)
-    )
-    far_cross = [across(after(far_head, seen[0]), chip) for chip in range(1, chips)]
-    far = [both([after(far_head, column), after(far_tail, column)])] + [both([after(r, then[1])]) for r in far_cross]
-    far_got = [
-        weigh(far[chip], after(far_codes, then[1] if chip == 0 else then[-2]), chip, own_start if chip == 0 else 0)
+        functools.partial(codes_kernel, chips, starts, tok, wide), [((1, owners * wide), F32)], parents, codes,
+        vmem=4,
+    )
+    cent, base = call(cent_kernel, [((slots, width), BF16), ((share, width), BF16)], centroids[0])
+
+    near_w, near_s, near_x = zip(*[
+        weigh(
+            near[chip], [place(chip, c, starts[chips - 1 - chip]) for c in range(CORES)],
+            after(codes, far_held[0]) if chip else codes,
+        )
         for chip in range(chips)
-    ]
-    far_w, _, far_x = zip(*far_got)
-
-    bits = []
-    bit = 1
-    while bit < half_bit:
-        bits.append(bit)
-        bit *= 2
+    ])
+
+    def forward(k, gate):
+        for chip in range(1, chips):
+            if k in parts[chips - 1 - chip]:
+                far_cross[chip, k] = swap(after(far_held[k], gate), "own", chip * CORES)
+
+    def pair(chip, k, gate):
+        rows = after(far_cross[chip, k] if chip else far_held[k], gate)
+        for core, r in enumerate((rows, swap(rows, "own", 1))):
+            far[int(k == parts[chips - 1 - chip][-1])].append((r, place(chip, core, pieces[k][0])))
+
+    far, far_cross = [[], []], {}
+    partial = sum(near_s)
+    came = swap(jnp.concatenate([partial, codes], axis=1), "pts", half_bit)
+    column, far_codes = partial + came[:, :slots], came[:, slots:]
+    forward(0, partial)
+    sums = [column]
+    for bit in powers(half_bit):
+        column = column + swap(column, "pts", bit)
+        sums.append(column)
+    far_held.append(swap(after(held[1], sums[0]), "pts", half_bit))
+    for piece in held[2:]:
+        far_held.append(swap(after(piece, sums[1]), "pts", half_bit))
+    balance = call(functools.partial(balance_kernel, chips), [((1, slots), F32)], *near_w, column)
+    balance = after(balance, [far_cross[chip, 0] for chip in range(1, chips) if (chip, 0) in far_cross])
+    steps = [balance]
+    for bit in powers(groups):
+        balance = balance + swap(balance, "pts", bit)
+        steps.append(balance)
+    for k in range(1, len(pieces)):
+        forward(k, steps[1])
+    for chip in range(chips):
+        mine = parts[chips - 1 - chip]
+        for k in mine:
+            pair(chip, k, steps[-2] if k == mine[-1] else steps[0])
+    far_w, _, far_x = zip(*[
+        weigh([r for r, _ in rows], [p for _, p in rows], after(far_codes, gate))
+        for rows, gate in zip(far, (steps[1], steps[-2]))
+    ])
+
+    bits = powers(half_bit)
     orders = bit_orders(bits)
     cols = width // len(orders)
     m = half_bit // 2
@@ -360,7 +386,7 @@
     total_rows = sum(r.shape[0] for r in rows)
     part = pltpu.VMEM((max(share, LANES), cols), F32)
     got = call(
-        functools.partial(send_kernel, [b[m:] for _, b in orders], half_bit, 2 * chips),
+        functools.partial(send_kernel, [b[m:] for _, b in orders], half_bit, len(near_w) + len(far_w)),
         [((m, share, cols), BF16)] * len(orders) + [((total_rows, slots // 2), BF16)],
         *near_w, *far_w, balance, *rows, scratch=[part],
     )
@@ -383,8 +409,6 @@
                 merge_kernel, [((n, share, cols), F32), ((n, share, cols), BF16)], keeps[r], c, vmem=8
             )
             sends.append(send)
-    own = lax.axis_index("pts") * share
-    base = lax.dynamic_slice_in_dim(cent, own, share, 0)
     flat = [t.reshape(share, cols) for pair in zip(keeps, last) for t in pair]
     out = call(
         functools.partial(final_kernel, len(orders), 2), [((share, width), BF16)], *flat, base, vmem=8

time: 123 us -> 104 us (0.85)
  local copies, waits for them, and re-layouts: 11.4 us -> 1.91 us
  waiting for transfers between devices: 64.4 us -> 58 us
  Pallas kernels: 24.5 us -> 23 us
    unnamed x32 -> x12, local copies, waits for them, and re-layouts: 11.3 us -> 1.91 us
    ppermute x20 -> x22, waiting for transfers between devices: 64.4 us -> 58 us  [swap(): lax.ppermute(values, axis, [(i, i ^ bit) for i in range(lax.axis_size(axi...]
    pallas_call x13, Pallas kernels: 24.5 us -> 23 us  [call(): pl.pallas_call(kernel, out_shape=shapes, in_specs=[pl.BlockSpec(memory_sp...]
    ppermute x20 -> x22, starting transfers between devices: 21.5 us -> 20.8 us  [swap(): lax.ppermute(values, axis, [(i, i ^ bit) for i in range(lax.axis_size(axi...]
  transfers between devices with their start and end apart: 20 -> 22, of which waited for: 11 -> 14; matrix products, arithmetic and copies ran while one was open for 0% -> 0% of each run, Pallas kernels for 11% -> 10%
where the time goes in v3:
time: 104 us
  waiting for transfers between devices  58 us (56%)
  Pallas kernels  23 us (22%)
  starting transfers between devices  20.8 us (20%)
  local copies, waits for them, and re-layouts  1.91 us (2%)
    ppermute x22, waiting for transfers between devices, swap(): lax.ppermute(values, axis, [(i, i ^ bit) for i in range(lax.axis_size(axi...  58 us
    pallas_call x13, Pallas kernels, call(): pl.pallas_call(kernel, out_shape=shapes, in_specs=[pl.BlockSpec(memory_sp...  23 us
    ppermute x22, starting transfers between devices, swap(): lax.ppermute(values, axis, [(i, i ^ bit) for i in range(lax.axis_size(axi...  20.8 us
  transfers between devices with their start and end apart: 22, of which 14 were waited for; matrix products, arithmetic and copies ran while one was open for 0% of the time, Pallas kernels for 10%

profile of v3, /device:TPU:0, one launch (start us, length us, event | category | flops | bytes accessed | tf_op | source)
XLA Modules:
  0.0 104.0 jit_solution(7684458133330369337)
XLA Ops:
  0.0 3.2 %shard_map.55 = (bf16[80,1536]{1,0:T(8,128)(2,1)}, bf16[96,1536]{1,0:T(8,128)(2,1)}, bf16[80,1536]{1,0:T(8,128)(2,1)}, bf16[176,1536]{1,0:T(8,128)(2,1)}, bf16[1...) custom-call(bf16[256,1536]{1,0:T(8,128)(2,1)} %refs_0_.1, s32[1,1024]{1,0:T(1,128)} %bitcast.14, ...), custom_call_target="tpu_custom_call" | custom-call | tf_op jit(solution)/shard_map/pallas_call | solution.py:255
  3.2 3.0 %collective-permute-start.1 = (bf16[176,1536]{1,0:T(8,128)(2,1)}, bf16[176,1536]{1,0:T(8,128)(2,1)S(1)}, u32[]{:S(2)}, u32[]{:S(2)}) collective-permute-start(bf16[176,1536]{1,0:T(8,128)(2,1)} %get-tuple-element.50), channel_id=1, source_target_pairs={{0,2},{1,3},{2,0},{3,1},{4,6},{5,7},{6,4},{7,5},{8,10},{9,11},{10,... | collective-permute-start | bytes 1622024 | tf_op jit(solution)/shard_map/ppermute | solution.py:272
  6.2 12.5 %collective-permute-done.1.refs_0_ = bf16[176,1536]{1,0:T(8,128)(2,1)S(1)} collective-permute-done((bf16[176,1536]{1,0:T(8,128)(2,1)}, bf16[176,1536]{1,0:T(8,128)(2,1)S(1)}, u32[]{:S(2)}, u32[]{:S(2)}) %collective-permute-start.1) | collective-permute-done | bytes 540704 | tf_op jit(solution)/shard_map/ppermute | solution.py:272
  18.7 2.8 %collective-permute-start.3 = (bf16[80,1536]{1,0:T(8,128)(2,1)}, bf16[80,1536]{1,0:T(8,128)(2,1)S(1)}, u32[]{:S(2)}, u32[]{:S(2)}) collective-permute-start(bf16[80,1536]{1,0:T(8,128)(2,1)} %get-tuple-element.51), channel_id=1, source_target_pairs={{0,16},{4,20},{8,24},{12,28},{16,0},{20,4},{24,8},{28,12},{1,17},{... | collective-permute-start | bytes 737288 | tf_op jit(solution)/shard_map/ppermute | solution.py:272
  21.6 1.9 %copy-done = bf16[1,1024,1536]{2,1,0:T(8,128)(2,1)S(1)} copy-done((bf16[1,1024,1536]{2,1,0:T(8,128)(2,1)S(1)}, bf16[1,1024,1536]{2,1,0:T(8,128)(2,1)}, u32[]{:S(2)}) %copy-start) | copy-done | bytes 3145752
  23.5 1.0 shard_map.57
  24.5 1.4 %shard_map.56.refs_2_ = f32[1,704]{1,0:T(1,128)S(1)} custom-call(s32[1,1024]{1,0:T(1,128)S(1)} %copy-done.2, f32[1,64]{1,0:T(1,128)S(1)} %copy-done.3), custom_call_target="tpu_custom_call" | custom-call | tf_op jit(solution)/shard_map/pallas_call | solution.py:255
  25.9 7.8 %collective-permute-done.3 = bf16[80,1536]{1,0:T(8,128)(2,1)S(1)} collective-permute-done((bf16[80,1536]{1,0:T(8,128)(2,1)}, bf16[80,1536]{1,0:T(8,128)(2,1)S(1)}, u32[]{:S(2)}, u32[]{:S(2)}) %collective-permute-start.3) | collective-permute-done | bytes 245792 | tf_op jit(solution)/shard_map/ppermute | solution.py:272
  33.7 2.6 %shard_map.58 = (f32[352,1024]{1,0:T(8,128)S(1)}, f32[1,1024]{1,0:T(1,128)S(1)}, bf16[352,1536]{1,0:T(8,128)(2,1)S(1)}) custom-call(bf16[176,1536]{1,0:T(8,128)(2,1)S(1)} %copy-done.1, bf16[176,1536]{1,0:T(8,128)(2,1)S(1)} %collective-permute-done.refs_1_, f32[1,704]{1,0:T(1,128)S(1)} %shard_map.56.refs_2_, ...), custom_call_target="tpu_custom_call" | custom-call | tf_op jit(solution)/shard_map/pallas_call | solution.py:255
  36.3 0.0 copy-start.4
  36.3 2.4 %shard_map.59 = (f32[352,1024]{1,0:T(8,128)S(1)}, f32[1,1024]{1,0:T(1,128)S(1)}, bf16[352,1536]{1,0:T(8,128)(2,1)S(1)}) custom-call(bf16[176,1536]{1,0:T(8,128)(2,1)S(1)} %collective-permute-done.1.refs_0_, bf16[176,1536]{1,0:T(8,128)(2,1)S(1)} %collective-permute-done.2.refs_1_, f32[1,704]{1,0:T(1,128)S(1)} %shard_map.56.refs_2_, ...), custom_call_target="tpu_custom_call" | custom-call | tf_op jit(solution)/shard_map/pallas_call | solution.py:255
  38.8 0.1 collective-permute-start.4
  38.9 4.6 %collective-permute-done.4 = f32[1,1728]{1,0:T(1,128)S(1)} collective-permute-done((f32[1,1728]{1,0:T(1,128)S(1)}, f32[1,1728]{1,0:T(1,128)S(1)}, u32[]{:S(2)}, u32[]{:S(2)}) %collective-permute-start.4) | collective-permute-done | bytes 6944 | tf_op jit(solution)/shard_map/ppermute | solution.py:272
  43.5 0.1 collective-permute-start.5
  43.6 1.5 %collective-permute-start.8 = (bf16[80,1536]{1,0:T(8,128)(2,1)S(1)}, bf16[80,1536]{1,0:T(8,128)(2,1)S(1)}, u32[]{:S(2)}, u32[]{:S(2)}) collective-permute-start(bf16[80,1536]{1,0:T(8,128)(2,1)S(1)} %collective-permute-done.3), channel_id=1, source_target_pairs={{0,2},{1,3},{2,0},{3,1},{4,6},{5,7},{6,4},{7,5},{8,10},{9,11},{10,... | collective-permute-start | bytes 737288 | tf_op jit(solution)/shard_map/ppermute | solution.py:272
  45.1 1.5 %collective-permute-start.6 = (f32[1,1024]{1,0:T(1,128)S(1)}, f32[1,1024]{1,0:T(1,128)S(1)}, u32[]{:S(2)}, u32[]{:S(2)}) collective-permute-start(f32[1,1024]{1,0:T(1,128)S(1)} %slice_add_fusion), channel_id=1, source_target_pairs={{0,4},{4,0},{8,12},{12,8},{16,20},{20,16},{24,28},{28,24},{1,5},{5... | collective-permute-start | bytes 12296 | tf_op jit(solution)/shard_map/ppermute | solution.py:272
  46.7 2.1 %collective-permute-done.6 = f32[1,1024]{1,0:T(1,128)S(1)} collective-permute-done((f32[1,1024]{1,0:T(1,128)S(1)}, f32[1,1024]{1,0:T(1,128)S(1)}, u32[]{:S(2)}, u32[]{:S(2)}) %collective-permute-start.6) | collective-permute-done | bytes 4128 | tf_op jit(solution)/shard_map/ppermute | solution.py:272
  48.7 4.7 %collective-permute-start.7 = (f32[1,1024]{1,0:T(1,128)S(1)}, f32[1,1024]{1,0:T(1,128)S(1)}, u32[]{:S(2)}, u32[]{:S(2)}) collective-permute-start(f32[1,1024]{1,0:T(1,128)S(1)} %add.23), channel_id=1, source_target_pairs={{0,8},{4,12},{8,0},{12,4},{16,24},{20,28},{24,16},{28,20},{1,9},{5... | collective-permute-start | bytes 12296 | tf_op jit(solution)/shard_map/ppermute | solution.py:272
  53.4 2.0 %collective-permute-done.7 = f32[1,1024]{1,0:T(1,128)S(1)} collective-permute-done((f32[1,1024]{1,0:T(1,128)S(1)}, f32[1,1024]{1,0:T(1,128)S(1)}, u32[]{:S(2)}, u32[]{:S(2)}) %collective-permute-start.7) | collective-permute-done | bytes 4128 | tf_op jit(solution)/shard_map/ppermute | solution.py:272
  55.4 0.6 shard_map.60
  56.0 0.0 collective-permute-done.8.refs_2_
  56.0 1.6 %collective-permute-start.11 = (f32[1,1024]{1,0:T(1,128)S(1)}, f32[1,1024]{1,0:T(1,128)S(1)}, u32[]{:S(2)}, u32[]{:S(2)}) collective-permute-start(f32[1,1024]{1,0:T(1,128)S(1)} %shard_map.60), channel_id=1, source_target_pairs={{0,4},{4,0},{8,12},{12,8},{16,20},{20,16},{24,28},{28,24},{1,5},{5... | collective-permute-start | bytes 12296 | tf_op jit(solution)/shard_map/ppermute | solution.py:272
  57.6 2.1 %collective-permute-done.11 = f32[1,1024]{1,0:T(1,128)S(1)} collective-permute-done((f32[1,1024]{1,0:T(1,128)S(1)}, f32[1,1024]{1,0:T(1,128)S(1)}, u32[]{:S(2)}, u32[]{:S(2)}) %collective-permute-start.11) | collective-permute-done | bytes 4128 | tf_op jit(solution)/shard_map/ppermute | solution.py:272
  59.7 0.0 collective-permute-done.5.refs_0_
  59.7 0.6 collective-permute-start.15
  60.3 0.0 collective-permute-start.12
  60.3 2.1 %collective-permute-start.13 = (f32[1,1024]{1,0:T(1,128)S(1)}, f32[1,1024]{1,0:T(1,128)S(1)}, u32[]{:S(2)}, u32[]{:S(2)}) collective-permute-start(f32[1,1024]{1,0:T(1,128)S(1)} %add.25), channel_id=1, source_target_pairs={{0,8},{4,12},{8,0},{12,4},{16,24},{20,28},{24,16},{28,20},{1,9},{5... | collective-permute-start | bytes 12296 | tf_op jit(solution)/shard_map/ppermute | solution.py:272
  62.4 1.7 %collective-permute-done.13 = f32[1,1024]{1,0:T(1,128)S(1)} collective-permute-done((f32[1,1024]{1,0:T(1,128)S(1)}, f32[1,1024]{1,0:T(1,128)S(1)}, u32[]{:S(2)}, u32[]{:S(2)}) %collective-permute-start.13) | collective-permute-done | bytes 4128 | tf_op jit(solution)/shard_map/ppermute | solution.py:272
  64.1 2.4 %collective-permute-done.15.refs_2_ = bf16[96,1536]{1,0:T(8,128)(2,1)S(1)} collective-permute-done((bf16[96,1536]{1,0:T(8,128)(2,1)S(1)}, bf16[96,1536]{1,0:T(8,128)(2,1)S(1)}, u32[]{:S(2)}, u32[]{:S(2)}) %collective-permute-start.15) | collective-permute-done | bytes 294944 | tf_op jit(solution)/shard_map/ppermute | solution.py:272
  66.5 0.0 collective-permute-start.16
  66.5 0.5 collective-permute-start.10
  67.0 5.2 %collective-permute-done.12.refs_0_ = bf16[80,1536]{1,0:T(8,128)(2,1)S(1)} collective-permute-done((bf16[80,1536]{1,0:T(8,128)(2,1)S(1)}, bf16[80,1536]{1,0:T(8,128)(2,1)S(1)}, u32[]{:S(2)}, u32[]{:S(2)}) %collective-permute-start.12) | collective-permute-done | bytes 245792 | tf_op jit(solution)/shard_map/ppermute | solution.py:272
  72.2 4.5 %collective-permute-done.17 = f32[1,1024]{1,0:T(1,128)S(1)} collective-permute-done((f32[1,1024]{1,0:T(1,128)S(1)}, f32[1,1024]{1,0:T(1,128)S(1)}, u32[]{:S(2)}, u32[]{:S(2)}) %collective-permute-start.17) | collective-permute-done | bytes 4128 | tf_op jit(solution)/shard_map/ppermute | solution.py:272
  76.7 3.0 %shard_map.61 = (f32[352,1024]{1,0:T(8,128)S(1)}, f32[1,1024]{1,0:T(1,128)}, bf16[352,1536]{1,0:T(8,128)(2,1)S(1)}) custom-call(bf16[96,1536]{1,0:T(8,128)(2,1)S(1)} %collective-permute-done.5.refs_0_, bf16[96,1536]{1,0:T(8,128)(2,1)S(1)} %collective-permute-done.9.refs_1_, bf16[80,1536]{1,0:T(8,128)(2,1)S(1)} %collective-permute-done.8.refs_2_, ...), custom_call_target="tpu_custom_call" | custom-call | tf_op jit(solution)/shard_map/pallas_call | solution.py:255
  79.8 0.0 collective-permute-done.14.refs_1_
  79.8 3.0 %shard_map.62 = (f32[352,1024]{1,0:T(8,128)S(1)}, f32[1,1024]{1,0:T(1,128)}, bf16[352,1536]{1,0:T(8,128)(2,1)S(1)}) custom-call(bf16[80,1536]{1,0:T(8,128)(2,1)S(1)} %collective-permute-done.12.refs_0_, bf16[80,1536]{1,0:T(8,128)(2,1)S(1)} %collective-permute-done.14.refs_1_, bf16[96,1536]{1,0:T(8,128)(2,1)S(1)} %collective-permute-done.15.refs_2_, ...), custom_call_target="tpu_custom_call" | custom-call | tf_op jit(solution)/shard_map/pallas_call | solution.py:255
  82.8 2.7 %shard_map.63 = (bf16[2,128,768]{2,1,0:T(8,128)(2,1)S(1)}, bf16[2,128,768]{2,1,0:T(8,128)(2,1)S(1)}, bf16[1408,512]{1,0:T(8,128)(2,1)S(1)}) custom-call(f32[352,1024]{1,0:T(8,128)S(1)} %get-tuple-element.49.refs_0_, f32[352,1024]{1,0:T(8,128)S(1)} %get-tuple-element.53.refs_1_, f32[352,1024]{1,0:T(8,128)S(1)} %get-tuple-element.63.refs_2_, ...), custom_call_target="tpu_custom_call" | custom-call | tf_op jit(solution)/shard_map/pallas_call | solution.py:255
  85.5 1.6 %collective-permute-start.18 = (bf16[2,128,768]{2,1,0:T(8,128)(2,1)S(1)}, bf16[2,128,768]{2,1,0:T(8,128)(2,1)S(1)}, u32[]{:S(2)}, u32[]{:S(2)}) collective-permute-start(bf16[2,128,768]{2,1,0:T(8,128)(2,1)S(1)} %get-tuple-element.77), channel_id=1, source_target_pairs={{0,4},{4,0},{8,12},{12,8},{16,20},{20,16},{24,28},{28,24},{1,5},{5... | collective-permute-start | bytes 1179656 | tf_op jit(solution)/shard_map/ppermute | solution.py:272
  87.1 1.9 %shard_map.64 = (f32[2,128,768]{2,1,0:T(8,128)S(1)}, f32[2,128,768]{2,1,0:T(8,128)S(1)}) custom-call(bf16[1408,512]{1,0:T(8,128)(2,1)S(1)} %get-tuple-element.75.refs_0_, bf16[352,1536]{1,0:T(8,128)(2,1)S(1)} %get-tuple-element.71.refs_5_.refs_1_, bf16[352,1536]{1,0:T(8,128)(2,1)S(1)} %get-tuple-element.72.refs_6_.refs_2_, ...), custom_call_target="tpu_custom_call" | custom-call | tf_op jit(solution)/shard_map/pallas_call | solution.py:255
  88.9 7.0 %collective-permute-done.18.came_ref = bf16[2,128,768]{2,1,0:T(8,128)(2,1)S(1)} collective-permute-done((bf16[2,128,768]{2,1,0:T(8,128)(2,1)S(1)}, bf16[2,128,768]{2,1,0:T(8,128)(2,1)S(1)}, u32[]{:S(2)}, u32[]{:S(2)}) %collective-permute-start.18) | collective-permute-done | bytes 393248 | tf_op jit(solution)/shard_map/ppermute | solution.py:272
  96.0 0.1 shard_map.65
  96.0 0.1 collective-permute-start.19
  96.1 1.1 %collective-permute-done.20.came_ref = bf16[2,128,768]{2,1,0:T(8,128)(2,1)S(1)} collective-permute-done((bf16[2,128,768]{2,1,0:T(8,128)(2,1)S(1)}, bf16[2,128,768]{2,1,0:T(8,128)(2,1)S(1)}, u32[]{:S(2)}, u32[]{:S(2)}) %collective-permute-start.20) | collective-permute-done | bytes 393248 | tf_op jit(solution)/shard_map/ppermute | solution.py:272
  97.2 0.1 shard_map.66
  97.3 0.6 collective-permute-start.21
  97.8 3.9 %collective-permute-done.19 = bf16[1,128,768]{2,1,0:T(8,128)(2,1)S(1)} collective-permute-done((bf16[1,128,768]{2,1,0:T(8,128)(2,1)S(1)}, bf16[1,128,768]{2,1,0:T(8,128)(2,1)S(1)}, u32[]{:S(2)}, u32[]{:S(2)}) %collective-permute-start.19) | collective-permute-done | bytes 196640 | tf_op jit(solution)/shard_map/ppermute | solution.py:272
  101.8 1.2 %collective-permute-done.21 = bf16[1,128,768]{2,1,0:T(8,128)(2,1)S(1)} collective-permute-done((bf16[1,128,768]{2,1,0:T(8,128)(2,1)S(1)}, bf16[1,128,768]{2,1,0:T(8,128)(2,1)S(1)}, u32[]{:S(2)}, u32[]{:S(2)}) %collective-permute-start.21) | collective-permute-done | bytes 196640 | tf_op jit(solution)/shard_map/ppermute | solution.py:272
  103.0 1.0 shard_map.67
  (30 shorter events, 0.1 us)
Async XLA Ops:
  3.2 15.5 %collective-permute-start.1 = (bf16[176,1536]{1,0:T(8,128)(2,1)}, bf16[176,1536]{1,0:T(8,128)(2,1)S(1)}, u32[]{:S(2)}, u32[]{:S(2)}) collective-permute-start(bf16[176,1536]{1,0:T(8,128)(2,1)} %get-tuple-element.50), channel_id=1, source_target_pairs={{0,2},{1,3},{2,0},{3,1},{4,6},{5,7},{6,4},{7,5},{8,10},{9,11},{10,... | collective-permute-start | bytes 1622024 | tf_op jit(solution)/shard_map/ppermute | solution.py:272
  6.2 27.4 %collective-permute-start = (bf16[176,1536]{1,0:T(8,128)(2,1)}, bf16[176,1536]{1,0:T(8,128)(2,1)S(1)}, u32[]{:S(2)}, u32[]{:S(2)}) collective-permute-start(bf16[176,1536]{1,0:T(8,128)(2,1)} %get-tuple-element.45.refs_0_), channel_id=1, source_target_pairs={{0,1},{1,0},{2,3},{3,2},{4,5},{5,4},{6,7},{7,6},{8,9},{9,8},{10,11... | collective-permute-start | bytes 1622024 | tf_op jit(solution)/shard_map/ppermute | solution.py:272
  18.7 17.6 %collective-permute-start.2 = (bf16[176,1536]{1,0:T(8,128)(2,1)S(1)}, bf16[176,1536]{1,0:T(8,128)(2,1)S(1)}, u32[]{:S(2)}, u32[]{:S(2)}) collective-permute-start(bf16[176,1536]{1,0:T(8,128)(2,1)S(1)} %collective-permute-done.1.refs_0_), channel_id=1, source_target_pairs={{0,1},{1,0},{2,3},{3,2},{4,5},{5,4},{6,7},{7,6},{8,9},{9,8},{10,11... | collective-permute-start | bytes 1622024 | tf_op jit(solution)/shard_map/ppermute | solution.py:272
  18.7 14.9 %collective-permute-start.3 = (bf16[80,1536]{1,0:T(8,128)(2,1)}, bf16[80,1536]{1,0:T(8,128)(2,1)S(1)}, u32[]{:S(2)}, u32[]{:S(2)}) collective-permute-start(bf16[80,1536]{1,0:T(8,128)(2,1)} %get-tuple-element.51), channel_id=1, source_target_pairs={{0,16},{4,20},{8,24},{12,28},{16,0},{20,4},{24,8},{28,12},{1,17},{... | collective-permute-start | bytes 737288 | tf_op jit(solution)/shard_map/ppermute | solution.py:272
  21.6 1.9 %copy-start = (bf16[1,1024,1536]{2,1,0:T(8,128)(2,1)S(1)}, bf16[1,1024,1536]{2,1,0:T(8,128)(2,1)}, u32[]{:S(2)}) copy-start(bf16[1,1024,1536]{2,1,0:T(8,128)(2,1)} %param.9) | copy-start | bytes 9437188
  23.5 1.0 copy-start.2
  23.5 1.0 copy-start.3
  23.5 10.2 %copy-start.1 = (bf16[176,1536]{1,0:T(8,128)(2,1)S(1)}, bf16[176,1536]{1,0:T(8,128)(2,1)}, u32[]{:S(2)}) copy-start(bf16[176,1536]{1,0:T(8,128)(2,1)} %get-tuple-element.45.refs_0_) | copy-start | bytes 1622020
  36.3 7.2 %copy-start.4 = (bf16[96,1536]{1,0:T(8,128)(2,1)S(1)}, bf16[96,1536]{1,0:T(8,128)(2,1)}, u32[]{:S(2)}) copy-start(bf16[96,1536]{1,0:T(8,128)(2,1)} %get-tuple-element.57) | copy-start | bytes 884740
  38.8 4.7 %collective-permute-start.4 = (f32[1,1728]{1,0:T(1,128)S(1)}, f32[1,1728]{1,0:T(1,128)S(1)}, u32[]{:S(2)}, u32[]{:S(2)}) collective-permute-start(f32[1,1728]{1,0:T(1,128)S(1)} %pad_maximum_fusion), channel_id=1, source_target_pairs={{0,16},{4,20},{8,24},{12,28},{16,0},{20,4},{24,8},{28,12},{1,17},{... | collective-permute-start | bytes 20744 | tf_op jit(solution)/shard_map/ppermute | solution.py:272
  43.5 16.2 %collective-permute-start.5 = (bf16[96,1536]{1,0:T(8,128)(2,1)S(1)}, bf16[96,1536]{1,0:T(8,128)(2,1)S(1)}, u32[]{:S(2)}, u32[]{:S(2)}) collective-permute-start(bf16[96,1536]{1,0:T(8,128)(2,1)S(1)} %copy-done.4), channel_id=1, source_target_pairs={{0,16},{4,20},{8,24},{12,28},{16,0},{20,4},{24,8},{28,12},{1,17},{... | collective-permute-start | bytes 884744 | tf_op jit(solution)/shard_map/ppermute | solution.py:272
  43.6 12.4 %collective-permute-start.8 = (bf16[80,1536]{1,0:T(8,128)(2,1)S(1)}, bf16[80,1536]{1,0:T(8,128)(2,1)S(1)}, u32[]{:S(2)}, u32[]{:S(2)}) collective-permute-start(bf16[80,1536]{1,0:T(8,128)(2,1)S(1)} %collective-permute-done.3), channel_id=1, source_target_pairs={{0,2},{1,3},{2,0},{3,1},{4,6},{5,7},{6,4},{7,5},{8,10},{9,11},{10,... | collective-permute-start | bytes 737288 | tf_op jit(solution)/shard_map/ppermute | solution.py:272
  45.1 3.6 %collective-permute-start.6 = (f32[1,1024]{1,0:T(1,128)S(1)}, f32[1,1024]{1,0:T(1,128)S(1)}, u32[]{:S(2)}, u32[]{:S(2)}) collective-permute-start(f32[1,1024]{1,0:T(1,128)S(1)} %slice_add_fusion), channel_id=1, source_target_pairs={{0,4},{4,0},{8,12},{12,8},{16,20},{20,16},{24,28},{28,24},{1,5},{5... | collective-permute-start | bytes 12296 | tf_op jit(solution)/shard_map/ppermute | solution.py:272
  48.7 6.7 %collective-permute-start.7 = (f32[1,1024]{1,0:T(1,128)S(1)}, f32[1,1024]{1,0:T(1,128)S(1)}, u32[]{:S(2)}, u32[]{:S(2)}) collective-permute-start(f32[1,1024]{1,0:T(1,128)S(1)} %add.23), channel_id=1, source_target_pairs={{0,8},{4,12},{8,0},{12,4},{16,24},{20,28},{24,16},{28,20},{1,9},{5... | collective-permute-start | bytes 12296 | tf_op jit(solution)/shard_map/ppermute | solution.py:272
  55.4 4.9 %copy-start.5 = (bf16[80,1536]{1,0:T(8,128)(2,1)S(1)}, bf16[80,1536]{1,0:T(8,128)(2,1)}, u32[]{:S(2)}) copy-start(bf16[80,1536]{1,0:T(8,128)(2,1)} %get-tuple-element.65) | copy-start | bytes 737284
  56.0 3.7 %collective-permute-start.11 = (f32[1,1024]{1,0:T(1,128)S(1)}, f32[1,1024]{1,0:T(1,128)S(1)}, u32[]{:S(2)}, u32[]{:S(2)}) collective-permute-start(f32[1,1024]{1,0:T(1,128)S(1)} %shard_map.60), channel_id=1, source_target_pairs={{0,4},{4,0},{8,12},{12,8},{16,20},{20,16},{24,28},{28,24},{1,5},{5... | collective-permute-start | bytes 12296 | tf_op jit(solution)/shard_map/ppermute | solution.py:272
  59.7 6.8 %collective-permute-start.15 = (bf16[96,1536]{1,0:T(8,128)(2,1)S(1)}, bf16[96,1536]{1,0:T(8,128)(2,1)S(1)}, u32[]{:S(2)}, u32[]{:S(2)}) collective-permute-start(bf16[96,1536]{1,0:T(8,128)(2,1)S(1)} %collective-permute-done.5.refs_0_), channel_id=1, source_target_pairs={{0,2},{1,3},{2,0},{3,1},{4,6},{5,7},{6,4},{7,5},{8,10},{9,11},{10,... | collective-permute-start | bytes 884744 | tf_op jit(solution)/shard_map/ppermute | solution.py:272
  60.3 11.9 %collective-permute-start.12 = (bf16[80,1536]{1,0:T(8,128)(2,1)S(1)}, bf16[80,1536]{1,0:T(8,128)(2,1)S(1)}, u32[]{:S(2)}, u32[]{:S(2)}) collective-permute-start(bf16[80,1536]{1,0:T(8,128)(2,1)S(1)} %copy-done.5), channel_id=1, source_target_pairs={{0,16},{4,20},{8,24},{12,28},{16,0},{20,4},{24,8},{28,12},{1,17},{... | collective-permute-start | bytes 737288 | tf_op jit(solution)/shard_map/ppermute | solution.py:272
  60.3 3.8 %collective-permute-start.13 = (f32[1,1024]{1,0:T(1,128)S(1)}, f32[1,1024]{1,0:T(1,128)S(1)}, u32[]{:S(2)}, u32[]{:S(2)}) collective-permute-start(f32[1,1024]{1,0:T(1,128)S(1)} %add.25), channel_id=1, source_target_pairs={{0,8},{4,12},{8,0},{12,4},{16,24},{20,28},{24,16},{28,20},{1,9},{5... | collective-permute-start | bytes 12296 | tf_op jit(solution)/shard_map/ppermute | solution.py:272
  64.1 12.7 %collective-permute-start.9 = (bf16[96,1536]{1,0:T(8,128)(2,1)S(1)}, bf16[96,1536]{1,0:T(8,128)(2,1)S(1)}, u32[]{:S(2)}, u32[]{:S(2)}) collective-permute-start(bf16[96,1536]{1,0:T(8,128)(2,1)S(1)} %collective-permute-done.5.refs_0_), channel_id=1, source_target_pairs={{0,1},{1,0},{2,3},{3,2},{4,5},{5,4},{6,7},{7,6},{8,9},{9,8},{10,11... | collective-permute-start | bytes 884744 | tf_op jit(solution)/shard_map/ppermute | solution.py:272
  66.5 13.3 %collective-permute-start.16 = (bf16[96,1536]{1,0:T(8,128)(2,1)S(1)}, bf16[96,1536]{1,0:T(8,128)(2,1)S(1)}, u32[]{:S(2)}, u32[]{:S(2)}) collective-permute-start(bf16[96,1536]{1,0:T(8,128)(2,1)S(1)} %collective-permute-done.15.refs_2_), channel_id=1, source_target_pairs={{0,1},{1,0},{2,3},{3,2},{4,5},{5,4},{6,7},{7,6},{8,9},{9,8},{10,11... | collective-permute-start | bytes 884744 | tf_op jit(solution)/shard_map/ppermute | solution.py:272
  66.5 10.2 %collective-permute-start.10 = (bf16[80,1536]{1,0:T(8,128)(2,1)S(1)}, bf16[80,1536]{1,0:T(8,128)(2,1)S(1)}, u32[]{:S(2)}, u32[]{:S(2)}) collective-permute-start(bf16[80,1536]{1,0:T(8,128)(2,1)S(1)} %collective-permute-done.8.refs_2_), channel_id=1, source_target_pairs={{0,1},{1,0},{2,3},{3,2},{4,5},{5,4},{6,7},{7,6},{8,9},{9,8},{10,11... | collective-permute-start | bytes 737288 | tf_op jit(solution)/shard_map/ppermute | solution.py:272
  72.2 7.6 %collective-permute-start.14 = (bf16[80,1536]{1,0:T(8,128)(2,1)S(1)}, bf16[80,1536]{1,0:T(8,128)(2,1)S(1)}, u32[]{:S(2)}, u32[]{:S(2)}) collective-permute-start(bf16[80,1536]{1,0:T(8,128)(2,1)S(1)} %collective-permute-done.12.refs_0_), channel_id=1, source_target_pairs={{0,1},{1,0},{2,3},{3,2},{4,5},{5,4},{6,7},{7,6},{8,9},{9,8},{10,11... | collective-permute-start | bytes 737288 | tf_op jit(solution)/shard_map/ppermute | solution.py:272
  72.2 4.5 %collective-permute-start.17 = (f32[1,1024]{1,0:T(1,128)S(1)}, f32[1,1024]{1,0:T(1,128)S(1)}, u32[]{:S(2)}, u32[]{:S(2)}) collective-permute-start(f32[1,1024]{1,0:T(1,128)S(1)} %add.26), channel_id=1, source_target_pairs={{0,16},{4,20},{8,24},{12,28},{16,0},{20,4},{24,8},{28,12},{1,17},{... | collective-permute-start | bytes 12296 | tf_op jit(solution)/shard_map/ppermute | solution.py:272
  85.5 10.4 %collective-permute-start.18 = (bf16[2,128,768]{2,1,0:T(8,128)(2,1)S(1)}, bf16[2,128,768]{2,1,0:T(8,128)(2,1)S(1)}, u32[]{:S(2)}, u32[]{:S(2)}) collective-permute-start(bf16[2,128,768]{2,1,0:T(8,128)(2,1)S(1)} %get-tuple-element.77), channel_id=1, source_target_pairs={{0,4},{4,0},{8,12},{12,8},{16,20},{20,16},{24,28},{28,24},{1,5},{5... | collective-permute-start | bytes 1179656 | tf_op jit(solution)/shard_map/ppermute | solution.py:272
  87.1 10.1 %collective-permute-start.20 = (bf16[2,128,768]{2,1,0:T(8,128)(2,1)S(1)}, bf16[2,128,768]{2,1,0:T(8,128)(2,1)S(1)}, u32[]{:S(2)}, u32[]{:S(2)}) collective-permute-start(bf16[2,128,768]{2,1,0:T(8,128)(2,1)S(1)} %get-tuple-element.81), channel_id=1, source_target_pairs={{0,8},{4,12},{8,0},{12,4},{16,24},{20,28},{24,16},{28,20},{1,9},{5... | collective-permute-start | bytes 1179656 | tf_op jit(solution)/shard_map/ppermute | solution.py:272
  96.0 5.7 %collective-permute-start.19 = (bf16[1,128,768]{2,1,0:T(8,128)(2,1)S(1)}, bf16[1,128,768]{2,1,0:T(8,128)(2,1)S(1)}, u32[]{:S(2)}, u32[]{:S(2)}) collective-permute-start(bf16[1,128,768]{2,1,0:T(8,128)(2,1)S(1)} %get-tuple-element.79), channel_id=1, source_target_pairs={{0,8},{4,12},{8,0},{12,4},{16,24},{20,28},{24,16},{28,20},{1,9},{5... | collective-permute-start | bytes 589832 | tf_op jit(solution)/shard_map/ppermute | solution.py:272
  97.3 5.7 %collective-permute-start.21 = (bf16[1,128,768]{2,1,0:T(8,128)(2,1)S(1)}, bf16[1,128,768]{2,1,0:T(8,128)(2,1)S(1)}, u32[]{:S(2)}, u32[]{:S(2)}) collective-permute-start(bf16[1,128,768]{2,1,0:T(8,128)(2,1)S(1)} %get-tuple-element.83), channel_id=1, source_target_pairs={{0,4},{4,0},{8,12},{12,8},{16,20},{20,16},{24,28},{28,24},{1,5},{5... | collective-permute-start | bytes 589832 | tf_op jit(solution)/shard_map/ppermute | solution.py:272

commit v4 on v3

--- a/solution.py
+++ b/solution.py
@@ -324,20 +324,23 @@
 
     near = [whole[-1]] + [swap(whole[chips - 1 - chip], "own", chip * CORES) for chip in range(1, chips)]
     far_held = [swap(held[0], "pts", half_bit)]
-    near = [(r, swap(r, "own", 1)) for r in near]
     codes = call(
         functools.partial(codes_kernel, chips, starts, tok, wide), [((1, owners * wide), F32)], parents, codes,
         vmem=4,
     )
     cent, base = call(cent_kernel, [((slots, width), BF16), ((share, width), BF16)], centroids[0])
 
-    near_w, near_s, near_x = zip(*[
-        weigh(
-            near[chip], [place(chip, c, starts[chips - 1 - chip]) for c in range(CORES)],
-            after(codes, far_held[0]) if chip else codes,
-        )
-        for chip in range(chips)
-    ])
+    far_codes = swap(codes, "pts", half_bit)
+
+    def weigh_near(chip, rows, codes):
+        start = starts[chips - 1 - chip]
+        return weigh((rows, swap(rows, "own", 1)), [place(chip, c, start) for c in range(CORES)], codes)
+
+    near_got = [weigh_near(0, near[0], codes)]
+    first = near_got[0][1]
+    for chip in range(1, chips):
+        near_got.append(weigh_near(chip, after(near[chip], (first, far_held[0], far_codes)), codes))
+    near_w, near_s, near_x = zip(*near_got)
 
     def forward(k, gate):
         for chip in range(1, chips):
@@ -349,34 +352,38 @@
         for core, r in enumerate((rows, swap(rows, "own", 1))):
             far[int(k == parts[chips - 1 - chip][-1])].append((r, place(chip, core, pieces[k][0])))
 
+    def weigh_far(late, gate):
+        rows = far[late]
+        return weigh([r for r, _ in rows], [p for _, p in rows], after(far_codes, gate))
+
     far, far_cross = [[], []], {}
     partial = sum(near_s)
-    came = swap(jnp.concatenate([partial, codes], axis=1), "pts", half_bit)
-    column, far_codes = partial + came[:, :slots], came[:, slots:]
+    masks = powers(half_bit) + [half_bit | half_bit >> 1]
+    far_held.append(swap(after(held[1], first), "pts", half_bit))
     forward(0, partial)
-    sums = [column]
-    for bit in powers(half_bit):
-        column = column + swap(column, "pts", bit)
-        sums.append(column)
-    far_held.append(swap(after(held[1], sums[0]), "pts", half_bit))
+    sums = [partial]
+    here = [far_cross[c, 0] for c in range(1, chips) if (c, 0) in far_cross]
+    for mask in masks[:-1]:
+        sums.append(sums[-1] + swap(sums[-1], "pts", mask))
+    sums.append(sums[-1] + swap(after(sums[-1], here), "pts", masks[-1]))
+    column = sums[-1]
     for piece in held[2:]:
-        far_held.append(swap(after(piece, sums[1]), "pts", half_bit))
+        far_held.append(swap(after(piece, first), "pts", half_bit))
     balance = call(functools.partial(balance_kernel, chips), [((1, slots), F32)], *near_w, column)
-    balance = after(balance, [far_cross[chip, 0] for chip in range(1, chips) if (chip, 0) in far_cross])
     steps = [balance]
-    for bit in powers(groups):
-        balance = balance + swap(balance, "pts", bit)
+    for k, mask in enumerate(masks[:-1]):
+        balance = balance + swap(balance, "pts", mask)
         steps.append(balance)
     for k in range(1, len(pieces)):
-        forward(k, steps[1])
+        forward(k, column)
     for chip in range(chips):
         mine = parts[chips - 1 - chip]
         for k in mine:
-            pair(chip, k, steps[-2] if k == mine[-1] else steps[0])
-    far_w, _, far_x = zip(*[
-        weigh([r for r, _ in rows], [p for _, p in rows], after(far_codes, gate))
-        for rows, gate in zip(far, (steps[1], steps[-2]))
-    ])
+            pair(chip, k, steps[-1] if k == mine[-1] else steps[0])
+    far_got = [weigh_far(0, steps[1])]
+    balance = balance + swap(after(balance, far_got[0][0]), "pts", masks[-1])
+    far_got.append(weigh_far(1, steps[-1]))
+    far_w, far_x = zip(*[(w, x) for w, _, x in far_got])
 
     bits = powers(half_bit)
     orders = bit_orders(bits)

time: 104 us -> 85.7 us (0.82)
  waiting for transfers between devices: 58 us -> 32.8 us
  starting transfers between devices: 20.8 us -> 26.2 us
  local copies, waits for them, and re-layouts: 1.91 us -> 3.25 us
    ppermute x22 -> x23, waiting for transfers between devices: 58 us -> 32.8 us  [swap(): lax.ppermute(values, axis, [(i, i ^ bit) for i in range(lax.axis_size(axi...]
    ppermute x22 -> x23, starting transfers between devices: 20.8 us -> 26.2 us  [swap(): lax.ppermute(values, axis, [(i, i ^ bit) for i in range(lax.axis_size(axi...]
    unnamed x12, local copies, waits for them, and re-layouts: 1.91 us -> 3.25 us
  transfers between devices with their start and end apart: 22 -> 23, of which waited for: 14 -> 14; matrix products, arithmetic and copies ran while one was open for 0% -> 0% of each run, Pallas kernels for 10% -> 15%
where the time goes in v4:
time: 85.7 us; the launch traced here: 85.5 us
  waiting for transfers between devices  32.8 us (38%)
  starting transfers between devices  26.2 us (31%)
  Pallas kernels  23 us (27%)
  local copies, waits for them, and re-layouts  3.25 us (4%)
    ppermute x23, waiting for transfers between devices, swap(): lax.ppermute(values, axis, [(i, i ^ bit) for i in range(lax.axis_size(axi...  32.8 us
    ppermute x23, starting transfers between devices, swap(): lax.ppermute(values, axis, [(i, i ^ bit) for i in range(lax.axis_size(axi...  26.2 us
    pallas_call x13, Pallas kernels, call(): pl.pallas_call(kernel, out_shape=shapes, in_specs=[pl.BlockSpec(memory_sp...  23 us
    unnamed x12, local copies, waits for them, and re-layouts  3.25 us
  transfers between devices with their start and end apart: 23, of which 14 were waited for; matrix products, arithmetic and copies ran while one was open for 0% of the time, Pallas kernels for 15%

profile of v4, /device:TPU:0, one launch (start us, length us, event | category | flops | bytes accessed | tf_op | source)
XLA Modules:
  0.0 85.5 jit_solution(13302831904352830881)
XLA Ops:
  0.0 3.2 %shard_map.55 = (bf16[80,1536]{1,0:T(8,128)(2,1)}, bf16[96,1536]{1,0:T(8,128)(2,1)}, bf16[80,1536]{1,0:T(8,128)(2,1)}, bf16[176,1536]{1,0:T(8,128)(2,1)}, bf16[1...) custom-call(bf16[256,1536]{1,0:T(8,128)(2,1)} %refs_0_.1, s32[1,1024]{1,0:T(1,128)} %bitcast.14, ...), custom_call_target="tpu_custom_call" | custom-call | tf_op jit(solution)/shard_map/pallas_call | solution.py:255
  3.2 0.5 collective-permute-start
  3.7 2.6 %collective-permute-start.1 = (bf16[176,1536]{1,0:T(8,128)(2,1)}, bf16[176,1536]{1,0:T(8,128)(2,1)S(1)}, u32[]{:S(2)}, u32[]{:S(2)}) collective-permute-start(bf16[176,1536]{1,0:T(8,128)(2,1)} %get-tuple-element.51), channel_id=1, source_target_pairs={{0,2},{1,3},{2,0},{3,1},{4,6},{5,7},{6,4},{7,5},{8,10},{9,11},{10,... | collective-permute-start | bytes 1622024 | tf_op jit(solution)/shard_map/ppermute | solution.py:272
  6.3 2.6 %collective-permute-start.2 = (bf16[80,1536]{1,0:T(8,128)(2,1)}, bf16[80,1536]{1,0:T(8,128)(2,1)S(1)}, u32[]{:S(2)}, u32[]{:S(2)}) collective-permute-start(bf16[80,1536]{1,0:T(8,128)(2,1)} %get-tuple-element.53), channel_id=1, source_target_pairs={{0,16},{4,20},{8,24},{12,28},{16,0},{20,4},{24,8},{28,12},{1,17},{... | collective-permute-start | bytes 737288 | tf_op jit(solution)/shard_map/ppermute | solution.py:272
  8.9 0.7 copy-done.2
  9.6 0.7 copy-done.3
  10.2 1.4 %shard_map.56.refs_2_ = f32[1,704]{1,0:T(1,128)S(1)} custom-call(s32[1,1024]{1,0:T(1,128)S(1)} %copy-done.2, f32[1,64]{1,0:T(1,128)S(1)} %copy-done.3), custom_call_target="tpu_custom_call" | custom-call | tf_op jit(solution)/shard_map/pallas_call | solution.py:255
  11.6 0.4 collective-permute-start.3
  12.0 1.9 %copy-done = bf16[1,1024,1536]{2,1,0:T(8,128)(2,1)S(1)} copy-done((bf16[1,1024,1536]{2,1,0:T(8,128)(2,1)S(1)}, bf16[1,1024,1536]{2,1,0:T(8,128)(2,1)}, u32[]{:S(2)}) %copy-start) | copy-done | bytes 3145752
  13.9 1.0 %shard_map.57 = (bf16[1024,1536]{1,0:T(8,128)(2,1)S(1)}, bf16[128,1536]{1,0:T(8,128)(2,1)S(1)}) custom-call(bf16[1024,1536]{1,0:T(8,128)(2,1)S(1)} %bitcast.9), custom_call_target="tpu_custom_call" | custom-call | tf_op jit(solution)/shard_map/pallas_call | solution.py:255
  15.0 2.6 %shard_map.58 = (f32[352,1024]{1,0:T(8,128)S(1)}, f32[1,1024]{1,0:T(1,128)S(1)}, bf16[352,1536]{1,0:T(8,128)(2,1)S(1)}) custom-call(bf16[176,1536]{1,0:T(8,128)(2,1)S(1)} %copy-done.1, bf16[176,1536]{1,0:T(8,128)(2,1)S(1)} %collective-permute-done.refs_1_, f32[1,704]{1,0:T(1,128)S(1)} %shard_map.56.refs_2_, ...), custom_call_target="tpu_custom_call" | custom-call | tf_op jit(solution)/shard_map/pallas_call | solution.py:255
  17.6 3.2 %collective-permute-done.3.refs_4_ = f32[1,704]{1,0:T(1,128)S(1)} collective-permute-done((f32[1,704]{1,0:T(1,128)S(1)}, f32[1,704]{1,0:T(1,128)S(1)}, u32[]{:S(2)}, u32[]{:S(2)}) %collective-permute-start.3) | collective-permute-done | bytes 2848 | tf_op jit(solution)/shard_map/ppermute | solution.py:272
  20.9 1.4 %collective-permute-start.5 = (bf16[96,1536]{1,0:T(8,128)(2,1)S(1)}, bf16[96,1536]{1,0:T(8,128)(2,1)S(1)}, u32[]{:S(2)}, u32[]{:S(2)}) collective-permute-start(bf16[96,1536]{1,0:T(8,128)(2,1)S(1)} %copy-done.4), channel_id=1, source_target_pairs={{0,16},{4,20},{8,24},{12,28},{16,0},{20,4},{24,8},{28,12},{1,17},{... | collective-permute-start | bytes 884744 | tf_op jit(solution)/shard_map/ppermute | solution.py:272
  22.3 0.5 collective-permute-done.4.refs_1_
  22.8 2.5 %shard_map.59 = (f32[352,1024]{1,0:T(8,128)S(1)}, f32[1,1024]{1,0:T(1,128)S(1)}, bf16[352,1536]{1,0:T(8,128)(2,1)S(1)}) custom-call(bf16[176,1536]{1,0:T(8,128)(2,1)S(1)} %collective-permute-done.1.refs_0_, bf16[176,1536]{1,0:T(8,128)(2,1)S(1)} %collective-permute-done.4.refs_1_, f32[1,704]{1,0:T(1,128)S(1)} %shard_map.56.refs_2_, ...), custom_call_target="tpu_custom_call" | custom-call | tf_op jit(solution)/shard_map/pallas_call | solution.py:255
  25.3 1.1 %collective-permute-start.8 = (bf16[80,1536]{1,0:T(8,128)(2,1)S(1)}, bf16[80,1536]{1,0:T(8,128)(2,1)S(1)}, u32[]{:S(2)}, u32[]{:S(2)}) collective-permute-start(bf16[80,1536]{1,0:T(8,128)(2,1)S(1)} %collective-permute-done.2), channel_id=1, source_target_pairs={{0,2},{1,3},{2,0},{3,1},{4,6},{5,7},{6,4},{7,5},{8,10},{9,11},{10,... | collective-permute-start | bytes 737288 | tf_op jit(solution)/shard_map/ppermute | solution.py:272
  26.4 1.5 %collective-permute-start.6 = (f32[1,1024]{1,0:T(1,128)S(1)}, f32[1,1024]{1,0:T(1,128)S(1)}, u32[]{:S(2)}, u32[]{:S(2)}) collective-permute-start(f32[1,1024]{1,0:T(1,128)S(1)} %add.21), channel_id=1, source_target_pairs={{0,4},{4,0},{8,12},{12,8},{16,20},{20,16},{24,28},{28,24},{1,5},{5... | collective-permute-start | bytes 12296 | tf_op jit(solution)/shard_map/ppermute | solution.py:272
  27.9 2.1 %collective-permute-done.6 = f32[1,1024]{1,0:T(1,128)S(1)} collective-permute-done((f32[1,1024]{1,0:T(1,128)S(1)}, f32[1,1024]{1,0:T(1,128)S(1)}, u32[]{:S(2)}, u32[]{:S(2)}) %collective-permute-start.6) | collective-permute-done | bytes 4128 | tf_op jit(solution)/shard_map/ppermute | solution.py:272
  30.0 1.7 %collective-permute-start.7 = (f32[1,1024]{1,0:T(1,128)S(1)}, f32[1,1024]{1,0:T(1,128)S(1)}, u32[]{:S(2)}, u32[]{:S(2)}) collective-permute-start(f32[1,1024]{1,0:T(1,128)S(1)} %add.22), channel_id=1, source_target_pairs={{0,8},{4,12},{8,0},{12,4},{16,24},{20,28},{24,16},{28,20},{1,9},{5... | collective-permute-start | bytes 12296 | tf_op jit(solution)/shard_map/ppermute | solution.py:272
  31.7 2.3 %collective-permute-done.7 = f32[1,1024]{1,0:T(1,128)S(1)} collective-permute-done((f32[1,1024]{1,0:T(1,128)S(1)}, f32[1,1024]{1,0:T(1,128)S(1)}, u32[]{:S(2)}, u32[]{:S(2)}) %collective-permute-start.7) | collective-permute-done | bytes 4128 | tf_op jit(solution)/shard_map/ppermute | solution.py:272
  34.0 3.0 %collective-permute-start.9 = (f32[1,1024]{1,0:T(1,128)S(1)}, f32[1,1024]{1,0:T(1,128)S(1)}, u32[]{:S(2)}, u32[]{:S(2)}) collective-permute-start(f32[1,1024]{1,0:T(1,128)S(1)} %add.23), channel_id=1, source_target_pairs={{0,24},{4,28},{8,16},{12,20},{16,8},{20,12},{24,0},{28,4},{1,25},{... | collective-permute-start | bytes 12296 | tf_op jit(solution)/shard_map/ppermute | solution.py:272
  37.0 2.5 %collective-permute-done.9 = f32[1,1024]{1,0:T(1,128)S(1)} collective-permute-done((f32[1,1024]{1,0:T(1,128)S(1)}, f32[1,1024]{1,0:T(1,128)S(1)}, u32[]{:S(2)}, u32[]{:S(2)}) %collective-permute-start.9) | collective-permute-done | bytes 4128 | tf_op jit(solution)/shard_map/ppermute | solution.py:272
  39.5 1.2 %collective-permute-start.16 = (bf16[96,1536]{1,0:T(8,128)(2,1)S(1)}, bf16[96,1536]{1,0:T(8,128)(2,1)S(1)}, u32[]{:S(2)}, u32[]{:S(2)}) collective-permute-start(bf16[96,1536]{1,0:T(8,128)(2,1)S(1)} %collective-permute-done.5.refs_0_), channel_id=1, source_target_pairs={{0,2},{1,3},{2,0},{3,1},{4,6},{5,7},{6,4},{7,5},{8,10},{9,11},{10,... | collective-permute-start | bytes 884744 | tf_op jit(solution)/shard_map/ppermute | solution.py:272
  40.7 0.6 shard_map.60
  41.2 1.6 %collective-permute-start.12 = (f32[1,1024]{1,0:T(1,128)S(1)}, f32[1,1024]{1,0:T(1,128)S(1)}, u32[]{:S(2)}, u32[]{:S(2)}) collective-permute-start(f32[1,1024]{1,0:T(1,128)S(1)} %shard_map.60), channel_id=1, source_target_pairs={{0,4},{4,0},{8,12},{12,8},{16,20},{20,16},{24,28},{28,24},{1,5},{5... | collective-permute-start | bytes 12296 | tf_op jit(solution)/shard_map/ppermute | solution.py:272
  42.8 2.1 %collective-permute-done.12 = f32[1,1024]{1,0:T(1,128)S(1)} collective-permute-done((f32[1,1024]{1,0:T(1,128)S(1)}, f32[1,1024]{1,0:T(1,128)S(1)}, u32[]{:S(2)}, u32[]{:S(2)}) %collective-permute-start.12) | collective-permute-done | bytes 4128 | tf_op jit(solution)/shard_map/ppermute | solution.py:272
  44.9 3.9 %collective-permute-start.14 = (f32[1,1024]{1,0:T(1,128)S(1)}, f32[1,1024]{1,0:T(1,128)S(1)}, u32[]{:S(2)}, u32[]{:S(2)}) collective-permute-start(f32[1,1024]{1,0:T(1,128)S(1)} %add.25), channel_id=1, source_target_pairs={{0,8},{4,12},{8,0},{12,4},{16,24},{20,28},{24,16},{28,20},{1,9},{5... | collective-permute-start | bytes 12296 | tf_op jit(solution)/shard_map/ppermute | solution.py:272
  48.8 2.0 %collective-permute-done.14 = f32[1,1024]{1,0:T(1,128)S(1)} collective-permute-done((f32[1,1024]{1,0:T(1,128)S(1)}, f32[1,1024]{1,0:T(1,128)S(1)}, u32[]{:S(2)}, u32[]{:S(2)}) %collective-permute-start.14) | collective-permute-done | bytes 4128 | tf_op jit(solution)/shard_map/ppermute | solution.py:272
  50.8 0.1 collective-permute-start.17
  50.9 0.5 collective-permute-start.11
  51.4 0.5 collective-permute-done.13.refs_0_
  51.8 1.0 %collective-permute-done.11.refs_3_ = bf16[80,1536]{1,0:T(8,128)(2,1)S(1)} collective-permute-done((bf16[80,1536]{1,0:T(8,128)(2,1)S(1)}, bf16[80,1536]{1,0:T(8,128)(2,1)S(1)}, u32[]{:S(2)}, u32[]{:S(2)}) %collective-permute-start.11) | collective-permute-done | bytes 245792 | tf_op jit(solution)/shard_map/ppermute | solution.py:272
  52.8 3.0 %shard_map.61 = (f32[352,1024]{1,0:T(8,128)S(1)}, f32[1,1024]{1,0:T(1,128)}, bf16[352,1536]{1,0:T(8,128)(2,1)S(1)}) custom-call(bf16[96,1536]{1,0:T(8,128)(2,1)S(1)} %collective-permute-done.5.refs_0_, bf16[96,1536]{1,0:T(8,128)(2,1)S(1)} %collective-permute-done.10.refs_1_, bf16[80,1536]{1,0:T(8,128)(2,1)S(1)} %collective-permute-done.8.refs_2_, ...), custom_call_target="tpu_custom_call" | custom-call | tf_op jit(solution)/shard_map/pallas_call | solution.py:255
  55.8 2.3 %collective-permute-start.18 = (f32[1,1024]{1,0:T(1,128)S(1)}, f32[1,1024]{1,0:T(1,128)S(1)}, u32[]{:S(2)}, u32[]{:S(2)}) collective-permute-start(f32[1,1024]{1,0:T(1,128)S(1)} %add.26), channel_id=1, source_target_pairs={{0,24},{4,28},{8,16},{12,20},{16,8},{20,12},{24,0},{28,4},{1,25},{... | collective-permute-start | bytes 12296 | tf_op jit(solution)/shard_map/ppermute | solution.py:272
  58.1 3.1 %collective-permute-done.18 = f32[1,1024]{1,0:T(1,128)S(1)} collective-permute-done((f32[1,1024]{1,0:T(1,128)S(1)}, f32[1,1024]{1,0:T(1,128)S(1)}, u32[]{:S(2)}, u32[]{:S(2)}) %collective-permute-start.18) | collective-permute-done | bytes 4128 | tf_op jit(solution)/shard_map/ppermute | solution.py:272
  61.3 3.0 %shard_map.62 = (f32[352,1024]{1,0:T(8,128)S(1)}, f32[1,1024]{1,0:T(1,128)}, bf16[352,1536]{1,0:T(8,128)(2,1)S(1)}) custom-call(bf16[80,1536]{1,0:T(8,128)(2,1)S(1)} %collective-permute-done.13.refs_0_, bf16[80,1536]{1,0:T(8,128)(2,1)S(1)} %collective-permute-done.15.refs_1_, bf16[96,1536]{1,0:T(8,128)(2,1)S(1)} %collective-permute-done.16.refs_2_, ...), custom_call_target="tpu_custom_call" | custom-call | tf_op jit(solution)/shard_map/pallas_call | solution.py:255
  64.3 2.7 %shard_map.63 = (bf16[2,128,768]{2,1,0:T(8,128)(2,1)S(1)}, bf16[2,128,768]{2,1,0:T(8,128)(2,1)S(1)}, bf16[1408,512]{1,0:T(8,128)(2,1)S(1)}) custom-call(f32[352,1024]{1,0:T(8,128)S(1)} %get-tuple-element.50.refs_0_, f32[352,1024]{1,0:T(8,128)S(1)} %get-tuple-element.55.refs_1_, f32[352,1024]{1,0:T(8,128)S(1)} %get-tuple-element.64.refs_2_, ...), custom_call_target="tpu_custom_call" | custom-call | tf_op jit(solution)/shard_map/pallas_call | solution.py:255
  67.0 1.6 %collective-permute-start.19 = (bf16[2,128,768]{2,1,0:T(8,128)(2,1)S(1)}, bf16[2,128,768]{2,1,0:T(8,128)(2,1)S(1)}, u32[]{:S(2)}, u32[]{:S(2)}) collective-permute-start(bf16[2,128,768]{2,1,0:T(8,128)(2,1)S(1)} %get-tuple-element.79), channel_id=1, source_target_pairs={{0,4},{4,0},{8,12},{12,8},{16,20},{20,16},{24,28},{28,24},{1,5},{5... | collective-permute-start | bytes 1179656 | tf_op jit(solution)/shard_map/ppermute | solution.py:272
  68.5 1.9 %shard_map.64 = (f32[2,128,768]{2,1,0:T(8,128)S(1)}, f32[2,128,768]{2,1,0:T(8,128)S(1)}) custom-call(bf16[1408,512]{1,0:T(8,128)(2,1)S(1)} %get-tuple-element.77.refs_0_, bf16[352,1536]{1,0:T(8,128)(2,1)S(1)} %get-tuple-element.73.refs_5_.refs_1_, bf16[352,1536]{1,0:T(8,128)(2,1)S(1)} %get-tuple-element.74.refs_6_.refs_2_, ...), custom_call_target="tpu_custom_call" | custom-call | tf_op jit(solution)/shard_map/pallas_call | solution.py:255
  70.4 6.6 %collective-permute-done.19.came_ref = bf16[2,128,768]{2,1,0:T(8,128)(2,1)S(1)} collective-permute-done((bf16[2,128,768]{2,1,0:T(8,128)(2,1)S(1)}, bf16[2,128,768]{2,1,0:T(8,128)(2,1)S(1)}, u32[]{:S(2)}, u32[]{:S(2)}) %collective-permute-start.19) | collective-permute-done | bytes 393248 | tf_op jit(solution)/shard_map/ppermute | solution.py:272
  77.0 0.1 shard_map.65
  77.1 0.1 collective-permute-start.20
  77.2 1.5 %collective-permute-done.21.came_ref = bf16[2,128,768]{2,1,0:T(8,128)(2,1)S(1)} collective-permute-done((bf16[2,128,768]{2,1,0:T(8,128)(2,1)S(1)}, bf16[2,128,768]{2,1,0:T(8,128)(2,1)S(1)}, u32[]{:S(2)}, u32[]{:S(2)}) %collective-permute-start.21) | collective-permute-done | bytes 393248 | tf_op jit(solution)/shard_map/ppermute | solution.py:272
  78.7 0.1 shard_map.66
  78.7 0.2 collective-permute-start.22
  78.9 3.9 %collective-permute-done.20 = bf16[1,128,768]{2,1,0:T(8,128)(2,1)S(1)} collective-permute-done((bf16[1,128,768]{2,1,0:T(8,128)(2,1)S(1)}, bf16[1,128,768]{2,1,0:T(8,128)(2,1)S(1)}, u32[]{:S(2)}, u32[]{:S(2)}) %collective-permute-start.20) | collective-permute-done | bytes 196640 | tf_op jit(solution)/shard_map/ppermute | solution.py:272
  82.9 1.6 %collective-permute-done.22 = bf16[1,128,768]{2,1,0:T(8,128)(2,1)S(1)} collective-permute-done((bf16[1,128,768]{2,1,0:T(8,128)(2,1)S(1)}, bf16[1,128,768]{2,1,0:T(8,128)(2,1)S(1)}, u32[]{:S(2)}, u32[]{:S(2)}) %collective-permute-start.22) | collective-permute-done | bytes 196640 | tf_op jit(solution)/shard_map/ppermute | solution.py:272
  84.5 1.0 %shard_map.67 = bf16[128,1536]{1,0:T(8,128)(2,1)} custom-call(f32[128,768]{1,0:T(8,128)S(1)} %bitcast.10, bf16[128,768]{1,0:T(8,128)(2,1)S(1)} %bitcast.12, f32[128,768]{1,0:T(8,128)S(1)} %bitcast.11, bf16[128,768]{1,0:T(8,128)(2,1)S(1)} %bitcast.13, bf16[128,1536]{1,0:T(8,128)(2,1)S(1)} %get-tuple-element.86.refs_4_), custom_call_target="tpu_custom_call" | custom-call | tf_op jit(solution)/shard_map/pallas_call | solution.py:255
  (30 shorter events, 0.1 us)
Async XLA Ops:
  3.2 11.7 %collective-permute-start = (bf16[176,1536]{1,0:T(8,128)(2,1)}, bf16[176,1536]{1,0:T(8,128)(2,1)S(1)}, u32[]{:S(2)}, u32[]{:S(2)}) collective-permute-start(bf16[176,1536]{1,0:T(8,128)(2,1)} %get-tuple-element.46.refs_0_), channel_id=1, source_target_pairs={{0,1},{1,0},{2,3},{3,2},{4,5},{5,4},{6,7},{7,6},{8,9},{9,8},{10,11... | collective-permute-start | bytes 1622024 | tf_op jit(solution)/shard_map/ppermute | solution.py:272
  3.7 17.1 %collective-permute-start.1 = (bf16[176,1536]{1,0:T(8,128)(2,1)}, bf16[176,1536]{1,0:T(8,128)(2,1)S(1)}, u32[]{:S(2)}, u32[]{:S(2)}) collective-permute-start(bf16[176,1536]{1,0:T(8,128)(2,1)} %get-tuple-element.51), channel_id=1, source_target_pairs={{0,2},{1,3},{2,0},{3,1},{4,6},{5,7},{6,4},{7,5},{8,10},{9,11},{10,... | collective-permute-start | bytes 1622024 | tf_op jit(solution)/shard_map/ppermute | solution.py:272
  6.3 14.5 %collective-permute-start.2 = (bf16[80,1536]{1,0:T(8,128)(2,1)}, bf16[80,1536]{1,0:T(8,128)(2,1)S(1)}, u32[]{:S(2)}, u32[]{:S(2)}) collective-permute-start(bf16[80,1536]{1,0:T(8,128)(2,1)} %get-tuple-element.53), channel_id=1, source_target_pairs={{0,16},{4,20},{8,24},{12,28},{16,0},{20,4},{24,8},{28,12},{1,17},{... | collective-permute-start | bytes 737288 | tf_op jit(solution)/shard_map/ppermute | solution.py:272
  8.9 0.7 copy-start.2
  9.6 0.7 copy-start.3
  11.6 9.2 %collective-permute-start.3 = (f32[1,704]{1,0:T(1,128)S(1)}, f32[1,704]{1,0:T(1,128)S(1)}, u32[]{:S(2)}, u32[]{:S(2)}) collective-permute-start(f32[1,704]{1,0:T(1,128)S(1)} %shard_map.56.refs_2_), channel_id=1, source_target_pairs={{0,16},{4,20},{8,24},{12,28},{16,0},{20,4},{24,8},{28,12},{1,17},{... | collective-permute-start | bytes 8456 | tf_op jit(solution)/shard_map/ppermute | solution.py:272
  12.0 1.9 %copy-start = (bf16[1,1024,1536]{2,1,0:T(8,128)(2,1)S(1)}, bf16[1,1024,1536]{2,1,0:T(8,128)(2,1)}, u32[]{:S(2)}) copy-start(bf16[1,1024,1536]{2,1,0:T(8,128)(2,1)} %param.9) | copy-start | bytes 9437188
  13.9 1.0 %copy-start.1 = (bf16[176,1536]{1,0:T(8,128)(2,1)S(1)}, bf16[176,1536]{1,0:T(8,128)(2,1)}, u32[]{:S(2)}) copy-start(bf16[176,1536]{1,0:T(8,128)(2,1)} %get-tuple-element.46.refs_0_) | copy-start | bytes 1622020
  15.0 5.9 %copy-start.4 = (bf16[96,1536]{1,0:T(8,128)(2,1)S(1)}, bf16[96,1536]{1,0:T(8,128)(2,1)}, u32[]{:S(2)}) copy-start(bf16[96,1536]{1,0:T(8,128)(2,1)} %get-tuple-element.57) | copy-start | bytes 884740
  20.8 1.9 %collective-permute-start.4 = (bf16[176,1536]{1,0:T(8,128)(2,1)S(1)}, bf16[176,1536]{1,0:T(8,128)(2,1)S(1)}, u32[]{:S(2)}, u32[]{:S(2)}) collective-permute-start(bf16[176,1536]{1,0:T(8,128)(2,1)S(1)} %collective-permute-done.1.refs_0_), channel_id=1, source_target_pairs={{0,1},{1,0},{2,3},{3,2},{4,5},{5,4},{6,7},{7,6},{8,9},{9,8},{10,11... | collective-permute-start | bytes 1622024 | tf_op jit(solution)/shard_map/ppermute | solution.py:272
  20.9 19.8 %copy-start.5 = (bf16[80,1536]{1,0:T(8,128)(2,1)S(1)}, bf16[80,1536]{1,0:T(8,128)(2,1)}, u32[]{:S(2)}) copy-start(bf16[80,1536]{1,0:T(8,128)(2,1)} %get-tuple-element.66) | copy-start | bytes 737284
  20.9 18.6 %collective-permute-start.5 = (bf16[96,1536]{1,0:T(8,128)(2,1)S(1)}, bf16[96,1536]{1,0:T(8,128)(2,1)S(1)}, u32[]{:S(2)}, u32[]{:S(2)}) collective-permute-start(bf16[96,1536]{1,0:T(8,128)(2,1)S(1)} %copy-done.4), channel_id=1, source_target_pairs={{0,16},{4,20},{8,24},{12,28},{16,0},{20,4},{24,8},{28,12},{1,17},{... | collective-permute-start | bytes 884744 | tf_op jit(solution)/shard_map/ppermute | solution.py:272
  25.3 8.7 %collective-permute-start.8 = (bf16[80,1536]{1,0:T(8,128)(2,1)S(1)}, bf16[80,1536]{1,0:T(8,128)(2,1)S(1)}, u32[]{:S(2)}, u32[]{:S(2)}) collective-permute-start(bf16[80,1536]{1,0:T(8,128)(2,1)S(1)} %collective-permute-done.2), channel_id=1, source_target_pairs={{0,2},{1,3},{2,0},{3,1},{4,6},{5,7},{6,4},{7,5},{8,10},{9,11},{10,... | collective-permute-start | bytes 737288 | tf_op jit(solution)/shard_map/ppermute | solution.py:272
  26.4 3.6 %collective-permute-start.6 = (f32[1,1024]{1,0:T(1,128)S(1)}, f32[1,1024]{1,0:T(1,128)S(1)}, u32[]{:S(2)}, u32[]{:S(2)}) collective-permute-start(f32[1,1024]{1,0:T(1,128)S(1)} %add.21), channel_id=1, source_target_pairs={{0,4},{4,0},{8,12},{12,8},{16,20},{20,16},{24,28},{28,24},{1,5},{5... | collective-permute-start | bytes 12296 | tf_op jit(solution)/shard_map/ppermute | solution.py:272
  30.0 4.0 %collective-permute-start.7 = (f32[1,1024]{1,0:T(1,128)S(1)}, f32[1,1024]{1,0:T(1,128)S(1)}, u32[]{:S(2)}, u32[]{:S(2)}) collective-permute-start(f32[1,1024]{1,0:T(1,128)S(1)} %add.22), channel_id=1, source_target_pairs={{0,8},{4,12},{8,0},{12,4},{16,24},{20,28},{24,16},{28,20},{1,9},{5... | collective-permute-start | bytes 12296 | tf_op jit(solution)/shard_map/ppermute | solution.py:272
  34.0 5.5 %collective-permute-start.9 = (f32[1,1024]{1,0:T(1,128)S(1)}, f32[1,1024]{1,0:T(1,128)S(1)}, u32[]{:S(2)}, u32[]{:S(2)}) collective-permute-start(f32[1,1024]{1,0:T(1,128)S(1)} %add.23), channel_id=1, source_target_pairs={{0,24},{4,28},{8,16},{12,20},{16,8},{20,12},{24,0},{28,4},{1,25},{... | collective-permute-start | bytes 12296 | tf_op jit(solution)/shard_map/ppermute | solution.py:272
  39.5 11.3 %collective-permute-start.16 = (bf16[96,1536]{1,0:T(8,128)(2,1)S(1)}, bf16[96,1536]{1,0:T(8,128)(2,1)S(1)}, u32[]{:S(2)}, u32[]{:S(2)}) collective-permute-start(bf16[96,1536]{1,0:T(8,128)(2,1)S(1)} %collective-permute-done.5.refs_0_), channel_id=1, source_target_pairs={{0,2},{1,3},{2,0},{3,1},{4,6},{5,7},{6,4},{7,5},{8,10},{9,11},{10,... | collective-permute-start | bytes 884744 | tf_op jit(solution)/shard_map/ppermute | solution.py:272
  40.7 11.2 %collective-permute-start.13 = (bf16[80,1536]{1,0:T(8,128)(2,1)S(1)}, bf16[80,1536]{1,0:T(8,128)(2,1)S(1)}, u32[]{:S(2)}, u32[]{:S(2)}) collective-permute-start(bf16[80,1536]{1,0:T(8,128)(2,1)S(1)} %copy-done.5), channel_id=1, source_target_pairs={{0,16},{4,20},{8,24},{12,28},{16,0},{20,4},{24,8},{28,12},{1,17},{... | collective-permute-start | bytes 737288 | tf_op jit(solution)/shard_map/ppermute | solution.py:272
  41.2 3.7 %collective-permute-start.12 = (f32[1,1024]{1,0:T(1,128)S(1)}, f32[1,1024]{1,0:T(1,128)S(1)}, u32[]{:S(2)}, u32[]{:S(2)}) collective-permute-start(f32[1,1024]{1,0:T(1,128)S(1)} %shard_map.60), channel_id=1, source_target_pairs={{0,4},{4,0},{8,12},{12,8},{16,20},{20,16},{24,28},{28,24},{1,5},{5... | collective-permute-start | bytes 12296 | tf_op jit(solution)/shard_map/ppermute | solution.py:272
  42.8 10.0 %collective-permute-start.10 = (bf16[96,1536]{1,0:T(8,128)(2,1)S(1)}, bf16[96,1536]{1,0:T(8,128)(2,1)S(1)}, u32[]{:S(2)}, u32[]{:S(2)}) collective-permute-start(bf16[96,1536]{1,0:T(8,128)(2,1)S(1)} %collective-permute-done.5.refs_0_), channel_id=1, source_target_pairs={{0,1},{1,0},{2,3},{3,2},{4,5},{5,4},{6,7},{7,6},{8,9},{9,8},{10,11... | collective-permute-start | bytes 884744 | tf_op jit(solution)/shard_map/ppermute | solution.py:272
  44.9 5.9 %collective-permute-start.14 = (f32[1,1024]{1,0:T(1,128)S(1)}, f32[1,1024]{1,0:T(1,128)S(1)}, u32[]{:S(2)}, u32[]{:S(2)}) collective-permute-start(f32[1,1024]{1,0:T(1,128)S(1)} %add.25), channel_id=1, source_target_pairs={{0,8},{4,12},{8,0},{12,4},{16,24},{20,28},{24,16},{28,20},{1,9},{5... | collective-permute-start | bytes 12296 | tf_op jit(solution)/shard_map/ppermute | solution.py:272
  50.8 10.5 %collective-permute-start.17 = (bf16[96,1536]{1,0:T(8,128)(2,1)S(1)}, bf16[96,1536]{1,0:T(8,128)(2,1)S(1)}, u32[]{:S(2)}, u32[]{:S(2)}) collective-permute-start(bf16[96,1536]{1,0:T(8,128)(2,1)S(1)} %collective-permute-done.16.refs_2_), channel_id=1, source_target_pairs={{0,1},{1,0},{2,3},{3,2},{4,5},{5,4},{6,7},{7,6},{8,9},{9,8},{10,11... | collective-permute-start | bytes 884744 | tf_op jit(solution)/shard_map/ppermute | solution.py:272
  50.9 1.9 %collective-permute-start.11 = (bf16[80,1536]{1,0:T(8,128)(2,1)S(1)}, bf16[80,1536]{1,0:T(8,128)(2,1)S(1)}, u32[]{:S(2)}, u32[]{:S(2)}) collective-permute-start(bf16[80,1536]{1,0:T(8,128)(2,1)S(1)} %collective-permute-done.8.refs_2_), channel_id=1, source_target_pairs={{0,1},{1,0},{2,3},{3,2},{4,5},{5,4},{6,7},{7,6},{8,9},{9,8},{10,11... | collective-permute-start | bytes 737288 | tf_op jit(solution)/shard_map/ppermute | solution.py:272
  51.8 9.4 %collective-permute-start.15 = (bf16[80,1536]{1,0:T(8,128)(2,1)S(1)}, bf16[80,1536]{1,0:T(8,128)(2,1)S(1)}, u32[]{:S(2)}, u32[]{:S(2)}) collective-permute-start(bf16[80,1536]{1,0:T(8,128)(2,1)S(1)} %collective-permute-done.13.refs_0_), channel_id=1, source_target_pairs={{0,1},{1,0},{2,3},{3,2},{4,5},{5,4},{6,7},{7,6},{8,9},{9,8},{10,11... | collective-permute-start | bytes 737288 | tf_op jit(solution)/shard_map/ppermute | solution.py:272
  55.8 5.4 %collective-permute-start.18 = (f32[1,1024]{1,0:T(1,128)S(1)}, f32[1,1024]{1,0:T(1,128)S(1)}, u32[]{:S(2)}, u32[]{:S(2)}) collective-permute-start(f32[1,1024]{1,0:T(1,128)S(1)} %add.26), channel_id=1, source_target_pairs={{0,24},{4,28},{8,16},{12,20},{16,8},{20,12},{24,0},{28,4},{1,25},{... | collective-permute-start | bytes 12296 | tf_op jit(solution)/shard_map/ppermute | solution.py:272
  67.0 10.1 %collective-permute-start.19 = (bf16[2,128,768]{2,1,0:T(8,128)(2,1)S(1)}, bf16[2,128,768]{2,1,0:T(8,128)(2,1)S(1)}, u32[]{:S(2)}, u32[]{:S(2)}) collective-permute-start(bf16[2,128,768]{2,1,0:T(8,128)(2,1)S(1)} %get-tuple-element.79), channel_id=1, source_target_pairs={{0,4},{4,0},{8,12},{12,8},{16,20},{20,16},{24,28},{28,24},{1,5},{5... | collective-permute-start | bytes 1179656 | tf_op jit(solution)/shard_map/ppermute | solution.py:272
  68.5 10.1 %collective-permute-start.21 = (bf16[2,128,768]{2,1,0:T(8,128)(2,1)S(1)}, bf16[2,128,768]{2,1,0:T(8,128)(2,1)S(1)}, u32[]{:S(2)}, u32[]{:S(2)}) collective-permute-start(bf16[2,128,768]{2,1,0:T(8,128)(2,1)S(1)} %get-tuple-element.83), channel_id=1, source_target_pairs={{0,8},{4,12},{8,0},{12,4},{16,24},{20,28},{24,16},{28,20},{1,9},{5... | collective-permute-start | bytes 1179656 | tf_op jit(solution)/shard_map/ppermute | solution.py:272
  77.1 5.7 %collective-permute-start.20 = (bf16[1,128,768]{2,1,0:T(8,128)(2,1)S(1)}, bf16[1,128,768]{2,1,0:T(8,128)(2,1)S(1)}, u32[]{:S(2)}, u32[]{:S(2)}) collective-permute-start(bf16[1,128,768]{2,1,0:T(8,128)(2,1)S(1)} %get-tuple-element.81), channel_id=1, source_target_pairs={{0,8},{4,12},{8,0},{12,4},{16,24},{20,28},{24,16},{28,20},{1,9},{5... | collective-permute-start | bytes 589832 | tf_op jit(solution)/shard_map/ppermute | solution.py:272
  78.7 5.7 %collective-permute-start.22 = (bf16[1,128,768]{2,1,0:T(8,128)(2,1)S(1)}, bf16[1,128,768]{2,1,0:T(8,128)(2,1)S(1)}, u32[]{:S(2)}, u32[]{:S(2)}) collective-permute-start(bf16[1,128,768]{2,1,0:T(8,128)(2,1)S(1)} %get-tuple-element.85), channel_id=1, source_target_pairs={{0,4},{4,0},{8,12},{12,8},{16,20},{20,16},{24,28},{28,24},{1,5},{5... | collective-permute-start | bytes 589832 | tf_op jit(solution)/shard_map/ppermute | solution.py:272

commit v5 on v4

--- a/solution.py
+++ b/solution.py
@@ -43,9 +43,10 @@
     wide = max(e - s for s, e in zip(starts, ends))
     starts = [min(s, tok - wide) for s in starts]
     starts = [min(s, tok - wide) for s in starts]
-    cuts = sorted(set(starts + [s + wide for s in starts] + [0, tok]))
+    soon = down(starts[min(1, chips - 1)] * 13 // 16)
+    cuts = sorted({0, soon, tok} | {s + wide for s in starts})
     pieces = list(zip(cuts[:-1], cuts[1:]))
-    parts = [[k for k, (lo, hi) in enumerate(pieces) if s <= lo and hi <= s + wide] for s in starts]
+    parts = [[k for k, (lo, hi) in enumerate(pieces) if lo < s + wide and s < hi] for s in starts]
     return starts, wide, pieces, parts
 
 
@@ -137,11 +138,10 @@
     slots, width = cent_ref.shape
     total = codes_ref.shape[1]
     at = 0
-    for row_ref, place in zip(row_refs, places):
-        size = row_ref.shape[0]
+    for row_ref, (place, skip, size) in zip(row_refs, places):
         part = slice(at, at + size)
         at += size
-        rows_ref[part, :] = row_ref[...]
+        rows_ref[part, :] = row_ref[skip : skip + size, :]
         hit = iota((size, total), 1) == iota((size, total), 0) + place
         code = jnp.sum(jnp.where(hit, codes_ref[...], 0.0), axis=1, keepdims=True).astype(I32)
         first = (code % OWNER_SHIFT) // FIRST_SHIFT
@@ -160,7 +160,7 @@
         sum_ref[:, pl.ds(at, tile)] = jnp.sum(w, axis=0, keepdims=True)
         return carry
 
-    lax.fori_loop(0, slots // tile, step, 0)
+    lax.fori_loop(0, slots // tile, step, 0, unroll=True)
 
 
 def inverse(values):
@@ -195,9 +195,9 @@
             at += ROWS * 2
 
 
-def move_kernel(routes, half_bit, assign_ref, row_refs, out_refs, part_ref):
+def move_kernel(wanted, half_bit, assign_ref, row_refs, out_refs, part_ref):
     low = lax.axis_index("pts") % half_bit
-    for which, (order, out_ref) in enumerate(zip(routes, out_refs)):
+    for (which, order), out_ref in zip(wanted, out_refs):
         share, cols = out_ref.shape[1:]
         block = part_ref.shape[0]
         lanes = slice(which * cols, (which + 1) * cols)
@@ -217,39 +217,45 @@
             out_ref[k] = moved.astype(out_ref.dtype)
 
 
-def send_kernel(routes, half_bit, nw, *refs):
-    n = len(routes)
+def send_kernel(wanted, half_bit, nw, *refs):
+    n = len(wanted)
     row_refs, out_refs = refs[nw + 1 : -n - 2], refs[-n - 2 : -2]
     assign_ref, part_ref = refs[-2:]
     assign_kernel(half_bit, *refs[: nw + 1], assign_ref)
-    move_kernel(routes, half_bit, assign_ref, row_refs, out_refs, part_ref)
-
-
-def keep_kernel(routes, half_bit, *refs):
-    n = len(routes)
-    move_kernel(routes, half_bit, refs[0], refs[1 : -n - 1], refs[-n - 1 : -1], refs[-1])
-
-
-def merge_kernel(keep_ref, came_ref, *out_refs):
-    total = keep_ref[...] + came_ref[...].astype(F32)
-    n = total.shape[0] // 2
-    out_refs[0][...] = total[:n]
-    out_refs[1][...] = total[n:].astype(BF16)
+    move_kernel(wanted, half_bit, assign_ref, row_refs, out_refs, part_ref)
+
+
+def keep_kernel(wanted, half_bit, *refs):
+    n = len(wanted)
+    move_kernel(wanted, half_bit, refs[0], refs[1 : -n - 1], refs[-n - 1 : -1], refs[-1])
+
+
+def forward_kernel(keep_ref, came_ref, *out_refs):
+    n = came_ref.shape[0]
+    total = (keep_ref[n:] + came_ref[...].astype(F32)).astype(BF16)
+    at = n
+    for out_ref in out_refs:
+        at -= out_ref.shape[0]
+        out_ref[...] = total[at : at + out_ref.shape[0]]
+
+
+def merge_kernel(keep_ref, came_ref, out_ref):
+    out_ref[...] = keep_ref[: came_ref.shape[0]] + came_ref[...].astype(F32)
 
 
 def final_kernel(nroute, nterm, *refs):
     base_ref, out_ref = refs[nroute * nterm], refs[nroute * nterm + 1]
     parts = []
     for which in range(nroute):
-        total = refs[which * nterm][...].astype(F32)
-        for k in range(1, nterm):
-            total = total + refs[which * nterm + k][...].astype(F32)
+        total = 0.0
+        for ref in refs[which * nterm : (which + 1) * nterm]:
+            total = total + ref[0].astype(F32)
         parts.append(total)
     moved = jnp.concatenate(parts, axis=1)
     out_ref[...] = unit_rms(base_ref[...].astype(F32) + 8.0 * moved).astype(BF16)
 
 
-def call(kernel, outs, *args, scratch=(), vmem=16, where=pltpu.VMEM):
+def call(kernel, outs, *args, scratch=(), flops=0, vmem=16, where=pltpu.VMEM):
     shapes = [jax.ShapeDtypeStruct(s, d) for s, d in outs]
     size = sum(a.size * a.dtype.itemsize for a in args) + sum(s.size * s.dtype.itemsize for s in shapes)
     got = pl.pallas_call(
@@ -259,7 +265,7 @@
         out_specs=[pl.BlockSpec(memory_space=pltpu.VMEM)] * len(shapes),
         scratch_shapes=list(scratch),
         compiler_params=pltpu.CompilerParams(vmem_limit_bytes=vmem << 20),
-        cost_estimate=pl.CostEstimate(flops=0, bytes_accessed=0, transcendentals=0),
+        cost_estimate=pl.CostEstimate(flops=flops, bytes_accessed=0, transcendentals=0),
     )(*args)
     return got[0] if len(shapes) == 1 else got
 
@@ -297,6 +303,7 @@
     parents = parent_of.T
     table = [owner_of.reshape(1, -1), child_count.reshape(1, -1)]
     half_bit = groups // 2
+    far_mask = half_bit | half_bit >> 1
 
     ranges = pieces + [(s, s + wide) for s in starts]
     *ordered, parents, codes = call(
@@ -311,30 +318,32 @@
     )
     held, whole = ordered[: len(pieces)], ordered[len(pieces) :]
 
-    def place(chip, core, lo):
-        return (chip * CORES + core) * wide + lo - starts[chips - 1 - chip]
-
-    def weigh(rows, places, codes):
-        count = sum(r.shape[0] for r in rows)
+    def place(chip, core, lo, hi):
+        start = starts[chips - 1 - chip]
+        first, last = max(lo, start), min(hi, start + wide)
+        return (chip * CORES + core) * wide + first - start, first - lo, last - first
+
+    def weigh(rows, places, codes, flops=0):
+        count = sum(size for _, _, size in places)
         return call(
             functools.partial(weights_kernel, places, min(slots, 256)),
             [((count, slots), F32), ((1, slots), F32), ((count, width), BF16)], *rows, codes, cent,
-            scratch=[pltpu.VMEM((count, 1), I32), pltpu.VMEM((count, 1), I32)],
+            scratch=[pltpu.VMEM((count, 1), I32), pltpu.VMEM((count, 1), I32)], flops=flops * count,
         )
 
     near = [whole[-1]] + [swap(whole[chips - 1 - chip], "own", chip * CORES) for chip in range(1, chips)]
-    far_held = [swap(held[0], "pts", half_bit)]
+    far_held = [swap(held[0], "pts", far_mask)]
     codes = call(
         functools.partial(codes_kernel, chips, starts, tok, wide), [((1, owners * wide), F32)], parents, codes,
         vmem=4,
     )
     cent, base = call(cent_kernel, [((slots, width), BF16), ((share, width), BF16)], centroids[0])
 
-    far_codes = swap(codes, "pts", half_bit)
+    far_codes = swap(codes, "pts", far_mask)
 
     def weigh_near(chip, rows, codes):
         start = starts[chips - 1 - chip]
-        return weigh((rows, swap(rows, "own", 1)), [place(chip, c, start) for c in range(CORES)], codes)
+        return weigh((rows, swap(rows, "own", 1)), [place(chip, c, start, start + wide) for c in range(CORES)], codes)
 
     near_got = [weigh_near(0, near[0], codes)]
     first = near_got[0][1]
@@ -350,7 +359,7 @@
     def pair(chip, k, gate):
         rows = after(far_cross[chip, k] if chip else far_held[k], gate)
         for core, r in enumerate((rows, swap(rows, "own", 1))):
-            far[int(k == parts[chips - 1 - chip][-1])].append((r, place(chip, core, pieces[k][0])))
+            far[int(k == parts[chips - 1 - chip][-1])].append((r, place(chip, core, *pieces[k])))
 
     def weigh_far(late, gate):
         rows = far[late]
@@ -358,8 +367,8 @@
 
     far, far_cross = [[], []], {}
     partial = sum(near_s)
-    masks = powers(half_bit) + [half_bit | half_bit >> 1]
-    far_held.append(swap(after(held[1], first), "pts", half_bit))
+    masks = powers(groups)
+    far_held.append(swap(after(held[1], first), "pts", far_mask))
     forward(0, partial)
     sums = [partial]
     here = [far_cross[c, 0] for c in range(1, chips) if (c, 0) in far_cross]
@@ -368,21 +377,25 @@
     sums.append(sums[-1] + swap(after(sums[-1], here), "pts", masks[-1]))
     column = sums[-1]
     for piece in held[2:]:
-        far_held.append(swap(after(piece, first), "pts", half_bit))
+        far_held.append(swap(after(piece, first), "pts", far_mask))
     balance = call(functools.partial(balance_kernel, chips), [((1, slots), F32)], *near_w, column)
     steps = [balance]
-    for k, mask in enumerate(masks[:-1]):
-        balance = balance + swap(balance, "pts", mask)
-        steps.append(balance)
     for k in range(1, len(pieces)):
         forward(k, column)
     for chip in range(chips):
         mine = parts[chips - 1 - chip]
-        for k in mine:
-            pair(chip, k, steps[-1] if k == mine[-1] else steps[0])
-    far_got = [weigh_far(0, steps[1])]
-    balance = balance + swap(after(balance, far_got[0][0]), "pts", masks[-1])
+        for k in mine[:-1]:
+            pair(chip, k, column)
+    far_got = [weigh_far(0, steps[0])]
+    for k, mask in enumerate(masks[:-1]):
+        came = swap(balance, "pts", mask)
+        balance = balance + (after(came, far_got[0][0]) if mask == masks[-2] else came)
+        steps.append(balance)
+    for chip in range(chips):
+        pair(chip, parts[chips - 1 - chip][-1], steps[-1])
+    came = swap(balance, "pts", masks[-1])
     far_got.append(weigh_far(1, steps[-1]))
+    balance = balance + after(came, far_got[1][0])
     far_w, far_x = zip(*[(w, x) for w, _, x in far_got])
 
     bits = powers(half_bit)
@@ -392,33 +405,51 @@
     rows = [*near_x, *far_x]
     total_rows = sum(r.shape[0] for r in rows)
     part = pltpu.VMEM((max(share, LANES), cols), F32)
-    got = call(
-        functools.partial(send_kernel, [b[m:] for _, b in orders], half_bit, len(near_w) + len(far_w)),
-        [((m, share, cols), BF16)] * len(orders) + [((total_rows, slots // 2), BF16)],
+    def halves(blocks):
+        n = len(blocks) // 2
+        return [blocks[n:], blocks[:n]] if n else [blocks]
+
+    early, late = [], []
+    for r, (_, blocks) in enumerate(orders):
+        first, *rest = halves(blocks[m:])
+        early.append((r, first))
+        late += [(r, blocks) for blocks in rest]
+    kept = [(r, blocks[:m]) for r, (_, blocks) in enumerate(orders)]
+
+    def shapes(wanted, dtype):
+        return [((len(blocks), share, cols), dtype) for _, blocks in wanted]
+
+    *firsts, assign = call(
+        functools.partial(send_kernel, early, half_bit, len(near_w) + len(far_w)),
+        shapes(early, BF16) + [((total_rows, slots // 2), BF16)],
         *near_w, *far_w, balance, *rows, scratch=[part],
     )
-    sends, assign = got[:-1], got[-1]
-    keeps = call(
-        functools.partial(keep_kernel, [b[:m] for _, b in orders], half_bit),
-        [((m, share, cols), F32)] * len(orders), assign, *rows, scratch=[part],
-    )
-    keeps = list(keeps) if len(orders) > 1 else [keeps]
-    last = []
+    got = list(call(
+        functools.partial(keep_kernel, late + kept, half_bit), shapes(late, BF16) + shapes(kept, F32),
+        assign, *rows, scratch=[part],
+    ))
+    seconds, keeps = got[: len(late)], got[len(late) :]
+    terms = [[k] for k in keeps]
+    sends = [[f] + seconds[r : r + 1] for r, f in enumerate(firsts)]
     for step in range(len(bits)):
-        came = [swap(s, "pts", orders[r][0][step]) for r, s in enumerate(sends)]
-        n = came[0].shape[0] // 2
-        if n == 0:
-            last = came
-            break
-        sends = []
-        for r, c in enumerate(came):
-            keeps[r], send = call(
-                merge_kernel, [((n, share, cols), F32), ((n, share, cols), BF16)], keeps[r], c, vmem=8
+        for r, (order, _) in enumerate(orders):
+            came = [swap(a, "pts", order[step]) for a in sends[r]]
+            n = came[0].shape[0]
+            if len(came) == 1:
+                terms[r].append(came[0])
+                continue
+            sends[r] = call(
+                forward_kernel, [((max(n // 2, 1), share, cols), BF16)] * min(n, 2), keeps[r], came[0], vmem=8
             )
-            sends.append(send)
-    flat = [t.reshape(share, cols) for pair in zip(keeps, last) for t in pair]
+            sends[r] = list(sends[r]) if n > 1 else [sends[r]]
+            if n > 1:
+                keeps[r] = call(merge_kernel, [((n, share, cols), F32)], keeps[r], came[1], vmem=8)
+                terms[r] = [keeps[r]]
+            else:
+                terms[r].append(came[1])
+    flat = [t for route in terms for t in route]
     out = call(
-        functools.partial(final_kernel, len(orders), 2), [((share, width), BF16)], *flat, base, vmem=8
+        functools.partial(final_kernel, len(orders), len(terms[0])), [((share, width), BF16)], *flat, base, vmem=8
     )
     return out[None]
 

time: 85.7 us -> 77 us (0.90)
  waiting for transfers between devices: 32.8 us -> 21 us
  starting transfers between devices: 26.2 us -> 31.8 us
  Pallas kernels: 23 us -> 20.5 us
    ppermute x23 -> x25, waiting for transfers between devices: 32.8 us -> 21 us  [swap(): lax.ppermute(values, axis, [(i, i ^ bit) for i in range(lax.axis_size(axi...]
    ppermute x23 -> x25, starting transfers between devices: 26.2 us -> 31.8 us  [swap(): lax.ppermute(values, axis, [(i, i ^ bit) for i in range(lax.axis_size(axi...]
    pallas_call x13, Pallas kernels: 23 us -> 20.5 us  [call(): pl.pallas_call(kernel, out_shape=shapes, in_specs=[pl.BlockSpec(memory_sp...]
  transfers between devices with their start and end apart: 23 -> 25, of which waited for: 14 -> 10; matrix products, arithmetic and copies ran while one was open for 0% -> 0% of each run, Pallas kernels for 15% -> 19%
where the time goes in v5:
time: 77 us; the launch traced here: 76.7 us
  starting transfers between devices  31.8 us (41%)
  waiting for transfers between devices  21 us (27%)
  Pallas kernels  20.5 us (27%)
  local copies, waits for them, and re-layouts  3.2 us (4%)
    ppermute x25, starting transfers between devices, swap(): lax.ppermute(values, axis, [(i, i ^ bit) for i in range(lax.axis_size(axi...  31.8 us
    ppermute x25, waiting for transfers between devices, swap(): lax.ppermute(values, axis, [(i, i ^ bit) for i in range(lax.axis_size(axi...  21 us
    pallas_call x13, Pallas kernels, call(): pl.pallas_call(kernel, out_shape=shapes, in_specs=[pl.BlockSpec(memory_sp...  20.5 us
    unnamed x12, local copies, waits for them, and re-layouts  3.2 us
  transfers between devices with their start and end apart: 25, of which 10 were waited for; matrix products, arithmetic and copies ran while one was open for 0% of the time, Pallas kernels for 19%

profile of v5, /device:TPU:0, one launch (start us, length us, event | category | flops | bytes accessed | tf_op | source)
XLA Modules:
  0.0 76.7 jit_solution(6670018191247628297)
XLA Ops:
  0.0 3.2 %shard_map.55 = (bf16[64,1536]{1,0:T(8,128)(2,1)}, bf16[112,1536]{1,0:T(8,128)(2,1)}, bf16[80,1536]{1,0:T(8,128)(2,1)}, bf16[176,1536]{1,0:T(8,128)(2,1)}, bf16[...) custom-call(bf16[256,1536]{1,0:T(8,128)(2,1)} %refs_0_.1, s32[1,1024]{1,0:T(1,128)} %bitcast.6, ...), custom_call_target="tpu_custom_call" | custom-call | tf_op jit(solution)/shard_map/pallas_call | solution.py:261
  3.2 0.5 collective-permute-start
  3.7 2.6 %collective-permute-start.1 = (bf16[176,1536]{1,0:T(8,128)(2,1)}, bf16[176,1536]{1,0:T(8,128)(2,1)S(1)}, u32[]{:S(2)}, u32[]{:S(2)}) collective-permute-start(bf16[176,1536]{1,0:T(8,128)(2,1)} %get-tuple-element.49), channel_id=1, source_target_pairs={{0,2},{1,3},{2,0},{3,1},{4,6},{5,7},{6,4},{7,5},{8,10},{9,11},{10,... | collective-permute-start | bytes 1622024 | tf_op jit(solution)/shard_map/ppermute | solution.py:278
  6.3 3.6 %collective-permute-start.2 = (bf16[64,1536]{1,0:T(8,128)(2,1)}, bf16[64,1536]{1,0:T(8,128)(2,1)S(1)}, u32[]{:S(2)}, u32[]{:S(2)}) collective-permute-start(bf16[64,1536]{1,0:T(8,128)(2,1)} %get-tuple-element.51), channel_id=1, source_target_pairs={{0,24},{4,28},{8,16},{12,20},{16,8},{20,12},{24,0},{28,4},{1,25},{... | collective-permute-start | bytes 589832 | tf_op jit(solution)/shard_map/ppermute | solution.py:278
  9.9 0.7 copy-done.2
  10.6 0.6 copy-done.3
  11.2 1.4 %shard_map.56.refs_2_ = f32[1,704]{1,0:T(1,128)S(1)} custom-call(s32[1,1024]{1,0:T(1,128)S(1)} %copy-done.2, f32[1,64]{1,0:T(1,128)S(1)} %copy-done.3), custom_call_target="tpu_custom_call" | custom-call | tf_op jit(solution)/shard_map/pallas_call | solution.py:261
  12.6 0.3 collective-permute-start.3
  12.9 1.9 %copy-done = bf16[1,1024,1536]{2,1,0:T(8,128)(2,1)S(1)} copy-done((bf16[1,1024,1536]{2,1,0:T(8,128)(2,1)S(1)}, bf16[1,1024,1536]{2,1,0:T(8,128)(2,1)}, u32[]{:S(2)}) %copy-start) | copy-done | bytes 3145752
  14.8 1.0 %shard_map.57 = (bf16[1024,1536]{1,0:T(8,128)(2,1)S(1)}, bf16[128,1536]{1,0:T(8,128)(2,1)S(1)}) custom-call(bf16[1024,1536]{1,0:T(8,128)(2,1)S(1)} %bitcast.5), custom_call_target="tpu_custom_call" | custom-call | tf_op jit(solution)/shard_map/pallas_call | solution.py:261
  15.8 0.0 copy-done.1
  15.8 1.8 %shard_map.58 = (f32[352,1024]{1,0:T(8,128)S(1)}, f32[1,1024]{1,0:T(1,128)S(1)}, bf16[352,1536]{1,0:T(8,128)(2,1)S(1)}) custom-call(bf16[176,1536]{1,0:T(8,128)(2,1)S(1)} %copy-done.1, bf16[176,1536]{1,0:T(8,128)(2,1)S(1)} %collective-permute-done.refs_1_, f32[1,704]{1,0:T(1,128)S(1)} %shard_map.56.refs_2_, ...), custom_call_target="tpu_custom_call" | custom-call | tf_op jit(solution)/shard_map/pallas_call | solution.py:261
  17.7 0.5 collective-permute-done.3.refs_4_
  18.1 1.2 %collective-permute-done.1.refs_0_ = bf16[176,1536]{1,0:T(8,128)(2,1)S(1)} collective-permute-done((bf16[176,1536]{1,0:T(8,128)(2,1)}, bf16[176,1536]{1,0:T(8,128)(2,1)S(1)}, u32[]{:S(2)}, u32[]{:S(2)}) %collective-permute-start.1) | collective-permute-done | bytes 540704 | tf_op jit(solution)/shard_map/ppermute | solution.py:278
  19.4 3.9 %collective-permute-start.5 = (bf16[112,1536]{1,0:T(8,128)(2,1)S(1)}, bf16[112,1536]{1,0:T(8,128)(2,1)S(1)}, u32[]{:S(2)}, u32[]{:S(2)}) collective-permute-start(bf16[112,1536]{1,0:T(8,128)(2,1)S(1)} %copy-done.4), channel_id=1, source_target_pairs={{0,24},{4,28},{8,16},{12,20},{16,8},{20,12},{24,0},{28,4},{1,25},{... | collective-permute-start | bytes 1032200 | tf_op jit(solution)/shard_map/ppermute | solution.py:278
  23.3 1.8 %shard_map.59 = (f32[352,1024]{1,0:T(8,128)S(1)}, f32[1,1024]{1,0:T(1,128)S(1)}, bf16[352,1536]{1,0:T(8,128)(2,1)S(1)}) custom-call(bf16[176,1536]{1,0:T(8,128)(2,1)S(1)} %collective-permute-done.1.refs_0_, bf16[176,1536]{1,0:T(8,128)(2,1)S(1)} %collective-permute-done.4.refs_1_, f32[1,704]{1,0:T(1,128)S(1)} %shard_map.56.refs_2_, ...), custom_call_target="tpu_custom_call" | custom-call | tf_op jit(solution)/shard_map/pallas_call | solution.py:261
  25.2 1.6 %collective-permute-start.8 = (bf16[64,1536]{1,0:T(8,128)(2,1)S(1)}, bf16[64,1536]{1,0:T(8,128)(2,1)S(1)}, u32[]{:S(2)}, u32[]{:S(2)}) collective-permute-start(bf16[64,1536]{1,0:T(8,128)(2,1)S(1)} %collective-permute-done.2), channel_id=1, source_target_pairs={{0,2},{1,3},{2,0},{3,1},{4,6},{5,7},{6,4},{7,5},{8,10},{9,11},{10,... | collective-permute-start | bytes 589832 | tf_op jit(solution)/shard_map/ppermute | solution.py:278
  26.7 1.5 %collective-permute-start.6 = (f32[1,1024]{1,0:T(1,128)S(1)}, f32[1,1024]{1,0:T(1,128)S(1)}, u32[]{:S(2)}, u32[]{:S(2)}) collective-permute-start(f32[1,1024]{1,0:T(1,128)S(1)} %add.21), channel_id=1, source_target_pairs={{0,4},{4,0},{8,12},{12,8},{16,20},{20,16},{24,28},{28,24},{1,5},{5... | collective-permute-start | bytes 12296 | tf_op jit(solution)/shard_map/ppermute | solution.py:278
  28.2 2.1 %collective-permute-done.6 = f32[1,1024]{1,0:T(1,128)S(1)} collective-permute-done((f32[1,1024]{1,0:T(1,128)S(1)}, f32[1,1024]{1,0:T(1,128)S(1)}, u32[]{:S(2)}, u32[]{:S(2)}) %collective-permute-start.6) | collective-permute-done | bytes 4128 | tf_op jit(solution)/shard_map/ppermute | solution.py:278
  30.3 3.6 %collective-permute-done.7 = f32[1,1024]{1,0:T(1,128)S(1)} collective-permute-done((f32[1,1024]{1,0:T(1,128)S(1)}, f32[1,1024]{1,0:T(1,128)S(1)}, u32[]{:S(2)}, u32[]{:S(2)}) %collective-permute-start.7) | collective-permute-done | bytes 4128 | tf_op jit(solution)/shard_map/ppermute | solution.py:278
  33.9 0.9 %collective-permute-start.9 = (f32[1,1024]{1,0:T(1,128)S(1)}, f32[1,1024]{1,0:T(1,128)S(1)}, u32[]{:S(2)}, u32[]{:S(2)}) collective-permute-start(f32[1,1024]{1,0:T(1,128)S(1)} %add.23), channel_id=1, source_target_pairs={{0,16},{4,20},{8,24},{12,28},{16,0},{20,4},{24,8},{28,12},{1,17},{... | collective-permute-start | bytes 12296 | tf_op jit(solution)/shard_map/ppermute | solution.py:278
  34.9 3.8 %collective-permute-done.9 = f32[1,1024]{1,0:T(1,128)S(1)} collective-permute-done((f32[1,1024]{1,0:T(1,128)S(1)}, f32[1,1024]{1,0:T(1,128)S(1)}, u32[]{:S(2)}, u32[]{:S(2)}) %collective-permute-start.9) | collective-permute-done | bytes 4128 | tf_op jit(solution)/shard_map/ppermute | solution.py:278
  38.7 0.1 collective-permute-start.10
  38.8 1.6 %collective-permute-start.16 = (bf16[112,1536]{1,0:T(8,128)(2,1)S(1)}, bf16[112,1536]{1,0:T(8,128)(2,1)S(1)}, u32[]{:S(2)}, u32[]{:S(2)}) collective-permute-start(bf16[112,1536]{1,0:T(8,128)(2,1)S(1)} %collective-permute-done.5.refs_0_), channel_id=1, source_target_pairs={{0,2},{1,3},{2,0},{3,1},{4,6},{5,7},{6,4},{7,5},{8,10},{9,11},{10,... | collective-permute-start | bytes 1032200 | tf_op jit(solution)/shard_map/ppermute | solution.py:278
  40.3 0.2 collective-permute-start.11
  40.5 2.5 %collective-permute-start.12 = (bf16[80,1536]{1,0:T(8,128)(2,1)S(1)}, bf16[80,1536]{1,0:T(8,128)(2,1)S(1)}, u32[]{:S(2)}, u32[]{:S(2)}) collective-permute-start(bf16[80,1536]{1,0:T(8,128)(2,1)S(1)} %copy-done.5), channel_id=1, source_target_pairs={{0,24},{4,28},{8,16},{12,20},{16,8},{20,12},{24,0},{28,4},{1,25},{... | collective-permute-start | bytes 737288 | tf_op jit(solution)/shard_map/ppermute | solution.py:278
  43.0 0.6 shard_map.60
  43.6 1.6 %collective-permute-start.13 = (f32[1,1024]{1,0:T(1,128)S(1)}, f32[1,1024]{1,0:T(1,128)S(1)}, u32[]{:S(2)}, u32[]{:S(2)}) collective-permute-start(f32[1,1024]{1,0:T(1,128)S(1)} %shard_map.60), channel_id=1, source_target_pairs={{0,4},{4,0},{8,12},{12,8},{16,20},{20,16},{24,28},{28,24},{1,5},{5... | collective-permute-start | bytes 12296 | tf_op jit(solution)/shard_map/ppermute | solution.py:278
  45.1 2.1 %collective-permute-done.13 = f32[1,1024]{1,0:T(1,128)S(1)} collective-permute-done((f32[1,1024]{1,0:T(1,128)S(1)}, f32[1,1024]{1,0:T(1,128)S(1)}, u32[]{:S(2)}, u32[]{:S(2)}) %collective-permute-start.13) | collective-permute-done | bytes 4128 | tf_op jit(solution)/shard_map/ppermute | solution.py:278
  47.3 2.3 %shard_map.61 = (f32[320,1024]{1,0:T(8,128)S(1)}, f32[1,1024]{1,0:T(1,128)}, bf16[320,1536]{1,0:T(8,128)(2,1)S(1)}) custom-call(bf16[112,1536]{1,0:T(8,128)(2,1)S(1)} %collective-permute-done.5.refs_0_, bf16[112,1536]{1,0:T(8,128)(2,1)S(1)} %collective-permute-done.10.refs_1_, bf16[64,1536]{1,0:T(8,128)(2,1)S(1)} %collective-permute-done.8.refs_2_, ...), custom_call_target="tpu_custom_call" | custom-call | tf_op jit(solution)/shard_map/pallas_call | solution.py:261
  49.5 1.3 %collective-permute-done.14 = f32[1,1024]{1,0:T(1,128)S(1)} collective-permute-done((f32[1,1024]{1,0:T(1,128)S(1)}, f32[1,1024]{1,0:T(1,128)S(1)}, u32[]{:S(2)}, u32[]{:S(2)}) %collective-permute-start.14) | collective-permute-done | bytes 4128 | tf_op jit(solution)/shard_map/ppermute | solution.py:278
  50.9 0.1 collective-permute-start.17
  50.9 0.5 collective-permute-start.15
  51.4 3.9 %collective-permute-start.18 = (f32[1,1024]{1,0:T(1,128)S(1)}, f32[1,1024]{1,0:T(1,128)S(1)}, u32[]{:S(2)}, u32[]{:S(2)}) collective-permute-start(f32[1,1024]{1,0:T(1,128)S(1)} %add.26), channel_id=1, source_target_pairs={{0,16},{4,20},{8,24},{12,28},{16,0},{20,4},{24,8},{28,12},{1,17},{... | collective-permute-start | bytes 12296 | tf_op jit(solution)/shard_map/ppermute | solution.py:278
  55.4 2.5 %shard_map.62 = (f32[384,1024]{1,0:T(8,128)S(1)}, f32[1,1024]{1,0:T(1,128)}, bf16[384,1536]{1,0:T(8,128)(2,1)S(1)}) custom-call(bf16[80,1536]{1,0:T(8,128)(2,1)S(1)} %collective-permute-done.12.refs_0_, bf16[80,1536]{1,0:T(8,128)(2,1)S(1)} %collective-permute-done.15.refs_1_, bf16[112,1536]{1,0:T(8,128)(2,1)S(1)} %collective-permute-done.16.refs_2_, ...), custom_call_target="tpu_custom_call" | custom-call | tf_op jit(solution)/shard_map/pallas_call | solution.py:261
  57.9 2.0 %shard_map.63 = (bf16[1,128,768]{2,1,0:T(8,128)(2,1)S(1)}, bf16[1,128,768]{2,1,0:T(8,128)(2,1)S(1)}, bf16[1408,512]{1,0:T(8,128)(2,1)S(1)}) custom-call(f32[352,1024]{1,0:T(8,128)S(1)} %get-tuple-element.48.refs_0_, f32[352,1024]{1,0:T(8,128)S(1)} %get-tuple-element.53.refs_1_, f32[320,1024]{1,0:T(8,128)S(1)} %get-tuple-element.62.refs_2_, ...), custom_call_target="tpu_custom_call" | custom-call | tf_op jit(solution)/shard_map/pallas_call | solution.py:261
  59.9 1.0 %collective-permute-start.23 = (bf16[1,128,768]{2,1,0:T(8,128)(2,1)S(1)}, bf16[1,128,768]{2,1,0:T(8,128)(2,1)S(1)}, u32[]{:S(2)}, u32[]{:S(2)}) collective-permute-start(bf16[1,128,768]{2,1,0:T(8,128)(2,1)S(1)} %get-tuple-element.81), channel_id=1, source_target_pairs={{0,8},{4,12},{8,0},{12,4},{16,24},{20,28},{24,16},{28,20},{1,9},{5... | collective-permute-start | bytes 589832 | tf_op jit(solution)/shard_map/ppermute | solution.py:278
  60.9 1.5 %collective-permute-start.20 = (bf16[1,128,768]{2,1,0:T(8,128)(2,1)S(1)}, bf16[1,128,768]{2,1,0:T(8,128)(2,1)S(1)}, u32[]{:S(2)}, u32[]{:S(2)}) collective-permute-start(bf16[1,128,768]{2,1,0:T(8,128)(2,1)S(1)} %get-tuple-element.78), channel_id=1, source_target_pairs={{0,4},{4,0},{8,12},{12,8},{16,20},{20,16},{24,28},{28,24},{1,5},{5... | collective-permute-start | bytes 589832 | tf_op jit(solution)/shard_map/ppermute | solution.py:278
  62.5 2.7 %shard_map.64 = (bf16[1,128,768]{2,1,0:T(8,128)(2,1)S(1)}, bf16[1,128,768]{2,1,0:T(8,128)(2,1)S(1)}, f32[2,128,768]{2,1,0:T(8,128)S(1)}, f32[2,128,768]{2,1,0:T(8,128)S(1)}) custom-call(bf16[1408,512]{1,0:T(8,128)(2,1)S(1)} %get-tuple-element.75.refs_0_, bf16[352,1536]{1,0:T(8,128)(2,1)S(1)} %get-tuple-element.71.refs_5_.refs_1_, ...), custom_call_target="tpu_custom_call" | custom-call | tf_op jit(solution)/shard_map/pallas_call | solution.py:261
  65.2 0.6 collective-permute-start.19
  65.7 1.1 %collective-permute-start.22 = (bf16[1,128,768]{2,1,0:T(8,128)(2,1)S(1)}, bf16[1,128,768]{2,1,0:T(8,128)(2,1)S(1)}, u32[]{:S(2)}, u32[]{:S(2)}) collective-permute-start(bf16[1,128,768]{2,1,0:T(8,128)(2,1)S(1)} %get-tuple-element.80), channel_id=1, source_target_pairs={{0,8},{4,12},{8,0},{12,4},{16,24},{20,28},{24,16},{28,20},{1,9},{5... | collective-permute-start | bytes 589832 | tf_op jit(solution)/shard_map/ppermute | solution.py:278
  66.8 0.2 collective-permute-done.23.came_ref
  67.1 1.6 %collective-permute-start.24 = (bf16[1,128,768]{2,1,0:T(8,128)(2,1)S(1)}, bf16[1,128,768]{2,1,0:T(8,128)(2,1)S(1)}, u32[]{:S(2)}, u32[]{:S(2)}) collective-permute-start(bf16[1,128,768]{2,1,0:T(8,128)(2,1)S(1)} %shard_map.66), channel_id=1, source_target_pairs={{0,4},{4,0},{8,12},{12,8},{16,20},{20,16},{24,28},{28,24},{1,5},{5... | collective-permute-start | bytes 589832 | tf_op jit(solution)/shard_map/ppermute | solution.py:278
  68.8 0.8 %collective-permute-start.21 = (bf16[1,128,768]{2,1,0:T(8,128)(2,1)S(1)}, bf16[1,128,768]{2,1,0:T(8,128)(2,1)S(1)}, u32[]{:S(2)}, u32[]{:S(2)}) collective-permute-start(bf16[1,128,768]{2,1,0:T(8,128)(2,1)S(1)} %shard_map.65), channel_id=1, source_target_pairs={{0,8},{4,12},{8,0},{12,4},{16,24},{20,28},{24,16},{28,20},{1,9},{5... | collective-permute-start | bytes 589832 | tf_op jit(solution)/shard_map/ppermute | solution.py:278
  69.5 3.5 %collective-permute-done.19.refs_1_ = bf16[1,128,768]{2,1,0:T(8,128)(2,1)S(1)} collective-permute-done((bf16[1,128,768]{2,1,0:T(8,128)(2,1)S(1)}, bf16[1,128,768]{2,1,0:T(8,128)(2,1)S(1)}, u32[]{:S(2)}, u32[]{:S(2)}) %collective-permute-start.19) | collective-permute-done | bytes 196640 | tf_op jit(solution)/shard_map/ppermute | solution.py:278
  73.1 2.5 %collective-permute-done.24.refs_5_ = bf16[1,128,768]{2,1,0:T(8,128)(2,1)S(1)} collective-permute-done((bf16[1,128,768]{2,1,0:T(8,128)(2,1)S(1)}, bf16[1,128,768]{2,1,0:T(8,128)(2,1)S(1)}, u32[]{:S(2)}, u32[]{:S(2)}) %collective-permute-start.24) | collective-permute-done | bytes 196640 | tf_op jit(solution)/shard_map/ppermute | solution.py:278
  75.6 0.0 collective-permute-done.21.refs_2_
  75.6 1.1 %shard_map.67 = bf16[128,1536]{1,0:T(8,128)(2,1)} custom-call(f32[2,128,768]{2,1,0:T(8,128)S(1)} %get-tuple-element.76.keep_ref.refs_0_, bf16[1,128,768]{2,1,0:T(8,128)(2,1)S(1)} %collective-permute-done.19.refs_1_, bf16[1,128,768]{2,1,0:T(8,128)(2,1)S(1)} %collective-permute-done.21.refs_2_, f32[2,128,768]{2,1,0:T(8,128)S(1)} %get-tuple-element.79.keep_ref.refs_3_, ...), custom_call_target="tpu_custom_call" | custom-call | tf_op jit(solution)/shard_map/pallas_call | solution.py:261
  (34 shorter events, 0.2 us)
Async XLA Ops:
  3.2 12.6 %collective-permute-start = (bf16[176,1536]{1,0:T(8,128)(2,1)}, bf16[176,1536]{1,0:T(8,128)(2,1)S(1)}, u32[]{:S(2)}, u32[]{:S(2)}) collective-permute-start(bf16[176,1536]{1,0:T(8,128)(2,1)} %get-tuple-element.44.refs_0_), channel_id=1, source_target_pairs={{0,1},{1,0},{2,3},{3,2},{4,5},{5,4},{6,7},{7,6},{8,9},{9,8},{10,11... | collective-permute-start | bytes 1622024 | tf_op jit(solution)/shard_map/ppermute | solution.py:278
  3.7 15.6 %collective-permute-start.1 = (bf16[176,1536]{1,0:T(8,128)(2,1)}, bf16[176,1536]{1,0:T(8,128)(2,1)S(1)}, u32[]{:S(2)}, u32[]{:S(2)}) collective-permute-start(bf16[176,1536]{1,0:T(8,128)(2,1)} %get-tuple-element.49), channel_id=1, source_target_pairs={{0,2},{1,3},{2,0},{3,1},{4,6},{5,7},{6,4},{7,5},{8,10},{9,11},{10,... | collective-permute-start | bytes 1622024 | tf_op jit(solution)/shard_map/ppermute | solution.py:278
  6.3 11.8 %collective-permute-start.2 = (bf16[64,1536]{1,0:T(8,128)(2,1)}, bf16[64,1536]{1,0:T(8,128)(2,1)S(1)}, u32[]{:S(2)}, u32[]{:S(2)}) collective-permute-start(bf16[64,1536]{1,0:T(8,128)(2,1)} %get-tuple-element.51), channel_id=1, source_target_pairs={{0,24},{4,28},{8,16},{12,20},{16,8},{20,12},{24,0},{28,4},{1,25},{... | collective-permute-start | bytes 589832 | tf_op jit(solution)/shard_map/ppermute | solution.py:278
  9.9 0.7 copy-start.2
  10.6 0.6 copy-start.3
  12.6 5.6 %collective-permute-start.3 = (f32[1,704]{1,0:T(1,128)S(1)}, f32[1,704]{1,0:T(1,128)S(1)}, u32[]{:S(2)}, u32[]{:S(2)}) collective-permute-start(f32[1,704]{1,0:T(1,128)S(1)} %shard_map.56.refs_2_), channel_id=1, source_target_pairs={{0,24},{4,28},{8,16},{12,20},{16,8},{20,12},{24,0},{28,4},{1,25},{... | collective-permute-start | bytes 8456 | tf_op jit(solution)/shard_map/ppermute | solution.py:278
  12.9 1.9 %copy-start = (bf16[1,1024,1536]{2,1,0:T(8,128)(2,1)S(1)}, bf16[1,1024,1536]{2,1,0:T(8,128)(2,1)}, u32[]{:S(2)}) copy-start(bf16[1,1024,1536]{2,1,0:T(8,128)(2,1)} %param.9) | copy-start | bytes 9437188
  14.8 1.0 %copy-start.1 = (bf16[176,1536]{1,0:T(8,128)(2,1)S(1)}, bf16[176,1536]{1,0:T(8,128)(2,1)}, u32[]{:S(2)}) copy-start(bf16[176,1536]{1,0:T(8,128)(2,1)} %get-tuple-element.44.refs_0_) | copy-start | bytes 1622020
  15.8 3.6 %copy-start.4 = (bf16[112,1536]{1,0:T(8,128)(2,1)S(1)}, bf16[112,1536]{1,0:T(8,128)(2,1)}, u32[]{:S(2)}) copy-start(bf16[112,1536]{1,0:T(8,128)(2,1)} %get-tuple-element.55) | copy-start | bytes 1032196
  19.4 3.9 %collective-permute-start.4 = (bf16[176,1536]{1,0:T(8,128)(2,1)S(1)}, bf16[176,1536]{1,0:T(8,128)(2,1)S(1)}, u32[]{:S(2)}, u32[]{:S(2)}) collective-permute-start(bf16[176,1536]{1,0:T(8,128)(2,1)S(1)} %collective-permute-done.1.refs_0_), channel_id=1, source_target_pairs={{0,1},{1,0},{2,3},{3,2},{4,5},{5,4},{6,7},{7,6},{8,9},{9,8},{10,11... | collective-permute-start | bytes 1622024 | tf_op jit(solution)/shard_map/ppermute | solution.py:278
  19.4 21.1 %copy-start.5 = (bf16[80,1536]{1,0:T(8,128)(2,1)S(1)}, bf16[80,1536]{1,0:T(8,128)(2,1)}, u32[]{:S(2)}) copy-start(bf16[80,1536]{1,0:T(8,128)(2,1)} %get-tuple-element.64) | copy-start | bytes 737284
  19.4 19.3 %collective-permute-start.5 = (bf16[112,1536]{1,0:T(8,128)(2,1)S(1)}, bf16[112,1536]{1,0:T(8,128)(2,1)S(1)}, u32[]{:S(2)}, u32[]{:S(2)}) collective-permute-start(bf16[112,1536]{1,0:T(8,128)(2,1)S(1)} %copy-done.4), channel_id=1, source_target_pairs={{0,24},{4,28},{8,16},{12,20},{16,8},{20,12},{24,0},{28,4},{1,25},{... | collective-permute-start | bytes 1032200 | tf_op jit(solution)/shard_map/ppermute | solution.py:278
  25.2 8.8 %collective-permute-start.8 = (bf16[64,1536]{1,0:T(8,128)(2,1)S(1)}, bf16[64,1536]{1,0:T(8,128)(2,1)S(1)}, u32[]{:S(2)}, u32[]{:S(2)}) collective-permute-start(bf16[64,1536]{1,0:T(8,128)(2,1)S(1)} %collective-permute-done.2), channel_id=1, source_target_pairs={{0,2},{1,3},{2,0},{3,1},{4,6},{5,7},{6,4},{7,5},{8,10},{9,11},{10,... | collective-permute-start | bytes 589832 | tf_op jit(solution)/shard_map/ppermute | solution.py:278
  26.7 3.6 %collective-permute-start.6 = (f32[1,1024]{1,0:T(1,128)S(1)}, f32[1,1024]{1,0:T(1,128)S(1)}, u32[]{:S(2)}, u32[]{:S(2)}) collective-permute-start(f32[1,1024]{1,0:T(1,128)S(1)} %add.21), channel_id=1, source_target_pairs={{0,4},{4,0},{8,12},{12,8},{16,20},{20,16},{24,28},{28,24},{1,5},{5... | collective-permute-start | bytes 12296 | tf_op jit(solution)/shard_map/ppermute | solution.py:278
  30.3 3.6 %collective-permute-start.7 = (f32[1,1024]{1,0:T(1,128)S(1)}, f32[1,1024]{1,0:T(1,128)S(1)}, u32[]{:S(2)}, u32[]{:S(2)}) collective-permute-start(f32[1,1024]{1,0:T(1,128)S(1)} %add.22), channel_id=1, source_target_pairs={{0,8},{4,12},{8,0},{12,4},{16,24},{20,28},{24,16},{28,20},{1,9},{5... | collective-permute-start | bytes 12296 | tf_op jit(solution)/shard_map/ppermute | solution.py:278
  33.9 4.7 %collective-permute-start.9 = (f32[1,1024]{1,0:T(1,128)S(1)}, f32[1,1024]{1,0:T(1,128)S(1)}, u32[]{:S(2)}, u32[]{:S(2)}) collective-permute-start(f32[1,1024]{1,0:T(1,128)S(1)} %add.23), channel_id=1, source_target_pairs={{0,16},{4,20},{8,24},{12,28},{16,0},{20,4},{24,8},{28,12},{1,17},{... | collective-permute-start | bytes 12296 | tf_op jit(solution)/shard_map/ppermute | solution.py:278
  38.7 8.6 %collective-permute-start.10 = (bf16[112,1536]{1,0:T(8,128)(2,1)S(1)}, bf16[112,1536]{1,0:T(8,128)(2,1)S(1)}, u32[]{:S(2)}, u32[]{:S(2)}) collective-permute-start(bf16[112,1536]{1,0:T(8,128)(2,1)S(1)} %collective-permute-done.5.refs_0_), channel_id=1, source_target_pairs={{0,1},{1,0},{2,3},{3,2},{4,5},{5,4},{6,7},{7,6},{8,9},{9,8},{10,11... | collective-permute-start | bytes 1032200 | tf_op jit(solution)/shard_map/ppermute | solution.py:278
  38.8 12.1 %collective-permute-start.16 = (bf16[112,1536]{1,0:T(8,128)(2,1)S(1)}, bf16[112,1536]{1,0:T(8,128)(2,1)S(1)}, u32[]{:S(2)}, u32[]{:S(2)}) collective-permute-start(bf16[112,1536]{1,0:T(8,128)(2,1)S(1)} %collective-permute-done.5.refs_0_), channel_id=1, source_target_pairs={{0,2},{1,3},{2,0},{3,1},{4,6},{5,7},{6,4},{7,5},{8,10},{9,11},{10,... | collective-permute-start | bytes 1032200 | tf_op jit(solution)/shard_map/ppermute | solution.py:278
  40.3 6.9 %collective-permute-start.11 = (bf16[64,1536]{1,0:T(8,128)(2,1)S(1)}, bf16[64,1536]{1,0:T(8,128)(2,1)S(1)}, u32[]{:S(2)}, u32[]{:S(2)}) collective-permute-start(bf16[64,1536]{1,0:T(8,128)(2,1)S(1)} %collective-permute-done.8.refs_2_), channel_id=1, source_target_pairs={{0,1},{1,0},{2,3},{3,2},{4,5},{5,4},{6,7},{7,6},{8,9},{9,8},{10,11... | collective-permute-start | bytes 589832 | tf_op jit(solution)/shard_map/ppermute | solution.py:278
  40.5 10.4 %collective-permute-start.12 = (bf16[80,1536]{1,0:T(8,128)(2,1)S(1)}, bf16[80,1536]{1,0:T(8,128)(2,1)S(1)}, u32[]{:S(2)}, u32[]{:S(2)}) collective-permute-start(bf16[80,1536]{1,0:T(8,128)(2,1)S(1)} %copy-done.5), channel_id=1, source_target_pairs={{0,24},{4,28},{8,16},{12,20},{16,8},{20,12},{24,0},{28,4},{1,25},{... | collective-permute-start | bytes 737288 | tf_op jit(solution)/shard_map/ppermute | solution.py:278
  43.6 3.7 %collective-permute-start.13 = (f32[1,1024]{1,0:T(1,128)S(1)}, f32[1,1024]{1,0:T(1,128)S(1)}, u32[]{:S(2)}, u32[]{:S(2)}) collective-permute-start(f32[1,1024]{1,0:T(1,128)S(1)} %shard_map.60), channel_id=1, source_target_pairs={{0,4},{4,0},{8,12},{12,8},{16,20},{20,16},{24,28},{28,24},{1,5},{5... | collective-permute-start | bytes 12296 | tf_op jit(solution)/shard_map/ppermute | solution.py:278
  47.2 3.6 %collective-permute-start.14 = (f32[1,1024]{1,0:T(1,128)S(1)}, f32[1,1024]{1,0:T(1,128)S(1)}, u32[]{:S(2)}, u32[]{:S(2)}) collective-permute-start(f32[1,1024]{1,0:T(1,128)S(1)} %add.25), channel_id=1, source_target_pairs={{0,8},{4,12},{8,0},{12,4},{16,24},{20,28},{24,16},{28,20},{1,9},{5... | collective-permute-start | bytes 12296 | tf_op jit(solution)/shard_map/ppermute | solution.py:278
  50.9 4.5 %collective-permute-start.17 = (bf16[112,1536]{1,0:T(8,128)(2,1)S(1)}, bf16[112,1536]{1,0:T(8,128)(2,1)S(1)}, u32[]{:S(2)}, u32[]{:S(2)}) collective-permute-start(bf16[112,1536]{1,0:T(8,128)(2,1)S(1)} %collective-permute-done.16.refs_2_), channel_id=1, source_target_pairs={{0,1},{1,0},{2,3},{3,2},{4,5},{5,4},{6,7},{7,6},{8,9},{9,8},{10,11... | collective-permute-start | bytes 1032200 | tf_op jit(solution)/shard_map/ppermute | solution.py:278
  50.9 4.4 %collective-permute-start.15 = (bf16[80,1536]{1,0:T(8,128)(2,1)S(1)}, bf16[80,1536]{1,0:T(8,128)(2,1)S(1)}, u32[]{:S(2)}, u32[]{:S(2)}) collective-permute-start(bf16[80,1536]{1,0:T(8,128)(2,1)S(1)} %collective-permute-done.12.refs_0_), channel_id=1, source_target_pairs={{0,1},{1,0},{2,3},{3,2},{4,5},{5,4},{6,7},{7,6},{8,9},{9,8},{10,11... | collective-permute-start | bytes 737288 | tf_op jit(solution)/shard_map/ppermute | solution.py:278
  51.4 6.5 %collective-permute-start.18 = (f32[1,1024]{1,0:T(1,128)S(1)}, f32[1,1024]{1,0:T(1,128)S(1)}, u32[]{:S(2)}, u32[]{:S(2)}) collective-permute-start(f32[1,1024]{1,0:T(1,128)S(1)} %add.26), channel_id=1, source_target_pairs={{0,16},{4,20},{8,24},{12,28},{16,0},{20,4},{24,8},{28,12},{1,17},{... | collective-permute-start | bytes 12296 | tf_op jit(solution)/shard_map/ppermute | solution.py:278
  59.9 7.1 %collective-permute-start.23 = (bf16[1,128,768]{2,1,0:T(8,128)(2,1)S(1)}, bf16[1,128,768]{2,1,0:T(8,128)(2,1)S(1)}, u32[]{:S(2)}, u32[]{:S(2)}) collective-permute-start(bf16[1,128,768]{2,1,0:T(8,128)(2,1)S(1)} %get-tuple-element.81), channel_id=1, source_target_pairs={{0,8},{4,12},{8,0},{12,4},{16,24},{20,28},{24,16},{28,20},{1,9},{5... | collective-permute-start | bytes 589832 | tf_op jit(solution)/shard_map/ppermute | solution.py:278
  60.9 7.7 %collective-permute-start.20 = (bf16[1,128,768]{2,1,0:T(8,128)(2,1)S(1)}, bf16[1,128,768]{2,1,0:T(8,128)(2,1)S(1)}, u32[]{:S(2)}, u32[]{:S(2)}) collective-permute-start(bf16[1,128,768]{2,1,0:T(8,128)(2,1)S(1)} %get-tuple-element.78), channel_id=1, source_target_pairs={{0,4},{4,0},{8,12},{12,8},{16,20},{20,16},{24,28},{28,24},{1,5},{5... | collective-permute-start | bytes 589832 | tf_op jit(solution)/shard_map/ppermute | solution.py:278
  65.2 7.9 %collective-permute-start.19 = (bf16[1,128,768]{2,1,0:T(8,128)(2,1)S(1)}, bf16[1,128,768]{2,1,0:T(8,128)(2,1)S(1)}, u32[]{:S(2)}, u32[]{:S(2)}) collective-permute-start(bf16[1,128,768]{2,1,0:T(8,128)(2,1)S(1)} %get-tuple-element.77), channel_id=1, source_target_pairs={{0,4},{4,0},{8,12},{12,8},{16,20},{20,16},{24,28},{28,24},{1,5},{5... | collective-permute-start | bytes 589832 | tf_op jit(solution)/shard_map/ppermute | solution.py:278
  65.7 7.3 %collective-permute-start.22 = (bf16[1,128,768]{2,1,0:T(8,128)(2,1)S(1)}, bf16[1,128,768]{2,1,0:T(8,128)(2,1)S(1)}, u32[]{:S(2)}, u32[]{:S(2)}) collective-permute-start(bf16[1,128,768]{2,1,0:T(8,128)(2,1)S(1)} %get-tuple-element.80), channel_id=1, source_target_pairs={{0,8},{4,12},{8,0},{12,4},{16,24},{20,28},{24,16},{28,20},{1,9},{5... | collective-permute-start | bytes 589832 | tf_op jit(solution)/shard_map/ppermute | solution.py:278
  67.1 8.5 %collective-permute-start.24 = (bf16[1,128,768]{2,1,0:T(8,128)(2,1)S(1)}, bf16[1,128,768]{2,1,0:T(8,128)(2,1)S(1)}, u32[]{:S(2)}, u32[]{:S(2)}) collective-permute-start(bf16[1,128,768]{2,1,0:T(8,128)(2,1)S(1)} %shard_map.66), channel_id=1, source_target_pairs={{0,4},{4,0},{8,12},{12,8},{16,20},{20,16},{24,28},{28,24},{1,5},{5... | collective-permute-start | bytes 589832 | tf_op jit(solution)/shard_map/ppermute | solution.py:278
  68.8 6.9 %collective-permute-start.21 = (bf16[1,128,768]{2,1,0:T(8,128)(2,1)S(1)}, bf16[1,128,768]{2,1,0:T(8,128)(2,1)S(1)}, u32[]{:S(2)}, u32[]{:S(2)}) collective-permute-start(bf16[1,128,768]{2,1,0:T(8,128)(2,1)S(1)} %shard_map.65), channel_id=1, source_target_pairs={{0,8},{4,12},{8,0},{12,4},{16,24},{20,28},{24,16},{28,20},{1,9},{5... | collective-permute-start | bytes 589832 | tf_op jit(solution)/shard_map/ppermute | solution.py:278

commit v6 on v5

--- a/solution.py
+++ b/solution.py
@@ -132,16 +132,13 @@
     base_ref[...] = out_ref[pl.ds(pl.multiple_of(lax.axis_index("pts") * share, share), share), :]
 
 
-def weights_kernel(places, tile, *refs):
-    row_refs, (codes_ref, cent_ref, w_ref, sum_ref, rows_ref, low_ref, high_ref) = refs[:-7], refs[-7:]
+def bounds_kernel(places, slots, codes_ref, low_ref, high_ref):
     me = lax.axis_index("own")
-    slots, width = cent_ref.shape
     total = codes_ref.shape[1]
     at = 0
-    for row_ref, (place, skip, size) in zip(row_refs, places):
+    for place, _, size in places:
         part = slice(at, at + size)
         at += size
-        rows_ref[part, :] = row_ref[skip : skip + size, :]
         hit = iota((size, total), 1) == iota((size, total), 0) + place
         code = jnp.sum(jnp.where(hit, codes_ref[...], 0.0), axis=1, keepdims=True).astype(I32)
         first = (code % OWNER_SHIFT) // FIRST_SHIFT
@@ -149,18 +146,39 @@
         low_ref[part, :] = low
         high_ref[part, :] = low + code % FIRST_SHIFT
 
+
+def coded_kernel(places, tile, half_bit, *refs):
+    codes_ref, cent_ref, low_ref, high_ref = refs[-7], refs[-6], refs[-2], refs[-1]
+    bounds_kernel(places, cent_ref.shape[0], codes_ref, low_ref, high_ref)
+    weights_kernel(places, tile, half_bit, *refs[:-7], low_ref, high_ref, *refs[-6:-2])
+
+
+def weights_kernel(places, tile, half_bit, *refs):
+    row_refs, (low_ref, high_ref, cent_ref, w_ref, sum_ref, rows_ref) = refs[:-6], refs[-6:]
+    slots, width = cent_ref.shape
+    at = 0
+    for row_ref, (_, skip, size) in zip(row_refs, places):
+        rows_ref[at : at + size, :] = row_ref[skip : skip + size, :]
+        at += size
+    span = w_ref.shape[1]
+    base = span_start(half_bit, slots, span)
+
     def step(i, carry):
         at = pl.multiple_of(i * tile, tile)
-        cent = cent_ref[pl.ds(at, tile), :]
+        cent = cent_ref[pl.ds(pl.multiple_of(base + at, LANES), tile), :]
         scores = lax.dot_general(rows_ref[...], cent, (((1,), (1,)), ((), ())), preferred_element_type=F32)
-        slot = iota(scores.shape, 1) + at
+        slot = iota(scores.shape, 1) + (base + at)
         live = (slot >= low_ref[...]) & (slot < high_ref[...])
         w = jnp.where(live, jnp.exp(scores * (1.0 / (width * 0.05))), 0.0)
         w_ref[:, pl.ds(at, tile)] = w
         sum_ref[:, pl.ds(at, tile)] = jnp.sum(w, axis=0, keepdims=True)
         return carry
 
-    lax.fori_loop(0, slots // tile, step, 0, unroll=True)
+    lax.fori_loop(0, span // tile, step, 0, unroll=True)
+
+
+def span_start(half_bit, slots, span):
+    return (lax.axis_index("pts") // half_bit) % 2 * (slots - span)
 
 
 def inverse(values):
@@ -182,15 +200,18 @@
 
 def assign_kernel(half_bit, *refs):
     w_refs, (t_ref, assign_ref) = refs[:-2], refs[-2:]
-    scale = inverse(t_ref[...])
-    half = assign_ref.shape[1]
+    slots, half = t_ref.shape[1], assign_ref.shape[1]
     upper = (lax.axis_index("pts") // half_bit) % 2
+    part = inverse(t_ref[:, pl.ds(pl.multiple_of(upper * half, half), half)])
     at = 0
     for w_ref in w_refs:
+        span = w_ref.shape[1]
+        base = span_start(half_bit, slots, span)
+        scale = inverse(t_ref[:, pl.ds(pl.multiple_of(base, LANES), span)])
+        columns = pl.ds(pl.multiple_of(upper * (span - half), LANES), half)
         for lo in range(0, w_ref.shape[0], ROWS * 2):
-            w = w_ref[lo : lo + ROWS * 2, :] * scale
-            row = inverse(jnp.sum(w, axis=1, keepdims=True))
-            mine = jnp.where(upper == 0, w[:, :half], w[:, half:])
+            row = inverse(jnp.sum(w_ref[lo : lo + ROWS * 2, :] * scale, axis=1, keepdims=True))
+            mine = w_ref[lo : lo + ROWS * 2, columns] * part
             assign_ref[at : at + ROWS * 2, :] = (mine * row).astype(BF16)
             at += ROWS * 2
 
@@ -323,12 +344,13 @@
         first, last = max(lo, start), min(hi, start + wide)
         return (chip * CORES + core) * wide + first - start, first - lo, last - first
 
-    def weigh(rows, places, codes, flops=0):
+    def weigh(rows, places, codes, span=slots, bounds=None):
         count = sum(size for _, _, size in places)
+        column = pltpu.VMEM((count, 1), I32)
         return call(
-            functools.partial(weights_kernel, places, min(slots, 256)),
-            [((count, slots), F32), ((1, slots), F32), ((count, width), BF16)], *rows, codes, cent,
-            scratch=[pltpu.VMEM((count, 1), I32), pltpu.VMEM((count, 1), I32)], flops=flops * count,
+            functools.partial(weights_kernel if bounds else coded_kernel, places, 256 if span % 256 == 0 else span, half_bit),
+            [((count, span), F32), ((1, span), F32), ((count, width), BF16)],
+            *rows, *(bounds or [codes]), cent, scratch=[] if bounds else [column, column],
         )
 
     near = [whole[-1]] + [swap(whole[chips - 1 - chip], "own", chip * CORES) for chip in range(1, chips)]
@@ -361,9 +383,9 @@
         for core, r in enumerate((rows, swap(rows, "own", 1))):
             far[int(k == parts[chips - 1 - chip][-1])].append((r, place(chip, core, *pieces[k])))
 
-    def weigh_far(late, gate):
-        rows = far[late]
-        return weigh([r for r, _ in rows], [p for _, p in rows], after(far_codes, gate))
+    def weigh_far(late, gate, bounds=None):
+        rows, places = zip(*far[late])
+        return weigh(rows, places, after(far_codes, gate), min(slots // 2 + LANES, slots), bounds)
 
     far, far_cross = [[], []], {}
     partial = sum(near_s)
@@ -386,7 +408,12 @@
         mine = parts[chips - 1 - chip]
         for k in mine[:-1]:
             pair(chip, k, column)
-    far_got = [weigh_far(0, steps[0])]
+    late = [place(chip, c, *pieces[parts[chips - 1 - chip][-1]]) for chip in range(chips) for c in range(CORES)]
+    count = sum(size for _, _, size in late)
+    bounds = call(
+        functools.partial(bounds_kernel, late, slots), [((count, 1), I32)] * 2, after(far_codes, steps[0]), vmem=4
+    )
+    far_got = [weigh_far(0, bounds[0])]
     for k, mask in enumerate(masks[:-1]):
         came = swap(balance, "pts", mask)
         balance = balance + (after(came, far_got[0][0]) if mask == masks[-2] else came)
@@ -394,7 +421,7 @@
     for chip in range(chips):
         pair(chip, parts[chips - 1 - chip][-1], steps[-1])
     came = swap(balance, "pts", masks[-1])
-    far_got.append(weigh_far(1, steps[-1]))
+    far_got.append(weigh_far(1, steps[-1], list(bounds)))
     balance = balance + after(came, far_got[1][0])
     far_w, far_x = zip(*[(w, x) for w, _, x in far_got])
 

time: 77 us -> 76.9 us (level)
    pallas_call x13 -> x14, Pallas kernels: 20.5 us -> 19.8 us  [call(): pl.pallas_call(kernel, out_shape=shapes, in_specs=[pl.BlockSpec(memory_sp...]
  transfers between devices with their start and end apart: 25 -> 25, of which waited for: 10 -> 12; matrix products, arithmetic and copies ran while one was open for 0% -> 0% of each run, Pallas kernels for 19% -> 18%
where the time goes in v6:
time: 76.9 us; the launch traced here: 76.6 us
  starting transfers between devices  32.5 us (42%)
  waiting for transfers between devices  20.9 us (27%)
  Pallas kernels  19.8 us (26%)
  local copies, waits for them, and re-layouts  3.18 us (4%)
    ppermute x25, starting transfers between devices, swap(): lax.ppermute(values, axis, [(i, i ^ bit) for i in range(lax.axis_size(axi...  32.5 us
    ppermute x25, waiting for transfers between devices, swap(): lax.ppermute(values, axis, [(i, i ^ bit) for i in range(lax.axis_size(axi...  20.9 us
    pallas_call x14, Pallas kernels, call(): pl.pallas_call(kernel, out_shape=shapes, in_specs=[pl.BlockSpec(memory_sp...  19.8 us
    unnamed x12, local copies, waits for them, and re-layouts  3.18 us
  transfers between devices with their start and end apart: 25, of which 12 were waited for; matrix products, arithmetic and copies ran while one was open for 0% of the time, Pallas kernels for 18%

profile of v6, /device:TPU:0, one launch (start us, length us, event | category | flops | bytes accessed | tf_op | source)
XLA Modules:
  0.0 76.6 jit_solution(5841763021665602892)
XLA Ops:
  0.0 3.2 %shard_map.55 = (bf16[64,1536]{1,0:T(8,128)(2,1)}, bf16[112,1536]{1,0:T(8,128)(2,1)}, bf16[80,1536]{1,0:T(8,128)(2,1)}, bf16[176,1536]{1,0:T(8,128)(2,1)}, bf16[...) custom-call(bf16[256,1536]{1,0:T(8,128)(2,1)} %refs_0_.1, s32[1,1024]{1,0:T(1,128)} %bitcast.6, ...), custom_call_target="tpu_custom_call" | custom-call | tf_op jit(solution)/shard_map/pallas_call | solution.py:282
  3.2 0.5 collective-permute-start
  3.8 2.6 %collective-permute-start.1 = (bf16[176,1536]{1,0:T(8,128)(2,1)}, bf16[176,1536]{1,0:T(8,128)(2,1)S(1)}, u32[]{:S(2)}, u32[]{:S(2)}) collective-permute-start(bf16[176,1536]{1,0:T(8,128)(2,1)} %get-tuple-element.51), channel_id=1, source_target_pairs={{0,2},{1,3},{2,0},{3,1},{4,6},{5,7},{6,4},{7,5},{8,10},{9,11},{10,... | collective-permute-start | bytes 1622024 | tf_op jit(solution)/shard_map/ppermute | solution.py:299
  6.3 3.6 %collective-permute-start.2 = (bf16[64,1536]{1,0:T(8,128)(2,1)}, bf16[64,1536]{1,0:T(8,128)(2,1)S(1)}, u32[]{:S(2)}, u32[]{:S(2)}) collective-permute-start(bf16[64,1536]{1,0:T(8,128)(2,1)} %get-tuple-element.53), channel_id=1, source_target_pairs={{0,24},{4,28},{8,16},{12,20},{16,8},{20,12},{24,0},{28,4},{1,25},{... | collective-permute-start | bytes 589832 | tf_op jit(solution)/shard_map/ppermute | solution.py:299
  9.9 0.7 copy-done.2
  10.6 0.6 copy-done.3
  11.2 1.4 %shard_map.56.refs_2_ = f32[1,704]{1,0:T(1,128)S(1)} custom-call(s32[1,1024]{1,0:T(1,128)S(1)} %copy-done.2, f32[1,64]{1,0:T(1,128)S(1)} %copy-done.3), custom_call_target="tpu_custom_call" | custom-call | tf_op jit(solution)/shard_map/pallas_call | solution.py:282
  12.6 0.3 collective-permute-start.3
  12.9 1.9 %copy-done = bf16[1,1024,1536]{2,1,0:T(8,128)(2,1)S(1)} copy-done((bf16[1,1024,1536]{2,1,0:T(8,128)(2,1)S(1)}, bf16[1,1024,1536]{2,1,0:T(8,128)(2,1)}, u32[]{:S(2)}) %copy-start) | copy-done | bytes 3145752
  14.8 1.0 %shard_map.57 = (bf16[1024,1536]{1,0:T(8,128)(2,1)S(1)}, bf16[128,1536]{1,0:T(8,128)(2,1)S(1)}) custom-call(bf16[1024,1536]{1,0:T(8,128)(2,1)S(1)} %bitcast.5), custom_call_target="tpu_custom_call" | custom-call | tf_op jit(solution)/shard_map/pallas_call | solution.py:282
  15.8 1.9 %shard_map.58 = (f32[352,1024]{1,0:T(8,128)S(1)}, f32[1,1024]{1,0:T(1,128)S(1)}, bf16[352,1536]{1,0:T(8,128)(2,1)S(1)}) custom-call(bf16[176,1536]{1,0:T(8,128)(2,1)S(1)} %copy-done.1, bf16[176,1536]{1,0:T(8,128)(2,1)S(1)} %collective-permute-done.refs_1_, f32[1,704]{1,0:T(1,128)S(1)} %shard_map.56.refs_2_, ...), custom_call_target="tpu_custom_call" | custom-call | tf_op jit(solution)/shard_map/pallas_call | solution.py:282
  17.7 0.5 collective-permute-done.3.codes_ref.refs_4_
  18.1 1.3 %collective-permute-done.1.refs_0_ = bf16[176,1536]{1,0:T(8,128)(2,1)S(1)} collective-permute-done((bf16[176,1536]{1,0:T(8,128)(2,1)}, bf16[176,1536]{1,0:T(8,128)(2,1)S(1)}, u32[]{:S(2)}, u32[]{:S(2)}) %collective-permute-start.1) | collective-permute-done | bytes 540704 | tf_op jit(solution)/shard_map/ppermute | solution.py:299
  19.4 3.9 %collective-permute-start.5 = (bf16[112,1536]{1,0:T(8,128)(2,1)S(1)}, bf16[112,1536]{1,0:T(8,128)(2,1)S(1)}, u32[]{:S(2)}, u32[]{:S(2)}) collective-permute-start(bf16[112,1536]{1,0:T(8,128)(2,1)S(1)} %copy-done.4), channel_id=1, source_target_pairs={{0,24},{4,28},{8,16},{12,20},{16,8},{20,12},{24,0},{28,4},{1,25},{... | collective-permute-start | bytes 1032200 | tf_op jit(solution)/shard_map/ppermute | solution.py:299
  23.3 1.8 %shard_map.59 = (f32[352,1024]{1,0:T(8,128)S(1)}, f32[1,1024]{1,0:T(1,128)S(1)}, bf16[352,1536]{1,0:T(8,128)(2,1)S(1)}) custom-call(bf16[176,1536]{1,0:T(8,128)(2,1)S(1)} %collective-permute-done.1.refs_0_, bf16[176,1536]{1,0:T(8,128)(2,1)S(1)} %collective-permute-done.4.refs_1_, f32[1,704]{1,0:T(1,128)S(1)} %shard_map.56.refs_2_, ...), custom_call_target="tpu_custom_call" | custom-call | tf_op jit(solution)/shard_map/pallas_call | solution.py:282
  25.2 1.6 %collective-permute-start.8 = (bf16[64,1536]{1,0:T(8,128)(2,1)S(1)}, bf16[64,1536]{1,0:T(8,128)(2,1)S(1)}, u32[]{:S(2)}, u32[]{:S(2)}) collective-permute-start(bf16[64,1536]{1,0:T(8,128)(2,1)S(1)} %collective-permute-done.2), channel_id=1, source_target_pairs={{0,2},{1,3},{2,0},{3,1},{4,6},{5,7},{6,4},{7,5},{8,10},{9,11},{10,... | collective-permute-start | bytes 589832 | tf_op jit(solution)/shard_map/ppermute | solution.py:299
  26.8 1.5 %collective-permute-start.6 = (f32[1,1024]{1,0:T(1,128)S(1)}, f32[1,1024]{1,0:T(1,128)S(1)}, u32[]{:S(2)}, u32[]{:S(2)}) collective-permute-start(f32[1,1024]{1,0:T(1,128)S(1)} %add.21), channel_id=1, source_target_pairs={{0,4},{4,0},{8,12},{12,8},{16,20},{20,16},{24,28},{28,24},{1,5},{5... | collective-permute-start | bytes 12296 | tf_op jit(solution)/shard_map/ppermute | solution.py:299
  28.3 2.1 %collective-permute-done.6 = f32[1,1024]{1,0:T(1,128)S(1)} collective-permute-done((f32[1,1024]{1,0:T(1,128)S(1)}, f32[1,1024]{1,0:T(1,128)S(1)}, u32[]{:S(2)}, u32[]{:S(2)}) %collective-permute-start.6) | collective-permute-done | bytes 4128 | tf_op jit(solution)/shard_map/ppermute | solution.py:299
  30.4 3.6 %collective-permute-done.7 = f32[1,1024]{1,0:T(1,128)S(1)} collective-permute-done((f32[1,1024]{1,0:T(1,128)S(1)}, f32[1,1024]{1,0:T(1,128)S(1)}, u32[]{:S(2)}, u32[]{:S(2)}) %collective-permute-start.7) | collective-permute-done | bytes 4128 | tf_op jit(solution)/shard_map/ppermute | solution.py:299
  34.0 0.9 %collective-permute-start.9 = (f32[1,1024]{1,0:T(1,128)S(1)}, f32[1,1024]{1,0:T(1,128)S(1)}, u32[]{:S(2)}, u32[]{:S(2)}) collective-permute-start(f32[1,1024]{1,0:T(1,128)S(1)} %add.23), channel_id=1, source_target_pairs={{0,16},{4,20},{8,24},{12,28},{16,0},{20,4},{24,8},{28,12},{1,17},{... | collective-permute-start | bytes 12296 | tf_op jit(solution)/shard_map/ppermute | solution.py:299
  34.9 3.8 %collective-permute-done.9 = f32[1,1024]{1,0:T(1,128)S(1)} collective-permute-done((f32[1,1024]{1,0:T(1,128)S(1)}, f32[1,1024]{1,0:T(1,128)S(1)}, u32[]{:S(2)}, u32[]{:S(2)}) %collective-permute-start.9) | collective-permute-done | bytes 4128 | tf_op jit(solution)/shard_map/ppermute | solution.py:299
  38.7 0.1 collective-permute-start.10
  38.8 1.6 %collective-permute-start.16 = (bf16[112,1536]{1,0:T(8,128)(2,1)S(1)}, bf16[112,1536]{1,0:T(8,128)(2,1)S(1)}, u32[]{:S(2)}, u32[]{:S(2)}) collective-permute-start(bf16[112,1536]{1,0:T(8,128)(2,1)S(1)} %collective-permute-done.5.refs_0_), channel_id=1, source_target_pairs={{0,2},{1,3},{2,0},{3,1},{4,6},{5,7},{6,4},{7,5},{8,10},{9,11},{10,... | collective-permute-start | bytes 1032200 | tf_op jit(solution)/shard_map/ppermute | solution.py:299
  40.4 0.2 collective-permute-start.11
  40.5 2.5 %collective-permute-start.12 = (bf16[80,1536]{1,0:T(8,128)(2,1)S(1)}, bf16[80,1536]{1,0:T(8,128)(2,1)S(1)}, u32[]{:S(2)}, u32[]{:S(2)}) collective-permute-start(bf16[80,1536]{1,0:T(8,128)(2,1)S(1)} %copy-done.5), channel_id=1, source_target_pairs={{0,24},{4,28},{8,16},{12,20},{16,8},{20,12},{24,0},{28,4},{1,25},{... | collective-permute-start | bytes 737288 | tf_op jit(solution)/shard_map/ppermute | solution.py:299
  43.0 0.6 shard_map.60
  43.6 1.6 %collective-permute-start.13 = (f32[1,1024]{1,0:T(1,128)S(1)}, f32[1,1024]{1,0:T(1,128)S(1)}, u32[]{:S(2)}, u32[]{:S(2)}) collective-permute-start(f32[1,1024]{1,0:T(1,128)S(1)} %shard_map.60), channel_id=1, source_target_pairs={{0,4},{4,0},{8,12},{12,8},{16,20},{20,16},{24,28},{28,24},{1,5},{5... | collective-permute-start | bytes 12296 | tf_op jit(solution)/shard_map/ppermute | solution.py:299
  45.2 2.1 %collective-permute-done.13 = f32[1,1024]{1,0:T(1,128)S(1)} collective-permute-done((f32[1,1024]{1,0:T(1,128)S(1)}, f32[1,1024]{1,0:T(1,128)S(1)}, u32[]{:S(2)}, u32[]{:S(2)}) %collective-permute-start.13) | collective-permute-done | bytes 4128 | tf_op jit(solution)/shard_map/ppermute | solution.py:299
  47.3 0.4 shard_map.61
  47.7 1.9 %shard_map.62 = (f32[320,640]{1,0:T(8,128)S(1)}, f32[1,640]{1,0:T(1,128)}, bf16[320,1536]{1,0:T(8,128)(2,1)S(1)}) custom-call(bf16[112,1536]{1,0:T(8,128)(2,1)S(1)} %collective-permute-done.5.refs_0_, bf16[112,1536]{1,0:T(8,128)(2,1)S(1)} %collective-permute-done.10.refs_1_, bf16[64,1536]{1,0:T(8,128)(2,1)S(1)} %collective-permute-done.8.refs_2_, ...), custom_call_target="tpu_custom_call" | custom-call | tf_op jit(solution)/shard_map/pallas_call | solution.py:282
  49.6 1.3 %collective-permute-done.14 = f32[1,1024]{1,0:T(1,128)S(1)} collective-permute-done((f32[1,1024]{1,0:T(1,128)S(1)}, f32[1,1024]{1,0:T(1,128)S(1)}, u32[]{:S(2)}, u32[]{:S(2)}) %collective-permute-start.14) | collective-permute-done | bytes 4128 | tf_op jit(solution)/shard_map/ppermute | solution.py:299
  50.9 0.1 collective-permute-start.17
  51.0 0.5 collective-permute-start.15
  51.4 3.9 %collective-permute-start.18 = (f32[1,1024]{1,0:T(1,128)S(1)}, f32[1,1024]{1,0:T(1,128)S(1)}, u32[]{:S(2)}, u32[]{:S(2)}) collective-permute-start(f32[1,1024]{1,0:T(1,128)S(1)} %add.26), channel_id=1, source_target_pairs={{0,16},{4,20},{8,24},{12,28},{16,0},{20,4},{24,8},{28,12},{1,17},{... | collective-permute-start | bytes 12296 | tf_op jit(solution)/shard_map/ppermute | solution.py:299
  55.4 1.8 %shard_map.63 = (f32[384,640]{1,0:T(8,128)S(1)}, f32[1,640]{1,0:T(1,128)}, bf16[384,1536]{1,0:T(8,128)(2,1)S(1)}) custom-call(bf16[80,1536]{1,0:T(8,128)(2,1)S(1)} %collective-permute-done.12.refs_0_, bf16[80,1536]{1,0:T(8,128)(2,1)S(1)} %collective-permute-done.15.refs_1_, bf16[112,1536]{1,0:T(8,128)(2,1)S(1)} %collective-permute-done.16.refs_2_, ...), custom_call_target="tpu_custom_call" | custom-call | tf_op jit(solution)/shard_map/pallas_call | solution.py:282
  57.2 1.9 %shard_map.64 = (bf16[1,128,768]{2,1,0:T(8,128)(2,1)S(1)}, bf16[1,128,768]{2,1,0:T(8,128)(2,1)S(1)}, bf16[1408,512]{1,0:T(8,128)(2,1)S(1)}) custom-call(f32[352,1024]{1,0:T(8,128)S(1)} %get-tuple-element.50.refs_0_, f32[352,1024]{1,0:T(8,128)S(1)} %get-tuple-element.55.refs_1_, f32[320,640]{1,0:T(8,128)S(1)} %get-tuple-element.66.refs_2_, ...), custom_call_target="tpu_custom_call" | custom-call | tf_op jit(solution)/shard_map/pallas_call | solution.py:282
  59.1 1.7 %collective-permute-start.23 = (bf16[1,128,768]{2,1,0:T(8,128)(2,1)S(1)}, bf16[1,128,768]{2,1,0:T(8,128)(2,1)S(1)}, u32[]{:S(2)}, u32[]{:S(2)}) collective-permute-start(bf16[1,128,768]{2,1,0:T(8,128)(2,1)S(1)} %get-tuple-element.85), channel_id=1, source_target_pairs={{0,8},{4,12},{8,0},{12,4},{16,24},{20,28},{24,16},{28,20},{1,9},{5... | collective-permute-start | bytes 589832 | tf_op jit(solution)/shard_map/ppermute | solution.py:299
  60.8 1.5 %collective-permute-start.20 = (bf16[1,128,768]{2,1,0:T(8,128)(2,1)S(1)}, bf16[1,128,768]{2,1,0:T(8,128)(2,1)S(1)}, u32[]{:S(2)}, u32[]{:S(2)}) collective-permute-start(bf16[1,128,768]{2,1,0:T(8,128)(2,1)S(1)} %get-tuple-element.82), channel_id=1, source_target_pairs={{0,4},{4,0},{8,12},{12,8},{16,20},{20,16},{24,28},{28,24},{1,5},{5... | collective-permute-start | bytes 589832 | tf_op jit(solution)/shard_map/ppermute | solution.py:299
  62.4 2.7 %shard_map.65 = (bf16[1,128,768]{2,1,0:T(8,128)(2,1)S(1)}, bf16[1,128,768]{2,1,0:T(8,128)(2,1)S(1)}, f32[2,128,768]{2,1,0:T(8,128)S(1)}, f32[2,128,768]{2,1,0:T(8,128)S(1)}) custom-call(bf16[1408,512]{1,0:T(8,128)(2,1)S(1)} %get-tuple-element.79.refs_0_, bf16[352,1536]{1,0:T(8,128)(2,1)S(1)} %get-tuple-element.75.refs_5_.refs_1_, ...), custom_call_target="tpu_custom_call" | custom-call | tf_op jit(solution)/shard_map/pallas_call | solution.py:282
  65.1 0.6 collective-permute-start.19
  65.6 0.4 collective-permute-start.22
  66.0 0.2 collective-permute-done.23.came_ref
  66.2 1.6 %collective-permute-start.24 = (bf16[1,128,768]{2,1,0:T(8,128)(2,1)S(1)}, bf16[1,128,768]{2,1,0:T(8,128)(2,1)S(1)}, u32[]{:S(2)}, u32[]{:S(2)}) collective-permute-start(bf16[1,128,768]{2,1,0:T(8,128)(2,1)S(1)} %shard_map.67), channel_id=1, source_target_pairs={{0,4},{4,0},{8,12},{12,8},{16,20},{20,16},{24,28},{28,24},{1,5},{5... | collective-permute-start | bytes 589832 | tf_op jit(solution)/shard_map/ppermute | solution.py:299
  67.9 1.5 %collective-permute-start.21 = (bf16[1,128,768]{2,1,0:T(8,128)(2,1)S(1)}, bf16[1,128,768]{2,1,0:T(8,128)(2,1)S(1)}, u32[]{:S(2)}, u32[]{:S(2)}) collective-permute-start(bf16[1,128,768]{2,1,0:T(8,128)(2,1)S(1)} %shard_map.66), channel_id=1, source_target_pairs={{0,8},{4,12},{8,0},{12,4},{16,24},{20,28},{24,16},{28,20},{1,9},{5... | collective-permute-start | bytes 589832 | tf_op jit(solution)/shard_map/ppermute | solution.py:299
  69.4 3.6 %collective-permute-done.19.refs_1_ = bf16[1,128,768]{2,1,0:T(8,128)(2,1)S(1)} collective-permute-done((bf16[1,128,768]{2,1,0:T(8,128)(2,1)S(1)}, bf16[1,128,768]{2,1,0:T(8,128)(2,1)S(1)}, u32[]{:S(2)}, u32[]{:S(2)}) %collective-permute-start.19) | collective-permute-done | bytes 196640 | tf_op jit(solution)/shard_map/ppermute | solution.py:299
  73.0 2.1 %collective-permute-done.24.refs_5_ = bf16[1,128,768]{2,1,0:T(8,128)(2,1)S(1)} collective-permute-done((bf16[1,128,768]{2,1,0:T(8,128)(2,1)S(1)}, bf16[1,128,768]{2,1,0:T(8,128)(2,1)S(1)}, u32[]{:S(2)}, u32[]{:S(2)}) %collective-permute-start.24) | collective-permute-done | bytes 196640 | tf_op jit(solution)/shard_map/ppermute | solution.py:299
  75.2 0.4 collective-permute-done.21.refs_2_
  75.5 1.1 %shard_map.68 = bf16[128,1536]{1,0:T(8,128)(2,1)} custom-call(f32[2,128,768]{2,1,0:T(8,128)S(1)} %get-tuple-element.80.keep_ref.refs_0_, bf16[1,128,768]{2,1,0:T(8,128)(2,1)S(1)} %collective-permute-done.19.refs_1_, bf16[1,128,768]{2,1,0:T(8,128)(2,1)S(1)} %collective-permute-done.21.refs_2_, f32[2,128,768]{2,1,0:T(8,128)S(1)} %get-tuple-element.83.keep_ref.refs_3_, ...), custom_call_target="tpu_custom_call" | custom-call | tf_op jit(solution)/shard_map/pallas_call | solution.py:282
  (35 shorter events, 0.2 us)
Async XLA Ops:
  3.2 12.5 %collective-permute-start = (bf16[176,1536]{1,0:T(8,128)(2,1)}, bf16[176,1536]{1,0:T(8,128)(2,1)S(1)}, u32[]{:S(2)}, u32[]{:S(2)}) collective-permute-start(bf16[176,1536]{1,0:T(8,128)(2,1)} %get-tuple-element.46.refs_0_), channel_id=1, source_target_pairs={{0,1},{1,0},{2,3},{3,2},{4,5},{5,4},{6,7},{7,6},{8,9},{9,8},{10,11... | collective-permute-start | bytes 1622024 | tf_op jit(solution)/shard_map/ppermute | solution.py:299
  3.8 15.6 %collective-permute-start.1 = (bf16[176,1536]{1,0:T(8,128)(2,1)}, bf16[176,1536]{1,0:T(8,128)(2,1)S(1)}, u32[]{:S(2)}, u32[]{:S(2)}) collective-permute-start(bf16[176,1536]{1,0:T(8,128)(2,1)} %get-tuple-element.51), channel_id=1, source_target_pairs={{0,2},{1,3},{2,0},{3,1},{4,6},{5,7},{6,4},{7,5},{8,10},{9,11},{10,... | collective-permute-start | bytes 1622024 | tf_op jit(solution)/shard_map/ppermute | solution.py:299
  6.3 11.8 %collective-permute-start.2 = (bf16[64,1536]{1,0:T(8,128)(2,1)}, bf16[64,1536]{1,0:T(8,128)(2,1)S(1)}, u32[]{:S(2)}, u32[]{:S(2)}) collective-permute-start(bf16[64,1536]{1,0:T(8,128)(2,1)} %get-tuple-element.53), channel_id=1, source_target_pairs={{0,24},{4,28},{8,16},{12,20},{16,8},{20,12},{24,0},{28,4},{1,25},{... | collective-permute-start | bytes 589832 | tf_op jit(solution)/shard_map/ppermute | solution.py:299
  9.9 0.7 copy-start.2
  10.6 0.6 copy-start.3
  12.6 5.6 %collective-permute-start.3 = (f32[1,704]{1,0:T(1,128)S(1)}, f32[1,704]{1,0:T(1,128)S(1)}, u32[]{:S(2)}, u32[]{:S(2)}) collective-permute-start(f32[1,704]{1,0:T(1,128)S(1)} %shard_map.56.refs_2_), channel_id=1, source_target_pairs={{0,24},{4,28},{8,16},{12,20},{16,8},{20,12},{24,0},{28,4},{1,25},{... | collective-permute-start | bytes 8456 | tf_op jit(solution)/shard_map/ppermute | solution.py:299
  12.9 1.9 %copy-start = (bf16[1,1024,1536]{2,1,0:T(8,128)(2,1)S(1)}, bf16[1,1024,1536]{2,1,0:T(8,128)(2,1)}, u32[]{:S(2)}) copy-start(bf16[1,1024,1536]{2,1,0:T(8,128)(2,1)} %param.9) | copy-start | bytes 9437188
  14.8 1.0 %copy-start.1 = (bf16[176,1536]{1,0:T(8,128)(2,1)S(1)}, bf16[176,1536]{1,0:T(8,128)(2,1)}, u32[]{:S(2)}) copy-start(bf16[176,1536]{1,0:T(8,128)(2,1)} %get-tuple-element.46.refs_0_) | copy-start | bytes 1622020
  15.8 3.6 %copy-start.4 = (bf16[112,1536]{1,0:T(8,128)(2,1)S(1)}, bf16[112,1536]{1,0:T(8,128)(2,1)}, u32[]{:S(2)}) copy-start(bf16[112,1536]{1,0:T(8,128)(2,1)} %get-tuple-element.57) | copy-start | bytes 1032196
  19.4 3.9 %collective-permute-start.4 = (bf16[176,1536]{1,0:T(8,128)(2,1)S(1)}, bf16[176,1536]{1,0:T(8,128)(2,1)S(1)}, u32[]{:S(2)}, u32[]{:S(2)}) collective-permute-start(bf16[176,1536]{1,0:T(8,128)(2,1)S(1)} %collective-permute-done.1.refs_0_), channel_id=1, source_target_pairs={{0,1},{1,0},{2,3},{3,2},{4,5},{5,4},{6,7},{7,6},{8,9},{9,8},{10,11... | collective-permute-start | bytes 1622024 | tf_op jit(solution)/shard_map/ppermute | solution.py:299
  19.4 21.1 %copy-start.5 = (bf16[80,1536]{1,0:T(8,128)(2,1)S(1)}, bf16[80,1536]{1,0:T(8,128)(2,1)}, u32[]{:S(2)}) copy-start(bf16[80,1536]{1,0:T(8,128)(2,1)} %get-tuple-element.68) | copy-start | bytes 737284
  19.4 19.3 %collective-permute-start.5 = (bf16[112,1536]{1,0:T(8,128)(2,1)S(1)}, bf16[112,1536]{1,0:T(8,128)(2,1)S(1)}, u32[]{:S(2)}, u32[]{:S(2)}) collective-permute-start(bf16[112,1536]{1,0:T(8,128)(2,1)S(1)} %copy-done.4), channel_id=1, source_target_pairs={{0,24},{4,28},{8,16},{12,20},{16,8},{20,12},{24,0},{28,4},{1,25},{... | collective-permute-start | bytes 1032200 | tf_op jit(solution)/shard_map/ppermute | solution.py:299
  25.2 8.8 %collective-permute-start.8 = (bf16[64,1536]{1,0:T(8,128)(2,1)S(1)}, bf16[64,1536]{1,0:T(8,128)(2,1)S(1)}, u32[]{:S(2)}, u32[]{:S(2)}) collective-permute-start(bf16[64,1536]{1,0:T(8,128)(2,1)S(1)} %collective-permute-done.2), channel_id=1, source_target_pairs={{0,2},{1,3},{2,0},{3,1},{4,6},{5,7},{6,4},{7,5},{8,10},{9,11},{10,... | collective-permute-start | bytes 589832 | tf_op jit(solution)/shard_map/ppermute | solution.py:299
  26.8 3.6 %collective-permute-start.6 = (f32[1,1024]{1,0:T(1,128)S(1)}, f32[1,1024]{1,0:T(1,128)S(1)}, u32[]{:S(2)}, u32[]{:S(2)}) collective-permute-start(f32[1,1024]{1,0:T(1,128)S(1)} %add.21), channel_id=1, source_target_pairs={{0,4},{4,0},{8,12},{12,8},{16,20},{20,16},{24,28},{28,24},{1,5},{5... | collective-permute-start | bytes 12296 | tf_op jit(solution)/shard_map/ppermute | solution.py:299
  30.4 3.6 %collective-permute-start.7 = (f32[1,1024]{1,0:T(1,128)S(1)}, f32[1,1024]{1,0:T(1,128)S(1)}, u32[]{:S(2)}, u32[]{:S(2)}) collective-permute-start(f32[1,1024]{1,0:T(1,128)S(1)} %add.22), channel_id=1, source_target_pairs={{0,8},{4,12},{8,0},{12,4},{16,24},{20,28},{24,16},{28,20},{1,9},{5... | collective-permute-start | bytes 12296 | tf_op jit(solution)/shard_map/ppermute | solution.py:299
  34.0 4.7 %collective-permute-start.9 = (f32[1,1024]{1,0:T(1,128)S(1)}, f32[1,1024]{1,0:T(1,128)S(1)}, u32[]{:S(2)}, u32[]{:S(2)}) collective-permute-start(f32[1,1024]{1,0:T(1,128)S(1)} %add.23), channel_id=1, source_target_pairs={{0,16},{4,20},{8,24},{12,28},{16,0},{20,4},{24,8},{28,12},{1,17},{... | collective-permute-start | bytes 12296 | tf_op jit(solution)/shard_map/ppermute | solution.py:299
  38.7 9.0 %collective-permute-start.10 = (bf16[112,1536]{1,0:T(8,128)(2,1)S(1)}, bf16[112,1536]{1,0:T(8,128)(2,1)S(1)}, u32[]{:S(2)}, u32[]{:S(2)}) collective-permute-start(bf16[112,1536]{1,0:T(8,128)(2,1)S(1)} %collective-permute-done.5.refs_0_), channel_id=1, source_target_pairs={{0,1},{1,0},{2,3},{3,2},{4,5},{5,4},{6,7},{7,6},{8,9},{9,8},{10,11... | collective-permute-start | bytes 1032200 | tf_op jit(solution)/shard_map/ppermute | solution.py:299
  38.8 12.1 %collective-permute-start.16 = (bf16[112,1536]{1,0:T(8,128)(2,1)S(1)}, bf16[112,1536]{1,0:T(8,128)(2,1)S(1)}, u32[]{:S(2)}, u32[]{:S(2)}) collective-permute-start(bf16[112,1536]{1,0:T(8,128)(2,1)S(1)} %collective-permute-done.5.refs_0_), channel_id=1, source_target_pairs={{0,2},{1,3},{2,0},{3,1},{4,6},{5,7},{6,4},{7,5},{8,10},{9,11},{10,... | collective-permute-start | bytes 1032200 | tf_op jit(solution)/shard_map/ppermute | solution.py:299
  40.4 7.3 %collective-permute-start.11 = (bf16[64,1536]{1,0:T(8,128)(2,1)S(1)}, bf16[64,1536]{1,0:T(8,128)(2,1)S(1)}, u32[]{:S(2)}, u32[]{:S(2)}) collective-permute-start(bf16[64,1536]{1,0:T(8,128)(2,1)S(1)} %collective-permute-done.8.refs_2_), channel_id=1, source_target_pairs={{0,1},{1,0},{2,3},{3,2},{4,5},{5,4},{6,7},{7,6},{8,9},{9,8},{10,11... | collective-permute-start | bytes 589832 | tf_op jit(solution)/shard_map/ppermute | solution.py:299
  40.5 10.4 %collective-permute-start.12 = (bf16[80,1536]{1,0:T(8,128)(2,1)S(1)}, bf16[80,1536]{1,0:T(8,128)(2,1)S(1)}, u32[]{:S(2)}, u32[]{:S(2)}) collective-permute-start(bf16[80,1536]{1,0:T(8,128)(2,1)S(1)} %copy-done.5), channel_id=1, source_target_pairs={{0,24},{4,28},{8,16},{12,20},{16,8},{20,12},{24,0},{28,4},{1,25},{... | collective-permute-start | bytes 737288 | tf_op jit(solution)/shard_map/ppermute | solution.py:299
  43.6 3.7 %collective-permute-start.13 = (f32[1,1024]{1,0:T(1,128)S(1)}, f32[1,1024]{1,0:T(1,128)S(1)}, u32[]{:S(2)}, u32[]{:S(2)}) collective-permute-start(f32[1,1024]{1,0:T(1,128)S(1)} %shard_map.60), channel_id=1, source_target_pairs={{0,4},{4,0},{8,12},{12,8},{16,20},{20,16},{24,28},{28,24},{1,5},{5... | collective-permute-start | bytes 12296 | tf_op jit(solution)/shard_map/ppermute | solution.py:299
  47.2 3.6 %collective-permute-start.14 = (f32[1,1024]{1,0:T(1,128)S(1)}, f32[1,1024]{1,0:T(1,128)S(1)}, u32[]{:S(2)}, u32[]{:S(2)}) collective-permute-start(f32[1,1024]{1,0:T(1,128)S(1)} %add.25), channel_id=1, source_target_pairs={{0,8},{4,12},{8,0},{12,4},{16,24},{20,28},{24,16},{28,20},{1,9},{5... | collective-permute-start | bytes 12296 | tf_op jit(solution)/shard_map/ppermute | solution.py:299
  50.9 4.5 %collective-permute-start.17 = (bf16[112,1536]{1,0:T(8,128)(2,1)S(1)}, bf16[112,1536]{1,0:T(8,128)(2,1)S(1)}, u32[]{:S(2)}, u32[]{:S(2)}) collective-permute-start(bf16[112,1536]{1,0:T(8,128)(2,1)S(1)} %collective-permute-done.16.refs_2_), channel_id=1, source_target_pairs={{0,1},{1,0},{2,3},{3,2},{4,5},{5,4},{6,7},{7,6},{8,9},{9,8},{10,11... | collective-permute-start | bytes 1032200 | tf_op jit(solution)/shard_map/ppermute | solution.py:299
  51.0 4.4 %collective-permute-start.15 = (bf16[80,1536]{1,0:T(8,128)(2,1)S(1)}, bf16[80,1536]{1,0:T(8,128)(2,1)S(1)}, u32[]{:S(2)}, u32[]{:S(2)}) collective-permute-start(bf16[80,1536]{1,0:T(8,128)(2,1)S(1)} %collective-permute-done.12.refs_0_), channel_id=1, source_target_pairs={{0,1},{1,0},{2,3},{3,2},{4,5},{5,4},{6,7},{7,6},{8,9},{9,8},{10,11... | collective-permute-start | bytes 737288 | tf_op jit(solution)/shard_map/ppermute | solution.py:299
  51.4 5.8 %collective-permute-start.18 = (f32[1,1024]{1,0:T(1,128)S(1)}, f32[1,1024]{1,0:T(1,128)S(1)}, u32[]{:S(2)}, u32[]{:S(2)}) collective-permute-start(f32[1,1024]{1,0:T(1,128)S(1)} %add.26), channel_id=1, source_target_pairs={{0,16},{4,20},{8,24},{12,28},{16,0},{20,4},{24,8},{28,12},{1,17},{... | collective-permute-start | bytes 12296 | tf_op jit(solution)/shard_map/ppermute | solution.py:299
  59.1 7.1 %collective-permute-start.23 = (bf16[1,128,768]{2,1,0:T(8,128)(2,1)S(1)}, bf16[1,128,768]{2,1,0:T(8,128)(2,1)S(1)}, u32[]{:S(2)}, u32[]{:S(2)}) collective-permute-start(bf16[1,128,768]{2,1,0:T(8,128)(2,1)S(1)} %get-tuple-element.85), channel_id=1, source_target_pairs={{0,8},{4,12},{8,0},{12,4},{16,24},{20,28},{24,16},{28,20},{1,9},{5... | collective-permute-start | bytes 589832 | tf_op jit(solution)/shard_map/ppermute | solution.py:299
  60.8 7.0 %collective-permute-start.20 = (bf16[1,128,768]{2,1,0:T(8,128)(2,1)S(1)}, bf16[1,128,768]{2,1,0:T(8,128)(2,1)S(1)}, u32[]{:S(2)}, u32[]{:S(2)}) collective-permute-start(bf16[1,128,768]{2,1,0:T(8,128)(2,1)S(1)} %get-tuple-element.82), channel_id=1, source_target_pairs={{0,4},{4,0},{8,12},{12,8},{16,20},{20,16},{24,28},{28,24},{1,5},{5... | collective-permute-start | bytes 589832 | tf_op jit(solution)/shard_map/ppermute | solution.py:299
  65.1 7.9 %collective-permute-start.19 = (bf16[1,128,768]{2,1,0:T(8,128)(2,1)S(1)}, bf16[1,128,768]{2,1,0:T(8,128)(2,1)S(1)}, u32[]{:S(2)}, u32[]{:S(2)}) collective-permute-start(bf16[1,128,768]{2,1,0:T(8,128)(2,1)S(1)} %get-tuple-element.81), channel_id=1, source_target_pairs={{0,4},{4,0},{8,12},{12,8},{16,20},{20,16},{24,28},{28,24},{1,5},{5... | collective-permute-start | bytes 589832 | tf_op jit(solution)/shard_map/ppermute | solution.py:299
  65.6 7.4 %collective-permute-start.22 = (bf16[1,128,768]{2,1,0:T(8,128)(2,1)S(1)}, bf16[1,128,768]{2,1,0:T(8,128)(2,1)S(1)}, u32[]{:S(2)}, u32[]{:S(2)}) collective-permute-start(bf16[1,128,768]{2,1,0:T(8,128)(2,1)S(1)} %get-tuple-element.84), channel_id=1, source_target_pairs={{0,8},{4,12},{8,0},{12,4},{16,24},{20,28},{24,16},{28,20},{1,9},{5... | collective-permute-start | bytes 589832 | tf_op jit(solution)/shard_map/ppermute | solution.py:299
  66.2 8.9 %collective-permute-start.24 = (bf16[1,128,768]{2,1,0:T(8,128)(2,1)S(1)}, bf16[1,128,768]{2,1,0:T(8,128)(2,1)S(1)}, u32[]{:S(2)}, u32[]{:S(2)}) collective-permute-start(bf16[1,128,768]{2,1,0:T(8,128)(2,1)S(1)} %shard_map.67), channel_id=1, source_target_pairs={{0,4},{4,0},{8,12},{12,8},{16,20},{20,16},{24,28},{28,24},{1,5},{5... | collective-permute-start | bytes 589832 | tf_op jit(solution)/shard_map/ppermute | solution.py:299
  67.9 7.6 %collective-permute-start.21 = (bf16[1,128,768]{2,1,0:T(8,128)(2,1)S(1)}, bf16[1,128,768]{2,1,0:T(8,128)(2,1)S(1)}, u32[]{:S(2)}, u32[]{:S(2)}) collective-permute-start(bf16[1,128,768]{2,1,0:T(8,128)(2,1)S(1)} %shard_map.66), channel_id=1, source_target_pairs={{0,8},{4,12},{8,0},{12,4},{16,24},{20,28},{24,16},{28,20},{1,9},{5... | collective-permute-start | bytes 589832 | tf_op jit(solution)/shard_map/ppermute | solution.py:299

commit v7 on v6

--- a/solution.py
+++ b/solution.py
@@ -43,7 +43,7 @@
     wide = max(e - s for s, e in zip(starts, ends))
     starts = [min(s, tok - wide) for s in starts]
     starts = [min(s, tok - wide) for s in starts]
-    soon = down(starts[min(1, chips - 1)] * 13 // 16)
+    soon = starts[min(1, chips - 1)]
     cuts = sorted({0, soon, tok} | {s + wide for s in starts})
     pieces = list(zip(cuts[:-1], cuts[1:]))
     parts = [[k for k, (lo, hi) in enumerate(pieces) if lo < s + wide and s < hi] for s in starts]

time: 76.9 us -> 75.5 us (0.982)
  starting transfers between devices: 32.5 us -> 31.1 us
    ppermute x25, starting transfers between devices: 32.5 us -> 31.1 us  [swap(): lax.ppermute(values, axis, [(i, i ^ bit) for i in range(lax.axis_size(axi...]
  transfers between devices with their start and end apart: 25 -> 25, of which waited for: 12 -> 13; matrix products, arithmetic and copies ran while one was open for 0% -> 0% of each run, Pallas kernels for 18% -> 18%
where the time goes in v7:
time: 75.5 us; the launch traced here: 75.2 us
  starting transfers between devices  31.1 us (41%)
  waiting for transfers between devices  21 us (28%)
  Pallas kernels  19.7 us (26%)
  local copies, waits for them, and re-layouts  3.26 us (4%)
    ppermute x25, starting transfers between devices, swap(): lax.ppermute(values, axis, [(i, i ^ bit) for i in range(lax.axis_size(axi...  31.1 us
    ppermute x25, waiting for transfers between devices, swap(): lax.ppermute(values, axis, [(i, i ^ bit) for i in range(lax.axis_size(axi...  21 us
    pallas_call x14, Pallas kernels, call(): pl.pallas_call(kernel, out_shape=shapes, in_specs=[pl.BlockSpec(memory_sp...  19.7 us
    unnamed x12, local copies, waits for them, and re-layouts  3.26 us
  transfers between devices with their start and end apart: 25, of which 13 were waited for; matrix products, arithmetic and copies ran while one was open for 0% of the time, Pallas kernels for 18%

profile of v7, /device:TPU:0, one launch (start us, length us, event | category | flops | bytes accessed | tf_op | source)
XLA Modules:
  0.0 75.2 jit_solution(12948556055334802948)
XLA Ops:
  0.0 3.2 %shard_map.55 = (bf16[80,1536]{1,0:T(8,128)(2,1)}, bf16[96,1536]{1,0:T(8,128)(2,1)}, bf16[80,1536]{1,0:T(8,128)(2,1)}, bf16[176,1536]{1,0:T(8,128)(2,1)}, bf16[1...) custom-call(bf16[256,1536]{1,0:T(8,128)(2,1)} %refs_0_.1, s32[1,1024]{1,0:T(1,128)} %bitcast.6, ...), custom_call_target="tpu_custom_call" | custom-call | tf_op jit(solution)/shard_map/pallas_call | solution.py:282
  3.2 0.5 collective-permute-start
  3.8 2.6 %collective-permute-start.1 = (bf16[176,1536]{1,0:T(8,128)(2,1)}, bf16[176,1536]{1,0:T(8,128)(2,1)S(1)}, u32[]{:S(2)}, u32[]{:S(2)}) collective-permute-start(bf16[176,1536]{1,0:T(8,128)(2,1)} %get-tuple-element.51), channel_id=1, source_target_pairs={{0,2},{1,3},{2,0},{3,1},{4,6},{5,7},{6,4},{7,5},{8,10},{9,11},{10,... | collective-permute-start | bytes 1622024 | tf_op jit(solution)/shard_map/ppermute | solution.py:299
  6.3 3.6 %collective-permute-start.2 = (bf16[80,1536]{1,0:T(8,128)(2,1)}, bf16[80,1536]{1,0:T(8,128)(2,1)S(1)}, u32[]{:S(2)}, u32[]{:S(2)}) collective-permute-start(bf16[80,1536]{1,0:T(8,128)(2,1)} %get-tuple-element.53), channel_id=1, source_target_pairs={{0,24},{4,28},{8,16},{12,20},{16,8},{20,12},{24,0},{28,4},{1,25},{... | collective-permute-start | bytes 737288 | tf_op jit(solution)/shard_map/ppermute | solution.py:299
  9.9 0.7 copy-done.2
  10.6 0.7 copy-done.3
  11.3 1.4 %shard_map.56.refs_2_ = f32[1,704]{1,0:T(1,128)S(1)} custom-call(s32[1,1024]{1,0:T(1,128)S(1)} %copy-done.2, f32[1,64]{1,0:T(1,128)S(1)} %copy-done.3), custom_call_target="tpu_custom_call" | custom-call | tf_op jit(solution)/shard_map/pallas_call | solution.py:282
  12.7 0.3 collective-permute-start.3
  13.0 1.9 %copy-done = bf16[1,1024,1536]{2,1,0:T(8,128)(2,1)S(1)} copy-done((bf16[1,1024,1536]{2,1,0:T(8,128)(2,1)S(1)}, bf16[1,1024,1536]{2,1,0:T(8,128)(2,1)}, u32[]{:S(2)}) %copy-start) | copy-done | bytes 3145752
  14.8 1.0 %shard_map.57 = (bf16[1024,1536]{1,0:T(8,128)(2,1)S(1)}, bf16[128,1536]{1,0:T(8,128)(2,1)S(1)}) custom-call(bf16[1024,1536]{1,0:T(8,128)(2,1)S(1)} %bitcast.5), custom_call_target="tpu_custom_call" | custom-call | tf_op jit(solution)/shard_map/pallas_call | solution.py:282
  15.9 1.8 %shard_map.58 = (f32[352,1024]{1,0:T(8,128)S(1)}, f32[1,1024]{1,0:T(1,128)S(1)}, bf16[352,1536]{1,0:T(8,128)(2,1)S(1)}) custom-call(bf16[176,1536]{1,0:T(8,128)(2,1)S(1)} %copy-done.1, bf16[176,1536]{1,0:T(8,128)(2,1)S(1)} %collective-permute-done.refs_1_, f32[1,704]{1,0:T(1,128)S(1)} %shard_map.56.refs_2_, ...), custom_call_target="tpu_custom_call" | custom-call | tf_op jit(solution)/shard_map/pallas_call | solution.py:282
  17.7 0.5 collective-permute-done.3.codes_ref.refs_4_
  18.2 1.2 %collective-permute-done.1.refs_0_ = bf16[176,1536]{1,0:T(8,128)(2,1)S(1)} collective-permute-done((bf16[176,1536]{1,0:T(8,128)(2,1)}, bf16[176,1536]{1,0:T(8,128)(2,1)S(1)}, u32[]{:S(2)}, u32[]{:S(2)}) %collective-permute-start.1) | collective-permute-done | bytes 540704 | tf_op jit(solution)/shard_map/ppermute | solution.py:299
  19.4 3.9 %collective-permute-start.5 = (bf16[96,1536]{1,0:T(8,128)(2,1)S(1)}, bf16[96,1536]{1,0:T(8,128)(2,1)S(1)}, u32[]{:S(2)}, u32[]{:S(2)}) collective-permute-start(bf16[96,1536]{1,0:T(8,128)(2,1)S(1)} %copy-done.4), channel_id=1, source_target_pairs={{0,24},{4,28},{8,16},{12,20},{16,8},{20,12},{24,0},{28,4},{1,25},{... | collective-permute-start | bytes 884744 | tf_op jit(solution)/shard_map/ppermute | solution.py:299
  23.3 1.8 %shard_map.59 = (f32[352,1024]{1,0:T(8,128)S(1)}, f32[1,1024]{1,0:T(1,128)S(1)}, bf16[352,1536]{1,0:T(8,128)(2,1)S(1)}) custom-call(bf16[176,1536]{1,0:T(8,128)(2,1)S(1)} %collective-permute-done.1.refs_0_, bf16[176,1536]{1,0:T(8,128)(2,1)S(1)} %collective-permute-done.4.refs_1_, f32[1,704]{1,0:T(1,128)S(1)} %shard_map.56.refs_2_, ...), custom_call_target="tpu_custom_call" | custom-call | tf_op jit(solution)/shard_map/pallas_call | solution.py:282
  25.2 1.6 %collective-permute-start.8 = (bf16[80,1536]{1,0:T(8,128)(2,1)S(1)}, bf16[80,1536]{1,0:T(8,128)(2,1)S(1)}, u32[]{:S(2)}, u32[]{:S(2)}) collective-permute-start(bf16[80,1536]{1,0:T(8,128)(2,1)S(1)} %collective-permute-done.2), channel_id=1, source_target_pairs={{0,2},{1,3},{2,0},{3,1},{4,6},{5,7},{6,4},{7,5},{8,10},{9,11},{10,... | collective-permute-start | bytes 737288 | tf_op jit(solution)/shard_map/ppermute | solution.py:299
  26.7 1.5 %collective-permute-start.6 = (f32[1,1024]{1,0:T(1,128)S(1)}, f32[1,1024]{1,0:T(1,128)S(1)}, u32[]{:S(2)}, u32[]{:S(2)}) collective-permute-start(f32[1,1024]{1,0:T(1,128)S(1)} %add.21), channel_id=1, source_target_pairs={{0,4},{4,0},{8,12},{12,8},{16,20},{20,16},{24,28},{28,24},{1,5},{5... | collective-permute-start | bytes 12296 | tf_op jit(solution)/shard_map/ppermute | solution.py:299
  28.3 2.1 %collective-permute-done.6 = f32[1,1024]{1,0:T(1,128)S(1)} collective-permute-done((f32[1,1024]{1,0:T(1,128)S(1)}, f32[1,1024]{1,0:T(1,128)S(1)}, u32[]{:S(2)}, u32[]{:S(2)}) %collective-permute-start.6) | collective-permute-done | bytes 4128 | tf_op jit(solution)/shard_map/ppermute | solution.py:299
  30.4 3.6 %collective-permute-done.7 = f32[1,1024]{1,0:T(1,128)S(1)} collective-permute-done((f32[1,1024]{1,0:T(1,128)S(1)}, f32[1,1024]{1,0:T(1,128)S(1)}, u32[]{:S(2)}, u32[]{:S(2)}) %collective-permute-start.7) | collective-permute-done | bytes 4128 | tf_op jit(solution)/shard_map/ppermute | solution.py:299
  34.0 0.9 %collective-permute-start.9 = (f32[1,1024]{1,0:T(1,128)S(1)}, f32[1,1024]{1,0:T(1,128)S(1)}, u32[]{:S(2)}, u32[]{:S(2)}) collective-permute-start(f32[1,1024]{1,0:T(1,128)S(1)} %add.23), channel_id=1, source_target_pairs={{0,16},{4,20},{8,24},{12,28},{16,0},{20,4},{24,8},{28,12},{1,17},{... | collective-permute-start | bytes 12296 | tf_op jit(solution)/shard_map/ppermute | solution.py:299
  34.9 3.7 %collective-permute-done.9 = f32[1,1024]{1,0:T(1,128)S(1)} collective-permute-done((f32[1,1024]{1,0:T(1,128)S(1)}, f32[1,1024]{1,0:T(1,128)S(1)}, u32[]{:S(2)}, u32[]{:S(2)}) %collective-permute-start.9) | collective-permute-done | bytes 4128 | tf_op jit(solution)/shard_map/ppermute | solution.py:299
  38.6 0.1 collective-permute-start.10
  38.6 0.8 %collective-permute-start.16 = (bf16[96,1536]{1,0:T(8,128)(2,1)S(1)}, bf16[96,1536]{1,0:T(8,128)(2,1)S(1)}, u32[]{:S(2)}, u32[]{:S(2)}) collective-permute-start(bf16[96,1536]{1,0:T(8,128)(2,1)S(1)} %collective-permute-done.5.refs_0_), channel_id=1, source_target_pairs={{0,2},{1,3},{2,0},{3,1},{4,6},{5,7},{6,4},{7,5},{8,10},{9,11},{10,... | collective-permute-start | bytes 884744 | tf_op jit(solution)/shard_map/ppermute | solution.py:299
  39.4 0.2 collective-permute-start.11
  39.6 1.8 %collective-permute-start.12 = (bf16[80,1536]{1,0:T(8,128)(2,1)S(1)}, bf16[80,1536]{1,0:T(8,128)(2,1)S(1)}, u32[]{:S(2)}, u32[]{:S(2)}) collective-permute-start(bf16[80,1536]{1,0:T(8,128)(2,1)S(1)} %copy-done.5), channel_id=1, source_target_pairs={{0,24},{4,28},{8,16},{12,20},{16,8},{20,12},{24,0},{28,4},{1,25},{... | collective-permute-start | bytes 737288 | tf_op jit(solution)/shard_map/ppermute | solution.py:299
  41.4 0.6 shard_map.60
  42.0 1.6 %collective-permute-start.13 = (f32[1,1024]{1,0:T(1,128)S(1)}, f32[1,1024]{1,0:T(1,128)S(1)}, u32[]{:S(2)}, u32[]{:S(2)}) collective-permute-start(f32[1,1024]{1,0:T(1,128)S(1)} %shard_map.60), channel_id=1, source_target_pairs={{0,4},{4,0},{8,12},{12,8},{16,20},{20,16},{24,28},{28,24},{1,5},{5... | collective-permute-start | bytes 12296 | tf_op jit(solution)/shard_map/ppermute | solution.py:299
  43.6 2.1 %collective-permute-done.13 = f32[1,1024]{1,0:T(1,128)S(1)} collective-permute-done((f32[1,1024]{1,0:T(1,128)S(1)}, f32[1,1024]{1,0:T(1,128)S(1)}, u32[]{:S(2)}, u32[]{:S(2)}) %collective-permute-start.13) | collective-permute-done | bytes 4128 | tf_op jit(solution)/shard_map/ppermute | solution.py:299
  45.7 0.4 shard_map.61
  46.1 2.0 %shard_map.62 = (f32[352,640]{1,0:T(8,128)S(1)}, f32[1,640]{1,0:T(1,128)}, bf16[352,1536]{1,0:T(8,128)(2,1)S(1)}) custom-call(bf16[96,1536]{1,0:T(8,128)(2,1)S(1)} %collective-permute-done.5.refs_0_, bf16[96,1536]{1,0:T(8,128)(2,1)S(1)} %collective-permute-done.10.refs_1_, bf16[80,1536]{1,0:T(8,128)(2,1)S(1)} %collective-permute-done.8.refs_2_, ...), custom_call_target="tpu_custom_call" | custom-call | tf_op jit(solution)/shard_map/pallas_call | solution.py:282
  48.1 1.5 %collective-permute-done.14 = f32[1,1024]{1,0:T(1,128)S(1)} collective-permute-done((f32[1,1024]{1,0:T(1,128)S(1)}, f32[1,1024]{1,0:T(1,128)S(1)}, u32[]{:S(2)}, u32[]{:S(2)}) %collective-permute-start.14) | collective-permute-done | bytes 4128 | tf_op jit(solution)/shard_map/ppermute | solution.py:299
  49.8 0.4 collective-permute-start.15
  50.2 3.8 %collective-permute-start.18 = (f32[1,1024]{1,0:T(1,128)S(1)}, f32[1,1024]{1,0:T(1,128)S(1)}, u32[]{:S(2)}, u32[]{:S(2)}) collective-permute-start(f32[1,1024]{1,0:T(1,128)S(1)} %add.26), channel_id=1, source_target_pairs={{0,16},{4,20},{8,24},{12,28},{16,0},{20,4},{24,8},{28,12},{1,17},{... | collective-permute-start | bytes 12296 | tf_op jit(solution)/shard_map/ppermute | solution.py:299
  54.0 1.7 %shard_map.63 = (f32[352,640]{1,0:T(8,128)S(1)}, f32[1,640]{1,0:T(1,128)}, bf16[352,1536]{1,0:T(8,128)(2,1)S(1)}) custom-call(bf16[80,1536]{1,0:T(8,128)(2,1)S(1)} %collective-permute-done.12.refs_0_, bf16[80,1536]{1,0:T(8,128)(2,1)S(1)} %collective-permute-done.15.refs_1_, bf16[96,1536]{1,0:T(8,128)(2,1)S(1)} %collective-permute-done.16.refs_2_, ...), custom_call_target="tpu_custom_call" | custom-call | tf_op jit(solution)/shard_map/pallas_call | solution.py:282
  55.8 1.9 %shard_map.64 = (bf16[1,128,768]{2,1,0:T(8,128)(2,1)S(1)}, bf16[1,128,768]{2,1,0:T(8,128)(2,1)S(1)}, bf16[1408,512]{1,0:T(8,128)(2,1)S(1)}) custom-call(f32[352,1024]{1,0:T(8,128)S(1)} %get-tuple-element.50.refs_0_, f32[352,1024]{1,0:T(8,128)S(1)} %get-tuple-element.55.refs_1_, f32[352,640]{1,0:T(8,128)S(1)} %get-tuple-element.66.refs_2_, ...), custom_call_target="tpu_custom_call" | custom-call | tf_op jit(solution)/shard_map/pallas_call | solution.py:282
  57.7 1.8 %collective-permute-start.23 = (bf16[1,128,768]{2,1,0:T(8,128)(2,1)S(1)}, bf16[1,128,768]{2,1,0:T(8,128)(2,1)S(1)}, u32[]{:S(2)}, u32[]{:S(2)}) collective-permute-start(bf16[1,128,768]{2,1,0:T(8,128)(2,1)S(1)} %get-tuple-element.85), channel_id=1, source_target_pairs={{0,8},{4,12},{8,0},{12,4},{16,24},{20,28},{24,16},{28,20},{1,9},{5... | collective-permute-start | bytes 589832 | tf_op jit(solution)/shard_map/ppermute | solution.py:299
  59.5 1.5 %collective-permute-start.20 = (bf16[1,128,768]{2,1,0:T(8,128)(2,1)S(1)}, bf16[1,128,768]{2,1,0:T(8,128)(2,1)S(1)}, u32[]{:S(2)}, u32[]{:S(2)}) collective-permute-start(bf16[1,128,768]{2,1,0:T(8,128)(2,1)S(1)} %get-tuple-element.82), channel_id=1, source_target_pairs={{0,4},{4,0},{8,12},{12,8},{16,20},{20,16},{24,28},{28,24},{1,5},{5... | collective-permute-start | bytes 589832 | tf_op jit(solution)/shard_map/ppermute | solution.py:299
  61.0 2.7 %shard_map.65 = (bf16[1,128,768]{2,1,0:T(8,128)(2,1)S(1)}, bf16[1,128,768]{2,1,0:T(8,128)(2,1)S(1)}, f32[2,128,768]{2,1,0:T(8,128)S(1)}, f32[2,128,768]{2,1,0:T(8,128)S(1)}) custom-call(bf16[1408,512]{1,0:T(8,128)(2,1)S(1)} %get-tuple-element.79.refs_0_, bf16[352,1536]{1,0:T(8,128)(2,1)S(1)} %get-tuple-element.75.refs_5_.refs_1_, ...), custom_call_target="tpu_custom_call" | custom-call | tf_op jit(solution)/shard_map/pallas_call | solution.py:282
  63.7 0.6 collective-permute-start.19
  64.3 0.3 collective-permute-start.22
  64.5 0.2 collective-permute-done.23.came_ref
  64.8 1.6 %collective-permute-start.24 = (bf16[1,128,768]{2,1,0:T(8,128)(2,1)S(1)}, bf16[1,128,768]{2,1,0:T(8,128)(2,1)S(1)}, u32[]{:S(2)}, u32[]{:S(2)}) collective-permute-start(bf16[1,128,768]{2,1,0:T(8,128)(2,1)S(1)} %shard_map.67), channel_id=1, source_target_pairs={{0,4},{4,0},{8,12},{12,8},{16,20},{20,16},{24,28},{28,24},{1,5},{5... | collective-permute-start | bytes 589832 | tf_op jit(solution)/shard_map/ppermute | solution.py:299
  66.4 1.6 %collective-permute-start.21 = (bf16[1,128,768]{2,1,0:T(8,128)(2,1)S(1)}, bf16[1,128,768]{2,1,0:T(8,128)(2,1)S(1)}, u32[]{:S(2)}, u32[]{:S(2)}) collective-permute-start(bf16[1,128,768]{2,1,0:T(8,128)(2,1)S(1)} %shard_map.66), channel_id=1, source_target_pairs={{0,8},{4,12},{8,0},{12,4},{16,24},{20,28},{24,16},{28,20},{1,9},{5... | collective-permute-start | bytes 589832 | tf_op jit(solution)/shard_map/ppermute | solution.py:299
  68.0 3.6 %collective-permute-done.19.refs_1_ = bf16[1,128,768]{2,1,0:T(8,128)(2,1)S(1)} collective-permute-done((bf16[1,128,768]{2,1,0:T(8,128)(2,1)S(1)}, bf16[1,128,768]{2,1,0:T(8,128)(2,1)S(1)}, u32[]{:S(2)}, u32[]{:S(2)}) %collective-permute-start.19) | collective-permute-done | bytes 196640 | tf_op jit(solution)/shard_map/ppermute | solution.py:299
  71.6 0.2 collective-permute-done.22.refs_4_
  71.7 2.0 %collective-permute-done.24.refs_5_ = bf16[1,128,768]{2,1,0:T(8,128)(2,1)S(1)} collective-permute-done((bf16[1,128,768]{2,1,0:T(8,128)(2,1)S(1)}, bf16[1,128,768]{2,1,0:T(8,128)(2,1)S(1)}, u32[]{:S(2)}, u32[]{:S(2)}) %collective-permute-start.24) | collective-permute-done | bytes 196640 | tf_op jit(solution)/shard_map/ppermute | solution.py:299
  73.8 0.4 collective-permute-done.21.refs_2_
  74.1 1.1 %shard_map.68 = bf16[128,1536]{1,0:T(8,128)(2,1)} custom-call(f32[2,128,768]{2,1,0:T(8,128)S(1)} %get-tuple-element.80.keep_ref.refs_0_, bf16[1,128,768]{2,1,0:T(8,128)(2,1)S(1)} %collective-permute-done.19.refs_1_, bf16[1,128,768]{2,1,0:T(8,128)(2,1)S(1)} %collective-permute-done.21.refs_2_, f32[2,128,768]{2,1,0:T(8,128)S(1)} %get-tuple-element.83.keep_ref.refs_3_, ...), custom_call_target="tpu_custom_call" | custom-call | tf_op jit(solution)/shard_map/pallas_call | solution.py:282
  (35 shorter events, 0.3 us)
Async XLA Ops:
  3.2 12.6 %collective-permute-start = (bf16[176,1536]{1,0:T(8,128)(2,1)}, bf16[176,1536]{1,0:T(8,128)(2,1)S(1)}, u32[]{:S(2)}, u32[]{:S(2)}) collective-permute-start(bf16[176,1536]{1,0:T(8,128)(2,1)} %get-tuple-element.46.refs_0_), channel_id=1, source_target_pairs={{0,1},{1,0},{2,3},{3,2},{4,5},{5,4},{6,7},{7,6},{8,9},{9,8},{10,11... | collective-permute-start | bytes 1622024 | tf_op jit(solution)/shard_map/ppermute | solution.py:299
  3.8 15.6 %collective-permute-start.1 = (bf16[176,1536]{1,0:T(8,128)(2,1)}, bf16[176,1536]{1,0:T(8,128)(2,1)S(1)}, u32[]{:S(2)}, u32[]{:S(2)}) collective-permute-start(bf16[176,1536]{1,0:T(8,128)(2,1)} %get-tuple-element.51), channel_id=1, source_target_pairs={{0,2},{1,3},{2,0},{3,1},{4,6},{5,7},{6,4},{7,5},{8,10},{9,11},{10,... | collective-permute-start | bytes 1622024 | tf_op jit(solution)/shard_map/ppermute | solution.py:299
  6.3 11.9 %collective-permute-start.2 = (bf16[80,1536]{1,0:T(8,128)(2,1)}, bf16[80,1536]{1,0:T(8,128)(2,1)S(1)}, u32[]{:S(2)}, u32[]{:S(2)}) collective-permute-start(bf16[80,1536]{1,0:T(8,128)(2,1)} %get-tuple-element.53), channel_id=1, source_target_pairs={{0,24},{4,28},{8,16},{12,20},{16,8},{20,12},{24,0},{28,4},{1,25},{... | collective-permute-start | bytes 737288 | tf_op jit(solution)/shard_map/ppermute | solution.py:299
  9.9 0.7 copy-start.2
  10.6 0.7 copy-start.3
  12.7 5.6 %collective-permute-start.3 = (f32[1,704]{1,0:T(1,128)S(1)}, f32[1,704]{1,0:T(1,128)S(1)}, u32[]{:S(2)}, u32[]{:S(2)}) collective-permute-start(f32[1,704]{1,0:T(1,128)S(1)} %shard_map.56.refs_2_), channel_id=1, source_target_pairs={{0,24},{4,28},{8,16},{12,20},{16,8},{20,12},{24,0},{28,4},{1,25},{... | collective-permute-start | bytes 8456 | tf_op jit(solution)/shard_map/ppermute | solution.py:299
  12.9 1.9 %copy-start = (bf16[1,1024,1536]{2,1,0:T(8,128)(2,1)S(1)}, bf16[1,1024,1536]{2,1,0:T(8,128)(2,1)}, u32[]{:S(2)}) copy-start(bf16[1,1024,1536]{2,1,0:T(8,128)(2,1)} %param.9) | copy-start | bytes 9437188
  14.8 1.0 %copy-start.1 = (bf16[176,1536]{1,0:T(8,128)(2,1)S(1)}, bf16[176,1536]{1,0:T(8,128)(2,1)}, u32[]{:S(2)}) copy-start(bf16[176,1536]{1,0:T(8,128)(2,1)} %get-tuple-element.46.refs_0_) | copy-start | bytes 1622020
  15.9 3.5 %copy-start.4 = (bf16[96,1536]{1,0:T(8,128)(2,1)S(1)}, bf16[96,1536]{1,0:T(8,128)(2,1)}, u32[]{:S(2)}) copy-start(bf16[96,1536]{1,0:T(8,128)(2,1)} %get-tuple-element.57) | copy-start | bytes 884740
  19.4 3.9 %collective-permute-start.4 = (bf16[176,1536]{1,0:T(8,128)(2,1)S(1)}, bf16[176,1536]{1,0:T(8,128)(2,1)S(1)}, u32[]{:S(2)}, u32[]{:S(2)}) collective-permute-start(bf16[176,1536]{1,0:T(8,128)(2,1)S(1)} %collective-permute-done.1.refs_0_), channel_id=1, source_target_pairs={{0,1},{1,0},{2,3},{3,2},{4,5},{5,4},{6,7},{7,6},{8,9},{9,8},{10,11... | collective-permute-start | bytes 1622024 | tf_op jit(solution)/shard_map/ppermute | solution.py:299
  19.4 20.2 %copy-start.5 = (bf16[80,1536]{1,0:T(8,128)(2,1)S(1)}, bf16[80,1536]{1,0:T(8,128)(2,1)}, u32[]{:S(2)}) copy-start(bf16[80,1536]{1,0:T(8,128)(2,1)} %get-tuple-element.68) | copy-start | bytes 737284
  19.4 19.1 %collective-permute-start.5 = (bf16[96,1536]{1,0:T(8,128)(2,1)S(1)}, bf16[96,1536]{1,0:T(8,128)(2,1)S(1)}, u32[]{:S(2)}, u32[]{:S(2)}) collective-permute-start(bf16[96,1536]{1,0:T(8,128)(2,1)S(1)} %copy-done.4), channel_id=1, source_target_pairs={{0,24},{4,28},{8,16},{12,20},{16,8},{20,12},{24,0},{28,4},{1,25},{... | collective-permute-start | bytes 884744 | tf_op jit(solution)/shard_map/ppermute | solution.py:299
  25.2 8.8 %collective-permute-start.8 = (bf16[80,1536]{1,0:T(8,128)(2,1)S(1)}, bf16[80,1536]{1,0:T(8,128)(2,1)S(1)}, u32[]{:S(2)}, u32[]{:S(2)}) collective-permute-start(bf16[80,1536]{1,0:T(8,128)(2,1)S(1)} %collective-permute-done.2), channel_id=1, source_target_pairs={{0,2},{1,3},{2,0},{3,1},{4,6},{5,7},{6,4},{7,5},{8,10},{9,11},{10,... | collective-permute-start | bytes 737288 | tf_op jit(solution)/shard_map/ppermute | solution.py:299
  26.7 3.6 %collective-permute-start.6 = (f32[1,1024]{1,0:T(1,128)S(1)}, f32[1,1024]{1,0:T(1,128)S(1)}, u32[]{:S(2)}, u32[]{:S(2)}) collective-permute-start(f32[1,1024]{1,0:T(1,128)S(1)} %add.21), channel_id=1, source_target_pairs={{0,4},{4,0},{8,12},{12,8},{16,20},{20,16},{24,28},{28,24},{1,5},{5... | collective-permute-start | bytes 12296 | tf_op jit(solution)/shard_map/ppermute | solution.py:299
  30.3 3.6 %collective-permute-start.7 = (f32[1,1024]{1,0:T(1,128)S(1)}, f32[1,1024]{1,0:T(1,128)S(1)}, u32[]{:S(2)}, u32[]{:S(2)}) collective-permute-start(f32[1,1024]{1,0:T(1,128)S(1)} %add.22), channel_id=1, source_target_pairs={{0,8},{4,12},{8,0},{12,4},{16,24},{20,28},{24,16},{28,20},{1,9},{5... | collective-permute-start | bytes 12296 | tf_op jit(solution)/shard_map/ppermute | solution.py:299
  34.0 4.6 %collective-permute-start.9 = (f32[1,1024]{1,0:T(1,128)S(1)}, f32[1,1024]{1,0:T(1,128)S(1)}, u32[]{:S(2)}, u32[]{:S(2)}) collective-permute-start(f32[1,1024]{1,0:T(1,128)S(1)} %add.23), channel_id=1, source_target_pairs={{0,16},{4,20},{8,24},{12,28},{16,0},{20,4},{24,8},{28,12},{1,17},{... | collective-permute-start | bytes 12296 | tf_op jit(solution)/shard_map/ppermute | solution.py:299
  38.6 7.5 %collective-permute-start.10 = (bf16[96,1536]{1,0:T(8,128)(2,1)S(1)}, bf16[96,1536]{1,0:T(8,128)(2,1)S(1)}, u32[]{:S(2)}, u32[]{:S(2)}) collective-permute-start(bf16[96,1536]{1,0:T(8,128)(2,1)S(1)} %collective-permute-done.5.refs_0_), channel_id=1, source_target_pairs={{0,1},{1,0},{2,3},{3,2},{4,5},{5,4},{6,7},{7,6},{8,9},{9,8},{10,11... | collective-permute-start | bytes 884744 | tf_op jit(solution)/shard_map/ppermute | solution.py:299
  38.6 11.0 %collective-permute-start.16 = (bf16[96,1536]{1,0:T(8,128)(2,1)S(1)}, bf16[96,1536]{1,0:T(8,128)(2,1)S(1)}, u32[]{:S(2)}, u32[]{:S(2)}) collective-permute-start(bf16[96,1536]{1,0:T(8,128)(2,1)S(1)} %collective-permute-done.5.refs_0_), channel_id=1, source_target_pairs={{0,2},{1,3},{2,0},{3,1},{4,6},{5,7},{6,4},{7,5},{8,10},{9,11},{10,... | collective-permute-start | bytes 884744 | tf_op jit(solution)/shard_map/ppermute | solution.py:299
  39.4 6.7 %collective-permute-start.11 = (bf16[80,1536]{1,0:T(8,128)(2,1)S(1)}, bf16[80,1536]{1,0:T(8,128)(2,1)S(1)}, u32[]{:S(2)}, u32[]{:S(2)}) collective-permute-start(bf16[80,1536]{1,0:T(8,128)(2,1)S(1)} %collective-permute-done.8.refs_2_), channel_id=1, source_target_pairs={{0,1},{1,0},{2,3},{3,2},{4,5},{5,4},{6,7},{7,6},{8,9},{9,8},{10,11... | collective-permute-start | bytes 737288 | tf_op jit(solution)/shard_map/ppermute | solution.py:299
  39.6 10.2 %collective-permute-start.12 = (bf16[80,1536]{1,0:T(8,128)(2,1)S(1)}, bf16[80,1536]{1,0:T(8,128)(2,1)S(1)}, u32[]{:S(2)}, u32[]{:S(2)}) collective-permute-start(bf16[80,1536]{1,0:T(8,128)(2,1)S(1)} %copy-done.5), channel_id=1, source_target_pairs={{0,24},{4,28},{8,16},{12,20},{16,8},{20,12},{24,0},{28,4},{1,25},{... | collective-permute-start | bytes 737288 | tf_op jit(solution)/shard_map/ppermute | solution.py:299
  42.0 3.7 %collective-permute-start.13 = (f32[1,1024]{1,0:T(1,128)S(1)}, f32[1,1024]{1,0:T(1,128)S(1)}, u32[]{:S(2)}, u32[]{:S(2)}) collective-permute-start(f32[1,1024]{1,0:T(1,128)S(1)} %shard_map.60), channel_id=1, source_target_pairs={{0,4},{4,0},{8,12},{12,8},{16,20},{20,16},{24,28},{28,24},{1,5},{5... | collective-permute-start | bytes 12296 | tf_op jit(solution)/shard_map/ppermute | solution.py:299
  45.7 3.9 %collective-permute-start.14 = (f32[1,1024]{1,0:T(1,128)S(1)}, f32[1,1024]{1,0:T(1,128)S(1)}, u32[]{:S(2)}, u32[]{:S(2)}) collective-permute-start(f32[1,1024]{1,0:T(1,128)S(1)} %add.25), channel_id=1, source_target_pairs={{0,8},{4,12},{8,0},{12,4},{16,24},{20,28},{24,16},{28,20},{1,9},{5... | collective-permute-start | bytes 12296 | tf_op jit(solution)/shard_map/ppermute | solution.py:299
  49.6 4.4 %collective-permute-start.17 = (bf16[96,1536]{1,0:T(8,128)(2,1)S(1)}, bf16[96,1536]{1,0:T(8,128)(2,1)S(1)}, u32[]{:S(2)}, u32[]{:S(2)}) collective-permute-start(bf16[96,1536]{1,0:T(8,128)(2,1)S(1)} %collective-permute-done.16.refs_2_), channel_id=1, source_target_pairs={{0,1},{1,0},{2,3},{3,2},{4,5},{5,4},{6,7},{7,6},{8,9},{9,8},{10,11... | collective-permute-start | bytes 884744 | tf_op jit(solution)/shard_map/ppermute | solution.py:299
  49.8 4.3 %collective-permute-start.15 = (bf16[80,1536]{1,0:T(8,128)(2,1)S(1)}, bf16[80,1536]{1,0:T(8,128)(2,1)S(1)}, u32[]{:S(2)}, u32[]{:S(2)}) collective-permute-start(bf16[80,1536]{1,0:T(8,128)(2,1)S(1)} %collective-permute-done.12.refs_0_), channel_id=1, source_target_pairs={{0,1},{1,0},{2,3},{3,2},{4,5},{5,4},{6,7},{7,6},{8,9},{9,8},{10,11... | collective-permute-start | bytes 737288 | tf_op jit(solution)/shard_map/ppermute | solution.py:299
  50.2 5.5 %collective-permute-start.18 = (f32[1,1024]{1,0:T(1,128)S(1)}, f32[1,1024]{1,0:T(1,128)S(1)}, u32[]{:S(2)}, u32[]{:S(2)}) collective-permute-start(f32[1,1024]{1,0:T(1,128)S(1)} %add.26), channel_id=1, source_target_pairs={{0,16},{4,20},{8,24},{12,28},{16,0},{20,4},{24,8},{28,12},{1,17},{... | collective-permute-start | bytes 12296 | tf_op jit(solution)/shard_map/ppermute | solution.py:299
  57.7 7.1 %collective-permute-start.23 = (bf16[1,128,768]{2,1,0:T(8,128)(2,1)S(1)}, bf16[1,128,768]{2,1,0:T(8,128)(2,1)S(1)}, u32[]{:S(2)}, u32[]{:S(2)}) collective-permute-start(bf16[1,128,768]{2,1,0:T(8,128)(2,1)S(1)} %get-tuple-element.85), channel_id=1, source_target_pairs={{0,8},{4,12},{8,0},{12,4},{16,24},{20,28},{24,16},{28,20},{1,9},{5... | collective-permute-start | bytes 589832 | tf_op jit(solution)/shard_map/ppermute | solution.py:299
  59.5 6.9 %collective-permute-start.20 = (bf16[1,128,768]{2,1,0:T(8,128)(2,1)S(1)}, bf16[1,128,768]{2,1,0:T(8,128)(2,1)S(1)}, u32[]{:S(2)}, u32[]{:S(2)}) collective-permute-start(bf16[1,128,768]{2,1,0:T(8,128)(2,1)S(1)} %get-tuple-element.82), channel_id=1, source_target_pairs={{0,4},{4,0},{8,12},{12,8},{16,20},{20,16},{24,28},{28,24},{1,5},{5... | collective-permute-start | bytes 589832 | tf_op jit(solution)/shard_map/ppermute | solution.py:299
  63.7 7.9 %collective-permute-start.19 = (bf16[1,128,768]{2,1,0:T(8,128)(2,1)S(1)}, bf16[1,128,768]{2,1,0:T(8,128)(2,1)S(1)}, u32[]{:S(2)}, u32[]{:S(2)}) collective-permute-start(bf16[1,128,768]{2,1,0:T(8,128)(2,1)S(1)} %get-tuple-element.81), channel_id=1, source_target_pairs={{0,4},{4,0},{8,12},{12,8},{16,20},{20,16},{24,28},{28,24},{1,5},{5... | collective-permute-start | bytes 589832 | tf_op jit(solution)/shard_map/ppermute | solution.py:299
  64.3 7.5 %collective-permute-start.22 = (bf16[1,128,768]{2,1,0:T(8,128)(2,1)S(1)}, bf16[1,128,768]{2,1,0:T(8,128)(2,1)S(1)}, u32[]{:S(2)}, u32[]{:S(2)}) collective-permute-start(bf16[1,128,768]{2,1,0:T(8,128)(2,1)S(1)} %get-tuple-element.84), channel_id=1, source_target_pairs={{0,8},{4,12},{8,0},{12,4},{16,24},{20,28},{24,16},{28,20},{1,9},{5... | collective-permute-start | bytes 589832 | tf_op jit(solution)/shard_map/ppermute | solution.py:299
  64.8 9.0 %collective-permute-start.24 = (bf16[1,128,768]{2,1,0:T(8,128)(2,1)S(1)}, bf16[1,128,768]{2,1,0:T(8,128)(2,1)S(1)}, u32[]{:S(2)}, u32[]{:S(2)}) collective-permute-start(bf16[1,128,768]{2,1,0:T(8,128)(2,1)S(1)} %shard_map.67), channel_id=1, source_target_pairs={{0,4},{4,0},{8,12},{12,8},{16,20},{20,16},{24,28},{28,24},{1,5},{5... | collective-permute-start | bytes 589832 | tf_op jit(solution)/shard_map/ppermute | solution.py:299
  66.4 7.7 %collective-permute-start.21 = (bf16[1,128,768]{2,1,0:T(8,128)(2,1)S(1)}, bf16[1,128,768]{2,1,0:T(8,128)(2,1)S(1)}, u32[]{:S(2)}, u32[]{:S(2)}) collective-permute-start(bf16[1,128,768]{2,1,0:T(8,128)(2,1)S(1)} %shard_map.66), channel_id=1, source_target_pairs={{0,8},{4,12},{8,0},{12,4},{16,24},{20,28},{24,16},{28,20},{1,9},{5... | collective-permute-start | bytes 589832 | tf_op jit(solution)/shard_map/ppermute | solution.py:299

commit v8 on v7

--- a/solution.py
+++ b/solution.py
@@ -391,7 +391,7 @@
     partial = sum(near_s)
     masks = powers(groups)
     far_held.append(swap(after(held[1], first), "pts", far_mask))
-    forward(0, partial)
+    forward(0, first)
     sums = [partial]
     here = [far_cross[c, 0] for c in range(1, chips) if (c, 0) in far_cross]
     for mask in masks[:-1]:

time: 75.5 us -> 75 us (level)
  starting transfers between devices: 31.1 us -> 30.1 us
    ppermute x25, starting transfers between devices: 31.1 us -> 30.1 us  [swap(): lax.ppermute(values, axis, [(i, i ^ bit) for i in range(lax.axis_size(axi...]
  transfers between devices with their start and end apart: 25 -> 25, of which waited for: 13 -> 11; matrix products, arithmetic and copies ran while one was open for 0% -> 0% of each run, Pallas kernels for 18% -> 18%
where the time goes in v8:
time: 75 us; the launch traced here: 74.7 us
  starting transfers between devices  30.1 us (40%)
  waiting for transfers between devices  21.5 us (29%)
  Pallas kernels  19.7 us (26%)
  local copies, waits for them, and re-layouts  3.26 us (4%)
    ppermute x25, starting transfers between devices, swap(): lax.ppermute(values, axis, [(i, i ^ bit) for i in range(lax.axis_size(axi...  30.1 us
    ppermute x25, waiting for transfers between devices, swap(): lax.ppermute(values, axis, [(i, i ^ bit) for i in range(lax.axis_size(axi...  21.5 us
    pallas_call x14, Pallas kernels, call(): pl.pallas_call(kernel, out_shape=shapes, in_specs=[pl.BlockSpec(memory_sp...  19.7 us
    unnamed x12, local copies, waits for them, and re-layouts  3.26 us
  transfers between devices with their start and end apart: 25, of which 11 were waited for; matrix products, arithmetic and copies ran while one was open for 0% of the time, Pallas kernels for 18%

profile of v8, /device:TPU:0, one launch (start us, length us, event | category | flops | bytes accessed | tf_op | source)
XLA Modules:
  0.0 74.7 jit_solution(6908924394097556502)
XLA Ops:
  0.0 3.2 %shard_map.55 = (bf16[80,1536]{1,0:T(8,128)(2,1)}, bf16[96,1536]{1,0:T(8,128)(2,1)}, bf16[80,1536]{1,0:T(8,128)(2,1)}, bf16[176,1536]{1,0:T(8,128)(2,1)}, bf16[1...) custom-call(bf16[256,1536]{1,0:T(8,128)(2,1)} %refs_0_.1, s32[1,1024]{1,0:T(1,128)} %bitcast.6, ...), custom_call_target="tpu_custom_call" | custom-call | tf_op jit(solution)/shard_map/pallas_call | solution.py:282
  3.2 0.5 collective-permute-start
  3.8 2.6 %collective-permute-start.1 = (bf16[176,1536]{1,0:T(8,128)(2,1)}, bf16[176,1536]{1,0:T(8,128)(2,1)S(1)}, u32[]{:S(2)}, u32[]{:S(2)}) collective-permute-start(bf16[176,1536]{1,0:T(8,128)(2,1)} %get-tuple-element.51), channel_id=1, source_target_pairs={{0,2},{1,3},{2,0},{3,1},{4,6},{5,7},{6,4},{7,5},{8,10},{9,11},{10,... | collective-permute-start | bytes 1622024 | tf_op jit(solution)/shard_map/ppermute | solution.py:299
  6.3 3.6 %collective-permute-start.2 = (bf16[80,1536]{1,0:T(8,128)(2,1)}, bf16[80,1536]{1,0:T(8,128)(2,1)S(1)}, u32[]{:S(2)}, u32[]{:S(2)}) collective-permute-start(bf16[80,1536]{1,0:T(8,128)(2,1)} %get-tuple-element.53), channel_id=1, source_target_pairs={{0,24},{4,28},{8,16},{12,20},{16,8},{20,12},{24,0},{28,4},{1,25},{... | collective-permute-start | bytes 737288 | tf_op jit(solution)/shard_map/ppermute | solution.py:299
  9.9 0.7 copy-done.2
  10.6 0.7 copy-done.3
  11.3 1.4 %shard_map.56.refs_2_ = f32[1,704]{1,0:T(1,128)S(1)} custom-call(s32[1,1024]{1,0:T(1,128)S(1)} %copy-done.2, f32[1,64]{1,0:T(1,128)S(1)} %copy-done.3), custom_call_target="tpu_custom_call" | custom-call | tf_op jit(solution)/shard_map/pallas_call | solution.py:282
  12.7 0.3 collective-permute-start.3
  13.0 1.9 %copy-done = bf16[1,1024,1536]{2,1,0:T(8,128)(2,1)S(1)} copy-done((bf16[1,1024,1536]{2,1,0:T(8,128)(2,1)S(1)}, bf16[1,1024,1536]{2,1,0:T(8,128)(2,1)}, u32[]{:S(2)}) %copy-start) | copy-done | bytes 3145752
  14.8 1.0 %shard_map.57 = (bf16[1024,1536]{1,0:T(8,128)(2,1)S(1)}, bf16[128,1536]{1,0:T(8,128)(2,1)S(1)}) custom-call(bf16[1024,1536]{1,0:T(8,128)(2,1)S(1)} %bitcast.5), custom_call_target="tpu_custom_call" | custom-call | tf_op jit(solution)/shard_map/pallas_call | solution.py:282
  15.9 1.8 %shard_map.58 = (f32[352,1024]{1,0:T(8,128)S(1)}, f32[1,1024]{1,0:T(1,128)S(1)}, bf16[352,1536]{1,0:T(8,128)(2,1)S(1)}) custom-call(bf16[176,1536]{1,0:T(8,128)(2,1)S(1)} %copy-done.1, bf16[176,1536]{1,0:T(8,128)(2,1)S(1)} %collective-permute-done.refs_1_, f32[1,704]{1,0:T(1,128)S(1)} %shard_map.56.refs_2_, ...), custom_call_target="tpu_custom_call" | custom-call | tf_op jit(solution)/shard_map/pallas_call | solution.py:282
  17.7 0.5 collective-permute-done.3.codes_ref.refs_4_
  18.2 1.2 %collective-permute-done.1.refs_0_ = bf16[176,1536]{1,0:T(8,128)(2,1)S(1)} collective-permute-done((bf16[176,1536]{1,0:T(8,128)(2,1)}, bf16[176,1536]{1,0:T(8,128)(2,1)S(1)}, u32[]{:S(2)}, u32[]{:S(2)}) %collective-permute-start.1) | collective-permute-done | bytes 540704 | tf_op jit(solution)/shard_map/ppermute | solution.py:299
  19.4 3.9 %collective-permute-start.5 = (bf16[96,1536]{1,0:T(8,128)(2,1)S(1)}, bf16[96,1536]{1,0:T(8,128)(2,1)S(1)}, u32[]{:S(2)}, u32[]{:S(2)}) collective-permute-start(bf16[96,1536]{1,0:T(8,128)(2,1)S(1)} %copy-done.4), channel_id=1, source_target_pairs={{0,24},{4,28},{8,16},{12,20},{16,8},{20,12},{24,0},{28,4},{1,25},{... | collective-permute-start | bytes 884744 | tf_op jit(solution)/shard_map/ppermute | solution.py:299
  23.3 1.5 %collective-permute-start.8 = (bf16[80,1536]{1,0:T(8,128)(2,1)S(1)}, bf16[80,1536]{1,0:T(8,128)(2,1)S(1)}, u32[]{:S(2)}, u32[]{:S(2)}) collective-permute-start(bf16[80,1536]{1,0:T(8,128)(2,1)S(1)} %collective-permute-done.2), channel_id=1, source_target_pairs={{0,2},{1,3},{2,0},{3,1},{4,6},{5,7},{6,4},{7,5},{8,10},{9,11},{10,... | collective-permute-start | bytes 737288 | tf_op jit(solution)/shard_map/ppermute | solution.py:299
  24.8 1.8 %shard_map.59 = (f32[352,1024]{1,0:T(8,128)S(1)}, f32[1,1024]{1,0:T(1,128)S(1)}, bf16[352,1536]{1,0:T(8,128)(2,1)S(1)}) custom-call(bf16[176,1536]{1,0:T(8,128)(2,1)S(1)} %collective-permute-done.1.refs_0_, bf16[176,1536]{1,0:T(8,128)(2,1)S(1)} %collective-permute-done.4.refs_1_, f32[1,704]{1,0:T(1,128)S(1)} %shard_map.56.refs_2_, ...), custom_call_target="tpu_custom_call" | custom-call | tf_op jit(solution)/shard_map/pallas_call | solution.py:282
  26.7 1.6 %collective-permute-start.6 = (f32[1,1024]{1,0:T(1,128)S(1)}, f32[1,1024]{1,0:T(1,128)S(1)}, u32[]{:S(2)}, u32[]{:S(2)}) collective-permute-start(f32[1,1024]{1,0:T(1,128)S(1)} %add.21), channel_id=1, source_target_pairs={{0,4},{4,0},{8,12},{12,8},{16,20},{20,16},{24,28},{28,24},{1,5},{5... | collective-permute-start | bytes 12296 | tf_op jit(solution)/shard_map/ppermute | solution.py:299
  28.3 2.1 %collective-permute-done.6 = f32[1,1024]{1,0:T(1,128)S(1)} collective-permute-done((f32[1,1024]{1,0:T(1,128)S(1)}, f32[1,1024]{1,0:T(1,128)S(1)}, u32[]{:S(2)}, u32[]{:S(2)}) %collective-permute-start.6) | collective-permute-done | bytes 4128 | tf_op jit(solution)/shard_map/ppermute | solution.py:299
  30.4 3.6 %collective-permute-done.7 = f32[1,1024]{1,0:T(1,128)S(1)} collective-permute-done((f32[1,1024]{1,0:T(1,128)S(1)}, f32[1,1024]{1,0:T(1,128)S(1)}, u32[]{:S(2)}, u32[]{:S(2)}) %collective-permute-start.7) | collective-permute-done | bytes 4128 | tf_op jit(solution)/shard_map/ppermute | solution.py:299
  34.0 0.1 collective-permute-start.9
  34.0 4.5 %collective-permute-done.9 = f32[1,1024]{1,0:T(1,128)S(1)} collective-permute-done((f32[1,1024]{1,0:T(1,128)S(1)}, f32[1,1024]{1,0:T(1,128)S(1)}, u32[]{:S(2)}, u32[]{:S(2)}) %collective-permute-start.9) | collective-permute-done | bytes 4128 | tf_op jit(solution)/shard_map/ppermute | solution.py:299
  38.6 0.1 collective-permute-start.10
  38.6 0.6 collective-permute-start.16
  39.2 0.2 collective-permute-start.11
  39.4 1.7 %collective-permute-start.12 = (bf16[80,1536]{1,0:T(8,128)(2,1)S(1)}, bf16[80,1536]{1,0:T(8,128)(2,1)S(1)}, u32[]{:S(2)}, u32[]{:S(2)}) collective-permute-start(bf16[80,1536]{1,0:T(8,128)(2,1)S(1)} %copy-done.5), channel_id=1, source_target_pairs={{0,24},{4,28},{8,16},{12,20},{16,8},{20,12},{24,0},{28,4},{1,25},{... | collective-permute-start | bytes 737288 | tf_op jit(solution)/shard_map/ppermute | solution.py:299
  41.1 0.6 shard_map.60
  41.6 1.6 %collective-permute-start.13 = (f32[1,1024]{1,0:T(1,128)S(1)}, f32[1,1024]{1,0:T(1,128)S(1)}, u32[]{:S(2)}, u32[]{:S(2)}) collective-permute-start(f32[1,1024]{1,0:T(1,128)S(1)} %shard_map.60), channel_id=1, source_target_pairs={{0,4},{4,0},{8,12},{12,8},{16,20},{20,16},{24,28},{28,24},{1,5},{5... | collective-permute-start | bytes 12296 | tf_op jit(solution)/shard_map/ppermute | solution.py:299
  43.2 2.1 %collective-permute-done.13 = f32[1,1024]{1,0:T(1,128)S(1)} collective-permute-done((f32[1,1024]{1,0:T(1,128)S(1)}, f32[1,1024]{1,0:T(1,128)S(1)}, u32[]{:S(2)}, u32[]{:S(2)}) %collective-permute-start.13) | collective-permute-done | bytes 4128 | tf_op jit(solution)/shard_map/ppermute | solution.py:299
  45.3 0.4 shard_map.61
  45.7 2.0 %shard_map.62 = (f32[352,640]{1,0:T(8,128)S(1)}, f32[1,640]{1,0:T(1,128)}, bf16[352,1536]{1,0:T(8,128)(2,1)S(1)}) custom-call(bf16[96,1536]{1,0:T(8,128)(2,1)S(1)} %collective-permute-done.5.refs_0_, bf16[96,1536]{1,0:T(8,128)(2,1)S(1)} %collective-permute-done.10.refs_1_, bf16[80,1536]{1,0:T(8,128)(2,1)S(1)} %collective-permute-done.8.refs_2_, ...), custom_call_target="tpu_custom_call" | custom-call | tf_op jit(solution)/shard_map/pallas_call | solution.py:282
  47.8 1.5 %collective-permute-done.14 = f32[1,1024]{1,0:T(1,128)S(1)} collective-permute-done((f32[1,1024]{1,0:T(1,128)S(1)}, f32[1,1024]{1,0:T(1,128)S(1)}, u32[]{:S(2)}, u32[]{:S(2)}) %collective-permute-start.14) | collective-permute-done | bytes 4128 | tf_op jit(solution)/shard_map/ppermute | solution.py:299
  49.3 0.1 collective-permute-start.17
  49.4 0.2 collective-permute-done.12.refs_0_
  49.6 0.3 collective-permute-start.15
  49.9 3.4 %collective-permute-start.18 = (f32[1,1024]{1,0:T(1,128)S(1)}, f32[1,1024]{1,0:T(1,128)S(1)}, u32[]{:S(2)}, u32[]{:S(2)}) collective-permute-start(f32[1,1024]{1,0:T(1,128)S(1)} %add.26), channel_id=1, source_target_pairs={{0,16},{4,20},{8,24},{12,28},{16,0},{20,4},{24,8},{28,12},{1,17},{... | collective-permute-start | bytes 12296 | tf_op jit(solution)/shard_map/ppermute | solution.py:299
  53.3 1.7 %shard_map.63 = (f32[352,640]{1,0:T(8,128)S(1)}, f32[1,640]{1,0:T(1,128)}, bf16[352,1536]{1,0:T(8,128)(2,1)S(1)}) custom-call(bf16[80,1536]{1,0:T(8,128)(2,1)S(1)} %collective-permute-done.12.refs_0_, bf16[80,1536]{1,0:T(8,128)(2,1)S(1)} %collective-permute-done.15.refs_1_, bf16[96,1536]{1,0:T(8,128)(2,1)S(1)} %collective-permute-done.16.refs_2_, ...), custom_call_target="tpu_custom_call" | custom-call | tf_op jit(solution)/shard_map/pallas_call | solution.py:282
  55.0 1.9 %shard_map.64 = (bf16[1,128,768]{2,1,0:T(8,128)(2,1)S(1)}, bf16[1,128,768]{2,1,0:T(8,128)(2,1)S(1)}, bf16[1408,512]{1,0:T(8,128)(2,1)S(1)}) custom-call(f32[352,1024]{1,0:T(8,128)S(1)} %get-tuple-element.50.refs_0_, f32[352,1024]{1,0:T(8,128)S(1)} %get-tuple-element.55.refs_1_, f32[352,640]{1,0:T(8,128)S(1)} %get-tuple-element.66.refs_2_, ...), custom_call_target="tpu_custom_call" | custom-call | tf_op jit(solution)/shard_map/pallas_call | solution.py:282
  56.9 2.4 %collective-permute-start.23 = (bf16[1,128,768]{2,1,0:T(8,128)(2,1)S(1)}, bf16[1,128,768]{2,1,0:T(8,128)(2,1)S(1)}, u32[]{:S(2)}, u32[]{:S(2)}) collective-permute-start(bf16[1,128,768]{2,1,0:T(8,128)(2,1)S(1)} %get-tuple-element.85), channel_id=1, source_target_pairs={{0,8},{4,12},{8,0},{12,4},{16,24},{20,28},{24,16},{28,20},{1,9},{5... | collective-permute-start | bytes 589832 | tf_op jit(solution)/shard_map/ppermute | solution.py:299
  59.3 1.5 %collective-permute-start.20 = (bf16[1,128,768]{2,1,0:T(8,128)(2,1)S(1)}, bf16[1,128,768]{2,1,0:T(8,128)(2,1)S(1)}, u32[]{:S(2)}, u32[]{:S(2)}) collective-permute-start(bf16[1,128,768]{2,1,0:T(8,128)(2,1)S(1)} %get-tuple-element.82), channel_id=1, source_target_pairs={{0,4},{4,0},{8,12},{12,8},{16,20},{20,16},{24,28},{28,24},{1,5},{5... | collective-permute-start | bytes 589832 | tf_op jit(solution)/shard_map/ppermute | solution.py:299
  60.8 2.7 %shard_map.65 = (bf16[1,128,768]{2,1,0:T(8,128)(2,1)S(1)}, bf16[1,128,768]{2,1,0:T(8,128)(2,1)S(1)}, f32[2,128,768]{2,1,0:T(8,128)S(1)}, f32[2,128,768]{2,1,0:T(8,128)S(1)}) custom-call(bf16[1408,512]{1,0:T(8,128)(2,1)S(1)} %get-tuple-element.79.refs_0_, bf16[352,1536]{1,0:T(8,128)(2,1)S(1)} %get-tuple-element.75.refs_5_.refs_1_, ...), custom_call_target="tpu_custom_call" | custom-call | tf_op jit(solution)/shard_map/pallas_call | solution.py:282
  63.5 0.6 collective-permute-start.19
  64.1 0.1 collective-permute-start.22
  64.3 1.6 %collective-permute-start.24 = (bf16[1,128,768]{2,1,0:T(8,128)(2,1)S(1)}, bf16[1,128,768]{2,1,0:T(8,128)(2,1)S(1)}, u32[]{:S(2)}, u32[]{:S(2)}) collective-permute-start(bf16[1,128,768]{2,1,0:T(8,128)(2,1)S(1)} %shard_map.67), channel_id=1, source_target_pairs={{0,4},{4,0},{8,12},{12,8},{16,20},{20,16},{24,28},{28,24},{1,5},{5... | collective-permute-start | bytes 589832 | tf_op jit(solution)/shard_map/ppermute | solution.py:299
  65.9 2.0 %collective-permute-start.21 = (bf16[1,128,768]{2,1,0:T(8,128)(2,1)S(1)}, bf16[1,128,768]{2,1,0:T(8,128)(2,1)S(1)}, u32[]{:S(2)}, u32[]{:S(2)}) collective-permute-start(bf16[1,128,768]{2,1,0:T(8,128)(2,1)S(1)} %shard_map.66), channel_id=1, source_target_pairs={{0,8},{4,12},{8,0},{12,4},{16,24},{20,28},{24,16},{28,20},{1,9},{5... | collective-permute-start | bytes 589832 | tf_op jit(solution)/shard_map/ppermute | solution.py:299
  67.9 3.6 %collective-permute-done.19.refs_1_ = bf16[1,128,768]{2,1,0:T(8,128)(2,1)S(1)} collective-permute-done((bf16[1,128,768]{2,1,0:T(8,128)(2,1)S(1)}, bf16[1,128,768]{2,1,0:T(8,128)(2,1)S(1)}, u32[]{:S(2)}, u32[]{:S(2)}) %collective-permute-start.19) | collective-permute-done | bytes 196640 | tf_op jit(solution)/shard_map/ppermute | solution.py:299
  71.5 0.1 collective-permute-done.22.refs_4_
  71.6 2.1 %collective-permute-done.24.refs_5_ = bf16[1,128,768]{2,1,0:T(8,128)(2,1)S(1)} collective-permute-done((bf16[1,128,768]{2,1,0:T(8,128)(2,1)S(1)}, bf16[1,128,768]{2,1,0:T(8,128)(2,1)S(1)}, u32[]{:S(2)}, u32[]{:S(2)}) %collective-permute-start.24) | collective-permute-done | bytes 196640 | tf_op jit(solution)/shard_map/ppermute | solution.py:299
  73.7 1.1 %shard_map.68 = bf16[128,1536]{1,0:T(8,128)(2,1)} custom-call(f32[2,128,768]{2,1,0:T(8,128)S(1)} %get-tuple-element.80.keep_ref.refs_0_, bf16[1,128,768]{2,1,0:T(8,128)(2,1)S(1)} %collective-permute-done.19.refs_1_, bf16[1,128,768]{2,1,0:T(8,128)(2,1)S(1)} %collective-permute-done.21.refs_2_, f32[2,128,768]{2,1,0:T(8,128)S(1)} %get-tuple-element.83.keep_ref.refs_3_, ...), custom_call_target="tpu_custom_call" | custom-call | tf_op jit(solution)/shard_map/pallas_call | solution.py:282
  (35 shorter events, 0.2 us)
Async XLA Ops:
  3.2 12.6 %collective-permute-start = (bf16[176,1536]{1,0:T(8,128)(2,1)}, bf16[176,1536]{1,0:T(8,128)(2,1)S(1)}, u32[]{:S(2)}, u32[]{:S(2)}) collective-permute-start(bf16[176,1536]{1,0:T(8,128)(2,1)} %get-tuple-element.46.refs_0_), channel_id=1, source_target_pairs={{0,1},{1,0},{2,3},{3,2},{4,5},{5,4},{6,7},{7,6},{8,9},{9,8},{10,11... | collective-permute-start | bytes 1622024 | tf_op jit(solution)/shard_map/ppermute | solution.py:299
  3.8 15.6 %collective-permute-start.1 = (bf16[176,1536]{1,0:T(8,128)(2,1)}, bf16[176,1536]{1,0:T(8,128)(2,1)S(1)}, u32[]{:S(2)}, u32[]{:S(2)}) collective-permute-start(bf16[176,1536]{1,0:T(8,128)(2,1)} %get-tuple-element.51), channel_id=1, source_target_pairs={{0,2},{1,3},{2,0},{3,1},{4,6},{5,7},{6,4},{7,5},{8,10},{9,11},{10,... | collective-permute-start | bytes 1622024 | tf_op jit(solution)/shard_map/ppermute | solution.py:299
  6.3 11.9 %collective-permute-start.2 = (bf16[80,1536]{1,0:T(8,128)(2,1)}, bf16[80,1536]{1,0:T(8,128)(2,1)S(1)}, u32[]{:S(2)}, u32[]{:S(2)}) collective-permute-start(bf16[80,1536]{1,0:T(8,128)(2,1)} %get-tuple-element.53), channel_id=1, source_target_pairs={{0,24},{4,28},{8,16},{12,20},{16,8},{20,12},{24,0},{28,4},{1,25},{... | collective-permute-start | bytes 737288 | tf_op jit(solution)/shard_map/ppermute | solution.py:299
  9.9 0.7 copy-start.2
  10.6 0.7 copy-start.3
  12.7 5.6 %collective-permute-start.3 = (f32[1,704]{1,0:T(1,128)S(1)}, f32[1,704]{1,0:T(1,128)S(1)}, u32[]{:S(2)}, u32[]{:S(2)}) collective-permute-start(f32[1,704]{1,0:T(1,128)S(1)} %shard_map.56.refs_2_), channel_id=1, source_target_pairs={{0,24},{4,28},{8,16},{12,20},{16,8},{20,12},{24,0},{28,4},{1,25},{... | collective-permute-start | bytes 8456 | tf_op jit(solution)/shard_map/ppermute | solution.py:299
  12.9 1.9 %copy-start = (bf16[1,1024,1536]{2,1,0:T(8,128)(2,1)S(1)}, bf16[1,1024,1536]{2,1,0:T(8,128)(2,1)}, u32[]{:S(2)}) copy-start(bf16[1,1024,1536]{2,1,0:T(8,128)(2,1)} %param.9) | copy-start | bytes 9437188
  14.8 1.0 %copy-start.1 = (bf16[176,1536]{1,0:T(8,128)(2,1)S(1)}, bf16[176,1536]{1,0:T(8,128)(2,1)}, u32[]{:S(2)}) copy-start(bf16[176,1536]{1,0:T(8,128)(2,1)} %get-tuple-element.46.refs_0_) | copy-start | bytes 1622020
  15.9 3.5 %copy-start.4 = (bf16[96,1536]{1,0:T(8,128)(2,1)S(1)}, bf16[96,1536]{1,0:T(8,128)(2,1)}, u32[]{:S(2)}) copy-start(bf16[96,1536]{1,0:T(8,128)(2,1)} %get-tuple-element.57) | copy-start | bytes 884740
  19.4 5.4 %collective-permute-start.4 = (bf16[176,1536]{1,0:T(8,128)(2,1)S(1)}, bf16[176,1536]{1,0:T(8,128)(2,1)S(1)}, u32[]{:S(2)}, u32[]{:S(2)}) collective-permute-start(bf16[176,1536]{1,0:T(8,128)(2,1)S(1)} %collective-permute-done.1.refs_0_), channel_id=1, source_target_pairs={{0,1},{1,0},{2,3},{3,2},{4,5},{5,4},{6,7},{7,6},{8,9},{9,8},{10,11... | collective-permute-start | bytes 1622024 | tf_op jit(solution)/shard_map/ppermute | solution.py:299
  19.4 20.0 %copy-start.5 = (bf16[80,1536]{1,0:T(8,128)(2,1)S(1)}, bf16[80,1536]{1,0:T(8,128)(2,1)}, u32[]{:S(2)}) copy-start(bf16[80,1536]{1,0:T(8,128)(2,1)} %get-tuple-element.68) | copy-start | bytes 737284
  19.4 19.1 %collective-permute-start.5 = (bf16[96,1536]{1,0:T(8,128)(2,1)S(1)}, bf16[96,1536]{1,0:T(8,128)(2,1)S(1)}, u32[]{:S(2)}, u32[]{:S(2)}) collective-permute-start(bf16[96,1536]{1,0:T(8,128)(2,1)S(1)} %copy-done.4), channel_id=1, source_target_pairs={{0,24},{4,28},{8,16},{12,20},{16,8},{20,12},{24,0},{28,4},{1,25},{... | collective-permute-start | bytes 884744 | tf_op jit(solution)/shard_map/ppermute | solution.py:299
  23.3 10.6 %collective-permute-start.8 = (bf16[80,1536]{1,0:T(8,128)(2,1)S(1)}, bf16[80,1536]{1,0:T(8,128)(2,1)S(1)}, u32[]{:S(2)}, u32[]{:S(2)}) collective-permute-start(bf16[80,1536]{1,0:T(8,128)(2,1)S(1)} %collective-permute-done.2), channel_id=1, source_target_pairs={{0,2},{1,3},{2,0},{3,1},{4,6},{5,7},{6,4},{7,5},{8,10},{9,11},{10,... | collective-permute-start | bytes 737288 | tf_op jit(solution)/shard_map/ppermute | solution.py:299
  26.7 3.7 %collective-permute-start.6 = (f32[1,1024]{1,0:T(1,128)S(1)}, f32[1,1024]{1,0:T(1,128)S(1)}, u32[]{:S(2)}, u32[]{:S(2)}) collective-permute-start(f32[1,1024]{1,0:T(1,128)S(1)} %add.21), channel_id=1, source_target_pairs={{0,4},{4,0},{8,12},{12,8},{16,20},{20,16},{24,28},{28,24},{1,5},{5... | collective-permute-start | bytes 12296 | tf_op jit(solution)/shard_map/ppermute | solution.py:299
  30.3 3.6 %collective-permute-start.7 = (f32[1,1024]{1,0:T(1,128)S(1)}, f32[1,1024]{1,0:T(1,128)S(1)}, u32[]{:S(2)}, u32[]{:S(2)}) collective-permute-start(f32[1,1024]{1,0:T(1,128)S(1)} %add.22), channel_id=1, source_target_pairs={{0,8},{4,12},{8,0},{12,4},{16,24},{20,28},{24,16},{28,20},{1,9},{5... | collective-permute-start | bytes 12296 | tf_op jit(solution)/shard_map/ppermute | solution.py:299
  34.0 4.6 %collective-permute-start.9 = (f32[1,1024]{1,0:T(1,128)S(1)}, f32[1,1024]{1,0:T(1,128)S(1)}, u32[]{:S(2)}, u32[]{:S(2)}) collective-permute-start(f32[1,1024]{1,0:T(1,128)S(1)} %add.23), channel_id=1, source_target_pairs={{0,16},{4,20},{8,24},{12,28},{16,0},{20,4},{24,8},{28,12},{1,17},{... | collective-permute-start | bytes 12296 | tf_op jit(solution)/shard_map/ppermute | solution.py:299
  38.6 7.2 %collective-permute-start.10 = (bf16[96,1536]{1,0:T(8,128)(2,1)S(1)}, bf16[96,1536]{1,0:T(8,128)(2,1)S(1)}, u32[]{:S(2)}, u32[]{:S(2)}) collective-permute-start(bf16[96,1536]{1,0:T(8,128)(2,1)S(1)} %collective-permute-done.5.refs_0_), channel_id=1, source_target_pairs={{0,1},{1,0},{2,3},{3,2},{4,5},{5,4},{6,7},{7,6},{8,9},{9,8},{10,11... | collective-permute-start | bytes 884744 | tf_op jit(solution)/shard_map/ppermute | solution.py:299
  38.6 10.6 %collective-permute-start.16 = (bf16[96,1536]{1,0:T(8,128)(2,1)S(1)}, bf16[96,1536]{1,0:T(8,128)(2,1)S(1)}, u32[]{:S(2)}, u32[]{:S(2)}) collective-permute-start(bf16[96,1536]{1,0:T(8,128)(2,1)S(1)} %collective-permute-done.5.refs_0_), channel_id=1, source_target_pairs={{0,2},{1,3},{2,0},{3,1},{4,6},{5,7},{6,4},{7,5},{8,10},{9,11},{10,... | collective-permute-start | bytes 884744 | tf_op jit(solution)/shard_map/ppermute | solution.py:299
  39.2 6.5 %collective-permute-start.11 = (bf16[80,1536]{1,0:T(8,128)(2,1)S(1)}, bf16[80,1536]{1,0:T(8,128)(2,1)S(1)}, u32[]{:S(2)}, u32[]{:S(2)}) collective-permute-start(bf16[80,1536]{1,0:T(8,128)(2,1)S(1)} %collective-permute-done.8.refs_2_), channel_id=1, source_target_pairs={{0,1},{1,0},{2,3},{3,2},{4,5},{5,4},{6,7},{7,6},{8,9},{9,8},{10,11... | collective-permute-start | bytes 737288 | tf_op jit(solution)/shard_map/ppermute | solution.py:299
  39.4 10.2 %collective-permute-start.12 = (bf16[80,1536]{1,0:T(8,128)(2,1)S(1)}, bf16[80,1536]{1,0:T(8,128)(2,1)S(1)}, u32[]{:S(2)}, u32[]{:S(2)}) collective-permute-start(bf16[80,1536]{1,0:T(8,128)(2,1)S(1)} %copy-done.5), channel_id=1, source_target_pairs={{0,24},{4,28},{8,16},{12,20},{16,8},{20,12},{24,0},{28,4},{1,25},{... | collective-permute-start | bytes 737288 | tf_op jit(solution)/shard_map/ppermute | solution.py:299
  41.6 3.7 %collective-permute-start.13 = (f32[1,1024]{1,0:T(1,128)S(1)}, f32[1,1024]{1,0:T(1,128)S(1)}, u32[]{:S(2)}, u32[]{:S(2)}) collective-permute-start(f32[1,1024]{1,0:T(1,128)S(1)} %shard_map.60), channel_id=1, source_target_pairs={{0,4},{4,0},{8,12},{12,8},{16,20},{20,16},{24,28},{28,24},{1,5},{5... | collective-permute-start | bytes 12296 | tf_op jit(solution)/shard_map/ppermute | solution.py:299
  45.3 3.9 %collective-permute-start.14 = (f32[1,1024]{1,0:T(1,128)S(1)}, f32[1,1024]{1,0:T(1,128)S(1)}, u32[]{:S(2)}, u32[]{:S(2)}) collective-permute-start(f32[1,1024]{1,0:T(1,128)S(1)} %add.25), channel_id=1, source_target_pairs={{0,8},{4,12},{8,0},{12,4},{16,24},{20,28},{24,16},{28,20},{1,9},{5... | collective-permute-start | bytes 12296 | tf_op jit(solution)/shard_map/ppermute | solution.py:299
  49.3 4.0 %collective-permute-start.17 = (bf16[96,1536]{1,0:T(8,128)(2,1)S(1)}, bf16[96,1536]{1,0:T(8,128)(2,1)S(1)}, u32[]{:S(2)}, u32[]{:S(2)}) collective-permute-start(bf16[96,1536]{1,0:T(8,128)(2,1)S(1)} %collective-permute-done.16.refs_2_), channel_id=1, source_target_pairs={{0,1},{1,0},{2,3},{3,2},{4,5},{5,4},{6,7},{7,6},{8,9},{9,8},{10,11... | collective-permute-start | bytes 884744 | tf_op jit(solution)/shard_map/ppermute | solution.py:299
  49.6 3.7 %collective-permute-start.15 = (bf16[80,1536]{1,0:T(8,128)(2,1)S(1)}, bf16[80,1536]{1,0:T(8,128)(2,1)S(1)}, u32[]{:S(2)}, u32[]{:S(2)}) collective-permute-start(bf16[80,1536]{1,0:T(8,128)(2,1)S(1)} %collective-permute-done.12.refs_0_), channel_id=1, source_target_pairs={{0,1},{1,0},{2,3},{3,2},{4,5},{5,4},{6,7},{7,6},{8,9},{9,8},{10,11... | collective-permute-start | bytes 737288 | tf_op jit(solution)/shard_map/ppermute | solution.py:299
  49.9 5.2 %collective-permute-start.18 = (f32[1,1024]{1,0:T(1,128)S(1)}, f32[1,1024]{1,0:T(1,128)S(1)}, u32[]{:S(2)}, u32[]{:S(2)}) collective-permute-start(f32[1,1024]{1,0:T(1,128)S(1)} %add.26), channel_id=1, source_target_pairs={{0,16},{4,20},{8,24},{12,28},{16,0},{20,4},{24,8},{28,12},{1,17},{... | collective-permute-start | bytes 12296 | tf_op jit(solution)/shard_map/ppermute | solution.py:299
  56.9 7.3 %collective-permute-start.23 = (bf16[1,128,768]{2,1,0:T(8,128)(2,1)S(1)}, bf16[1,128,768]{2,1,0:T(8,128)(2,1)S(1)}, u32[]{:S(2)}, u32[]{:S(2)}) collective-permute-start(bf16[1,128,768]{2,1,0:T(8,128)(2,1)S(1)} %get-tuple-element.85), channel_id=1, source_target_pairs={{0,8},{4,12},{8,0},{12,4},{16,24},{20,28},{24,16},{28,20},{1,9},{5... | collective-permute-start | bytes 589832 | tf_op jit(solution)/shard_map/ppermute | solution.py:299
  59.3 6.5 %collective-permute-start.20 = (bf16[1,128,768]{2,1,0:T(8,128)(2,1)S(1)}, bf16[1,128,768]{2,1,0:T(8,128)(2,1)S(1)}, u32[]{:S(2)}, u32[]{:S(2)}) collective-permute-start(bf16[1,128,768]{2,1,0:T(8,128)(2,1)S(1)} %get-tuple-element.82), channel_id=1, source_target_pairs={{0,4},{4,0},{8,12},{12,8},{16,20},{20,16},{24,28},{28,24},{1,5},{5... | collective-permute-start | bytes 589832 | tf_op jit(solution)/shard_map/ppermute | solution.py:299
  63.5 7.9 %collective-permute-start.19 = (bf16[1,128,768]{2,1,0:T(8,128)(2,1)S(1)}, bf16[1,128,768]{2,1,0:T(8,128)(2,1)S(1)}, u32[]{:S(2)}, u32[]{:S(2)}) collective-permute-start(bf16[1,128,768]{2,1,0:T(8,128)(2,1)S(1)} %get-tuple-element.81), channel_id=1, source_target_pairs={{0,4},{4,0},{8,12},{12,8},{16,20},{20,16},{24,28},{28,24},{1,5},{5... | collective-permute-start | bytes 589832 | tf_op jit(solution)/shard_map/ppermute | solution.py:299
  64.1 7.4 %collective-permute-start.22 = (bf16[1,128,768]{2,1,0:T(8,128)(2,1)S(1)}, bf16[1,128,768]{2,1,0:T(8,128)(2,1)S(1)}, u32[]{:S(2)}, u32[]{:S(2)}) collective-permute-start(bf16[1,128,768]{2,1,0:T(8,128)(2,1)S(1)} %get-tuple-element.84), channel_id=1, source_target_pairs={{0,8},{4,12},{8,0},{12,4},{16,24},{20,28},{24,16},{28,20},{1,9},{5... | collective-permute-start | bytes 589832 | tf_op jit(solution)/shard_map/ppermute | solution.py:299
  64.3 9.4 %collective-permute-start.24 = (bf16[1,128,768]{2,1,0:T(8,128)(2,1)S(1)}, bf16[1,128,768]{2,1,0:T(8,128)(2,1)S(1)}, u32[]{:S(2)}, u32[]{:S(2)}) collective-permute-start(bf16[1,128,768]{2,1,0:T(8,128)(2,1)S(1)} %shard_map.67), channel_id=1, source_target_pairs={{0,4},{4,0},{8,12},{12,8},{16,20},{20,16},{24,28},{28,24},{1,5},{5... | collective-permute-start | bytes 589832 | tf_op jit(solution)/shard_map/ppermute | solution.py:299
  65.9 7.8 %collective-permute-start.21 = (bf16[1,128,768]{2,1,0:T(8,128)(2,1)S(1)}, bf16[1,128,768]{2,1,0:T(8,128)(2,1)S(1)}, u32[]{:S(2)}, u32[]{:S(2)}) collective-permute-start(bf16[1,128,768]{2,1,0:T(8,128)(2,1)S(1)} %shard_map.66), channel_id=1, source_target_pairs={{0,8},{4,12},{8,0},{12,4},{16,24},{20,28},{24,16},{28,20},{1,9},{5... | collective-permute-start | bytes 589832 | tf_op jit(solution)/shard_map/ppermute | solution.py:299
